TPU v7x, 512 devices: a whole 4x4x16 slice. The times are simulated.
512 devices in a mesh: dp: 8 (over x, y_hi), mp: 64 (over y_lo, z, core).
Axes of the slice: x: 4, y: 4 (y_hi: 2, y_lo: 2; y = y_hi * 2 + y_lo), z: 16, core: 2. Of those that a mesh axis runs over, the one named last changes fastest.
Arguments:
- inputs: bfloat16 [2048, 3072], P(('dp', 'mp')), may hold values from -1.5 to 1.5
- gain: float32 [3072], replicated, may hold values from 0.1 to 1.9
- w_in: bfloat16 [3072, 12288], P(None, 'mp'), may hold values from -0.109375 to 0.109375
- w_out: bfloat16 [12288, 3072], P('mp'), may hold values from -0.0546875 to 0.0546875
- cotangent: bfloat16 [2048, 3072], P(('dp', 'mp')), may hold values from -6 to 6
Outputs:
- input_grad: bfloat16 [2048, 3072], P(('dp', 'mp'))
- grad_in: bfloat16 [3072, 12288], P(None, 'mp')
- grad_out: bfloat16 [12288, 3072], P('mp')
All inputs are finite; a program needn't handle non-finite values.
Results may differ from a plain program's by a relative error of at most 0.017.
Values may be sent and summed in bfloat16 or wider, within the bound.
No kernel may reach another device: no remote copies, remote signals or barrier semaphores. Data moves between devices by JAX's collectives and lax.ppermute only.
A program may use at most 64 MiB of HBM per device.

v0:
```python
import math

import jax
import jax.numpy as jnp
from jax import lax
from jax.sharding import PartitionSpec as P

contract_last = (((1,), (1,)), ((), ()))
contract_first = (((0,), (0,)), ((), ()))


def gelu_value(value):
    slope = math.sqrt(2.0 / math.pi)
    return 0.5 * value * (1.0 + jnp.tanh(slope * (value + 0.044715 * value * value * value)))


def gelu_slope(value):
    slope = math.sqrt(2.0 / math.pi)
    tangent = jnp.tanh(slope * (value + 0.044715 * value * value * value))
    return 0.5 * (1.0 + tangent) + 0.5 * value * (1.0 - tangent * tangent) * slope * (
        1.0 + 3.0 * 0.044715 * value * value
    )


def local_terms(normed_part, grad_part, w_in, w_out):
    hidden = jnp.dot(normed_part, w_in, preferred_element_type=jnp.float32)
    activated = gelu_value(hidden).astype(jnp.bfloat16)
    act_grad = lax.dot_general(grad_part, w_out, contract_last, preferred_element_type=jnp.float32)
    hidden_grad = (act_grad * gelu_slope(hidden)).astype(jnp.bfloat16)
    part_in = lax.dot_general(
        normed_part, hidden_grad, contract_first, preferred_element_type=jnp.float32
    )
    part_out = lax.dot_general(
        activated, grad_part, contract_first, preferred_element_type=jnp.float32
    )
    return (hidden_grad, part_in, part_out)


def body(inputs, gain, w_in, w_out, cotangent):
    widened = inputs.astype(jnp.float32)
    row_mean = jnp.mean(widened, axis=1, keepdims=True)
    centred = widened - row_mean
    variance = jnp.mean(centred * centred, axis=1, keepdims=True)
    inverse = 1.0 / jnp.sqrt(variance + 1e-06)
    normal = centred * inverse
    normed = (normal * gain[None, :]).astype(jnp.bfloat16)
    normed_all = lax.all_gather(normed, "mp", axis=0, tiled=True)
    grad_all = lax.all_gather(cotangent, "mp", axis=0, tiled=True)
    hidden_grad, part_in, part_out = local_terms(normed_all, grad_all, w_in, w_out)
    summed_in, summed_out = (
        lax.psum(part_in.astype(jnp.bfloat16), "dp").astype(jnp.float32),
        lax.psum(part_out.astype(jnp.bfloat16), "dp").astype(jnp.float32),
    )
    groups = lax.axis_size("dp")
    grad_in = (summed_in / groups).astype(jnp.bfloat16)
    grad_out = (summed_out / groups).astype(jnp.bfloat16)
    whole_sum = lax.dot_general(
        hidden_grad, w_in, contract_last, preferred_element_type=jnp.float32
    )
    normed_grad = lax.psum_scatter(whole_sum, "mp", scatter_dimension=0, tiled=True)
    scaled = normed_grad * gain[None, :]
    first_mean = jnp.mean(scaled, axis=1, keepdims=True)
    second_mean = jnp.mean(scaled * normal, axis=1, keepdims=True)
    result = cotangent.astype(jnp.float32) + (scaled - first_mean - normal * second_mean) * inverse
    return (result.astype(jnp.bfloat16), grad_in, grad_out)


def solution(mesh):
    in_specs = (P(("dp", "mp"), None), P(), P(None, "mp"), P("mp", None), P(("dp", "mp"), None))
    out_specs = (P(("dp", "mp"), None), P(None, "mp"), P("mp", None))
    return jax.shard_map(body, mesh=mesh, in_specs=in_specs, out_specs=out_specs, check_vma=False)
```

profile of v0, /device:TPU:1, one launch (start us, length us, event | category | flops | bytes accessed | tf_op | source)
XLA Modules:
  0.0 850.9 jit_solution(2225781671589846530)
XLA Ops:
  7.2 0.0 all-gather.7.cloned.1.call-start
  7.2 1.0 convert_reduce_fusion
  8.2 0.9 fusion.21
  9.1 1.4 fusion.23
  10.6 0.0 all-gather.5.cloned.1.call-start
  10.7 0.7 all-gather.5.cloned.1.call-update
  11.4 0.0 all-reduce.7.cloned.1.call-start
  11.4 126.9 %all-gather.7.cloned.1.call-done = bf16[64,4,3072]{2,1,0:T(4,128)(2,1)} async-done(((bf16[1,4,3072]{2,1,0:T(4,128)(2,1)}), bf16[64,4,3072]{2,1,0:T(4,128)(2,1)}) %all-gather.7.cloned.1.call-update) | async-done | bytes 1572880 | tf_op jit(solution)/shard_map/all_gather | solution.py:47
  138.3 2.7 reshape.31
  141.0 0.7 fusion.28
  141.7 116.8 %all-gather.5.cloned.1.call-done = bf16[64,4,3072]{2,1,0:T(4,128)(2,1)} async-done(((bf16[1,4,3072]{2,1,0:T(4,128)(2,1)}), bf16[64,4,3072]{2,1,0:T(4,128)(2,1)}) %all-gather.5.cloned.1.call-update) | async-done | bytes 1572880 | tf_op jit(solution)/shard_map/all_gather | solution.py:48
  258.5 3.7 reshape.29
  262.2 3.1 convolution_convert_fusion.1
  265.3 0.7 fusion
  266.0 1.5 convolution_convert_fusion
  267.5 0.0 all-reduce.5.cloned.1.call-start
  267.6 2.3 fusion.29
  269.9 1.3 dynamic-slice
  271.8 124.5 %all-reduce.7.cloned.1.call-done = (bf16[3072,192]{0,1:T(8,128)(2,1)}, bf16[192,3072]{1,0:T(8,128)(2,1)}) async-done(((bf16[3072,192]{0,1:T(8,128)(2,1)}, bf16[192,3072]{1,0:T(8,128)(2,1)}), (bf16[3072,192]{0,1:T(8,128)(2,1)}, bf16[192,3072]{1,0:T(8,128)(2,1)})) %all-reduce.7.cloned.1.call-update) | async-done | bytes 2359312 | tf_op jit(solution)/shard_map/psum | solution.py:51
  396.3 2.6 multiply_convert_fusion.1
  398.9 1.3 multiply_convert_fusion
  400.2 441.4 %all-reduce.5.cloned.1.call-done = f32[256,3072]{1,0:T(8,128)} async-done(((f32[256,3072]{1,0:T(8,128)}), f32[256,3072]{1,0:T(8,128)}) %all-reduce.5.cloned.1.call-update) | async-done | bytes 3145744
  841.6 1.1 fusion.22
  842.7 1.6 fusion.20
  (20 shorter events, 0.1 us)
Async XLA Ops:
  7.2 133.8 %copy-start = (bf16[3072,192]{0,1:T(8,128)(2,1)S(1)}, bf16[3072,192]{0,1:T(8,128)(2,1)}, u32[]{:S(2)}) copy-start(bf16[3072,192]{0,1:T(8,128)(2,1)} %param.7) | copy-start | bytes 3538948
  7.2 131.1 %all-gather.7.cloned.1.call-start = ((), (), s32[]{:S(2)}) async-start(), calls=%async_computation.1 | async-start | bytes 1597440 | tf_op jit(solution)/shard_map/all_gather | solution.py:47
  10.6 247.9 %all-gather.5.cloned.1.call-start = ((), (), s32[]{:S(2)}) async-start(), calls=%async_computation | async-start | bytes 1597440 | tf_op jit(solution)/shard_map/all_gather | solution.py:48
  11.4 384.9 %all-reduce.7.cloned.1.call-start = ((), (), s32[]{:S(2)}) async-start(), calls=%async_computation.3 | async-start | bytes 4718592 | tf_op jit(solution)/shard_map/psum | solution.py:51
  262.2 3.1 copy-start.1
  262.2 3.1 copy-start.6
  267.5 574.0 %all-reduce.5.cloned.1.call-start = ((), (), s32[]{:S(2)}) async-start(), calls=%async_computation.2 | async-start | bytes 6291456
  396.3 2.6 copy-start.2
  398.9 442.7 %copy-start.3 = (bf16[4,3072]{1,0:T(4,128)(2,1)S(1)}, bf16[4,3072]{1,0:T(4,128)(2,1)}, u32[]{:S(2)}) copy-start(bf16[4,3072]{1,0:T(4,128)(2,1)} %param.5) | copy-start | bytes 73732
  398.9 442.7 %copy-start.4 = (f32[3072]{0:T(1024)S(1)}, f32[3072]{0:T(1024)}, u32[]{:S(2)}) copy-start(f32[3072]{0:T(1024)} %param.6) | copy-start | bytes 36868
  398.9 443.8 %copy-start.5 = (bf16[4,3072]{1,0:T(4,128)(2,1)S(1)}, bf16[4,3072]{1,0:T(4,128)(2,1)}, u32[]{:S(2)}) copy-start(bf16[4,3072]{1,0:T(4,128)(2,1)} %param.9) | copy-start | bytes 73732
Sparse Core Ops, SparseCore 0:
  10.7 127.4 all-gather.6
  140.4 118.0 all-gather.4
  267.7 128.5 all-reduce.6
  399.1 442.4 all-reduce.4
where the time goes:
time: 851 us
  waiting for transfers between devices  810 us (95%)
  between operations  14.5 us (2%)
  other arithmetic  9.97 us (1%)
    unnamed x5, waiting for transfers between devices  442 us
    all_gather x1, waiting for transfers between devices, body(): normed_all = lax.all_gather(normed, 'mp', axis=0, tiled=True)  127 us
    psum x1, waiting for transfers between devices, body(): lax.psum(part_in.astype(jnp.bfloat16), 'dp').astype(jnp.float32)  124 us
    all_gather x1, waiting for transfers between devices, body(): grad_all = lax.all_gather(cotangent, 'mp', axis=0, tiled=True)  117 us
  transfers between devices with their start and end apart: 4, of which 4 were waited for; matrix products, arithmetic and copies ran while one was open for 1% of the time, Pallas kernels for 0%

commit v1 on v0

v1 whole, which is shorter than its diff:
```python
import math

import jax
import jax.numpy as jnp
from jax import lax
from jax.sharding import Mesh, PartitionSpec as P

AXES = ("x", "yh", "yl", "z", "core")
DP = ("x", "yh")
MP = ("yl", "z", "core")
contract_last = (((1,), (1,)), ((), ()))
contract_first = (((0,), (0,)), ((), ()))
SWAP = [(0, 1), (1, 0)]


def gelu_both(value):
    slope = math.sqrt(2.0 / math.pi)
    tangent = jnp.tanh(slope * (value + 0.044715 * value * value * value))
    gelu = 0.5 * value * (1.0 + tangent)
    derivative = 0.5 * (1.0 + tangent) + 0.5 * value * (1.0 - tangent * tangent) * slope * (
        1.0 + 3.0 * 0.044715 * value * value
    )
    return gelu, derivative


def body(inputs, gain, w_in, w_out, cotangent):
    rows, width = inputs.shape
    hidden_units = w_out.shape[0]
    n_dp = lax.axis_size(DP)
    n_z = lax.axis_size("z")
    widened = inputs.astype(jnp.float32)
    row_mean = jnp.mean(widened, axis=1, keepdims=True)
    centred = widened - row_mean
    variance = jnp.mean(centred * centred, axis=1, keepdims=True)
    inverse = 1.0 / jnp.sqrt(variance + 1e-06)
    normal = centred * inverse
    normed = (normal * gain[None, :]).astype(jnp.bfloat16)

    both = jnp.concatenate([normed, cotangent], axis=1)
    both = lax.all_gather(both, "z", axis=0, tiled=True)
    both = jnp.concatenate([both, lax.ppermute(both, "yl", SWAP)], axis=0)
    both = jnp.concatenate([both, lax.ppermute(both, "core", SWAP)], axis=0)
    normed_all, grad_all = both[:, :width], both[:, width:]

    hidden = jnp.dot(normed_all, w_in, preferred_element_type=jnp.float32)
    gelu, derivative = gelu_both(hidden)
    activated = gelu.astype(jnp.bfloat16)
    act_grad = lax.dot_general(grad_all, w_out, contract_last, preferred_element_type=jnp.float32)
    hidden_grad = (act_grad * derivative).astype(jnp.bfloat16)
    part_in = lax.dot_general(
        hidden_grad, normed_all, contract_first, preferred_element_type=jnp.float32
    ).astype(jnp.bfloat16)
    part_out = lax.dot_general(
        activated, grad_all, contract_first, preferred_element_type=jnp.float32
    ).astype(jnp.bfloat16)
    whole_sum = lax.dot_general(
        hidden_grad, w_in, contract_last, preferred_element_type=jnp.float32
    )

    block = hidden_units // n_dp
    parts = jnp.stack(
        [part_in.reshape(n_dp, block, width), part_out.reshape(n_dp, block, width)], axis=1
    ).reshape(n_dp, 2 * block, width)
    parts = lax.all_to_all(parts, DP, 0, 0, tiled=True)
    mine = (jnp.sum(parts.astype(jnp.float32), axis=0) / n_dp).astype(jnp.bfloat16)
    other = lax.ppermute(mine, "yh", SWAP)
    first = lax.axis_index("yh") == 0
    pair = jnp.stack([jnp.where(first, mine, other), jnp.where(first, other, mine)])
    spread = lax.all_gather(pair, "x", axis=0, tiled=True).reshape(n_dp, 2, block, width)
    grad_in = spread[:, 0].reshape(hidden_units, width).T
    grad_out = spread[:, 1].reshape(hidden_units, width)

    for axis in ("core", "yl"):
        half = whole_sum.shape[0] // 2
        away = lax.ppermute(whole_sum[half:].astype(jnp.bfloat16), axis, SWAP)
        whole_sum = whole_sum[:half] + away.astype(jnp.float32)
    terms = whole_sum.astype(jnp.bfloat16).reshape(n_z, rows, width)
    terms = lax.all_to_all(terms, "z", 0, 0, tiled=True)
    normed_grad = jnp.sum(terms.astype(jnp.float32), axis=0)
    scaled = normed_grad * gain[None, :]
    first_mean = jnp.mean(scaled, axis=1, keepdims=True)
    second_mean = jnp.mean(scaled * normal, axis=1, keepdims=True)
    result = cotangent.astype(jnp.float32) + (scaled - first_mean - normal * second_mean) * inverse
    return (result.astype(jnp.bfloat16), grad_in, grad_out)


def solution(mesh):
    fine = Mesh(mesh.devices.reshape(4, 2, 2, 16, 2), AXES)
    rows, hidden_split = P(DP + MP, None), P(None, MP)
    in_specs = (rows, P(), hidden_split, P(MP, None), rows)
    out_specs = (rows, hidden_split, P(MP, None))
    return jax.shard_map(body, mesh=fine, in_specs=in_specs, out_specs=out_specs, check_vma=False)
```

time: 851 us -> 179 us (0.21)
  waiting for transfers between devices: 810 us -> 54.8 us
  blocking collectives: 0 us -> 57.4 us
  starting transfers between devices: 0.16 us -> 29.3 us
    unnamed x5 -> x1, waiting for transfers between devices: 442 us -> 0.02 us
    all_gather x2 -> x1, waiting for transfers between devices: 244 us -> 4.29 us  [body(): lax.all_gather(pair, 'x', axis=0, tiled=True).reshape(n_dp, 2, block, width)]
    psum x1 -> x0, waiting for transfers between devices: 124 us -> none  [body(): lax.psum(part_in.astype(jnp.bfloat16), 'dp').astype(jnp.float32)]
    all_gather x0 -> x1, blocking collectives: none -> 33.9 us  [body(): both = lax.all_gather(both, 'z', axis=0, tiled=True)]
    all_to_all x0 -> x1, waiting for transfers between devices: none -> 27.7 us  [body(): parts = lax.all_to_all(parts, DP, 0, 0, tiled=True)]
    all_to_all x0 -> x1, blocking collectives: none -> 23.5 us  [body(): terms = lax.all_to_all(terms, 'z', 0, 0, tiled=True)]
    ppermute x0 -> x5, waiting for transfers between devices: none -> 22.8 us  [the longest x1 9.98 us: body(): both = jnp.concatenate([both, lax.ppermute(both, 'yl', SWAP)], axis=0)]
    ppermute x0 -> x5, starting transfers between devices: none -> 22.6 us  [the longest x1 10.6 us: body(): both = jnp.concatenate([both, lax.ppermute(both, 'core', SWAP)], axis=0)]
  transfers between devices with their start and end apart: 4 -> 7, of which waited for: 4 -> 6; matrix products, arithmetic and copies ran while one was open for 1% -> 4% of each run, Pallas kernels for 0% -> 0%
where the time goes in v1:
time: 179 us; the launch traced here: 177 us
  blocking collectives  57.4 us (32%)
  waiting for transfers between devices  54.8 us (31%)
  starting transfers between devices  29.3 us (16%)
  between operations  14.3 us (8%)
  other arithmetic  10.1 us (6%)
  local copies, waits for them, and re-layouts  7.36 us (4%)
  matrix products  3.86 us (2%)
    all_gather x1, blocking collectives, body(): both = lax.all_gather(both, 'z', axis=0, tiled=True)  33.9 us
    all_to_all x1, waiting for transfers between devices, body(): parts = lax.all_to_all(parts, DP, 0, 0, tiled=True)  27.7 us
    all_to_all x1, blocking collectives, body(): terms = lax.all_to_all(terms, 'z', 0, 0, tiled=True)  23.5 us
    ppermute x1, starting transfers between devices, body(): both = jnp.concatenate([both, lax.ppermute(both, 'core', SWAP)], axis=0)  10.6 us
    ppermute x1, waiting for transfers between devices, body(): both = jnp.concatenate([both, lax.ppermute(both, 'yl', SWAP)], axis=0)  9.98 us
    ppermute x2, waiting for transfers between devices, body(): away = lax.ppermute(whole_sum[half:].astype(jnp.bfloat16), axis, SWAP)  6.97 us
    all_to_all x1, starting transfers between devices, body(): parts = lax.all_to_all(parts, DP, 0, 0, tiled=True)  6.65 us
    ppermute x2, starting transfers between devices, body(): away = lax.ppermute(whole_sum[half:].astype(jnp.bfloat16), axis, SWAP)  4.85 us
  transfers between devices with their start and end apart: 7, of which 6 were waited for; matrix products, arithmetic and copies ran while one was open for 4% of the time, Pallas kernels for 0%

profile of v1, /device:TPU:1, one launch (start us, length us, event | category | flops | bytes accessed | tf_op | source)
XLA Modules:
  0.0 177.1 jit_solution(93815577385694056)
XLA Ops:
  7.2 1.0 convert_reduce_fusion.2
  8.2 0.9 fusion.33
  10.7 33.9 %all-gather = bf16[16,4,6144]{2,1,0:T(4,128)(2,1)S(1)} all-gather(bf16[1,4,6144]{2,1,0:T(4,128)(2,1)S(1)} %maximum_bitcast_fusion), channel_id=1, replica_groups=mesh['x'=4,'yh'=2,'yl'=2,'z'=16,'core'=2] {'z'}, dimensions={0}, use_global_device_ids=true | all-gather | bytes 835584 | tf_op jit(solution)/shard_map/all_gather | solution.py:40
  44.8 3.2 %collective-permute-start = (bf16[64,6144]{1,0:T(8,128)(2,1)S(1)}, bf16[64,6144]{1,0:T(8,128)(2,1)S(1)}, u32[]{:S(2)}, u32[]{:S(2)}) collective-permute-start(bf16[64,6144]{1,0:T(8,128)(2,1)S(1)} %reshape.41), channel_id=1, source_target_pairs={{0,32},{32,0},{1,33},{33,1},{2,34},{34,2},{3,35},{35,3},{4,36},{36... | collective-permute-start | bytes 2359304 | tf_op jit(solution)/shard_map/ppermute | solution.py:41
  48.0 10.0 %collective-permute-done = bf16[64,6144]{1,0:T(8,128)(2,1)S(1)} collective-permute-done((bf16[64,6144]{1,0:T(8,128)(2,1)S(1)}, bf16[64,6144]{1,0:T(8,128)(2,1)S(1)}, u32[]{:S(2)}, u32[]{:S(2)}) %collective-permute-start) | collective-permute-done | bytes 786464 | tf_op jit(solution)/shard_map/ppermute | solution.py:41
  58.1 10.6 %collective-permute-start.1 = (bf16[128,6144]{1,0:T(8,128)(2,1)S(1)}, bf16[128,6144]{1,0:T(8,128)(2,1)S(1)}, u32[]{:S(2)}, u32[]{:S(2)}) collective-permute-start(bf16[128,6144]{1,0:T(8,128)(2,1)S(1)} %pad_maximum_fusion.1), channel_id=1, source_target_pairs={{0,1},{1,0},{2,3},{3,2},{4,5},{5,4},{6,7},{7,6},{8,9},{9,8},{10,11... | collective-permute-start | bytes 4718600 | tf_op jit(solution)/shard_map/ppermute | solution.py:42
  68.8 2.9 %collective-permute-done.1 = bf16[128,6144]{1,0:T(8,128)(2,1)S(1)} collective-permute-done((bf16[128,6144]{1,0:T(8,128)(2,1)S(1)}, bf16[128,6144]{1,0:T(8,128)(2,1)S(1)}, u32[]{:S(2)}, u32[]{:S(2)}) %collective-permute-start.1) | collective-permute-done | bytes 1572896 | tf_op jit(solution)/shard_map/ppermute | solution.py:42
  75.2 1.7 pad_maximum_fusion
  76.8 6.6 %all-to-all-start.1 = ((bf16[8,48,3072]{2,1,0:T(8,128)(2,1)}), bf16[8,48,3072]{2,1,0:T(8,128)(2,1)S(1)}, u32[]{:S(2)}, u32[]{:S(2)}) async-start(bf16[8,48,3072]{2,1,0:T(8,128)(2,1)} %bitcast.23), calls=%async_computation.1 | async-start | bytes 4718592 | tf_op jit(solution)/shard_map/all_to_all | solution.py:64
  83.5 1.5 fusion.39
  85.0 1.6 copy-done.1
  86.7 1.0 slice.60
  87.7 2.5 %collective-permute-start.2 = (bf16[128,3072]{1,0:T(8,128)(2,1)}, bf16[128,3072]{1,0:T(8,128)(2,1)}, u32[]{:S(2)}, u32[]{:S(2)}) collective-permute-start(bf16[128,3072]{1,0:T(8,128)(2,1)} %slice.60), channel_id=1, source_target_pairs={{0,1},{1,0},{2,3},{3,2},{4,5},{5,4},{6,7},{7,6},{8,9},{9,8},{10,11... | collective-permute-start | bytes 2359304 | tf_op jit(solution)/shard_map/ppermute | solution.py:75
  90.2 27.7 %all-to-all-done.1 = bf16[8,48,3072]{2,1,0:T(8,128)(2,1)S(1)} async-done(((bf16[8,48,3072]{2,1,0:T(8,128)(2,1)}), bf16[8,48,3072]{2,1,0:T(8,128)(2,1)S(1)}, u32[]{:S(2)}, u32[]{:S(2)}) %all-to-all-start.1) | async-done | bytes 2359328 | tf_op jit(solution)/shard_map/all_to_all | solution.py:64
  118.3 3.9 %collective-permute-start.4 = (bf16[48,3072]{1,0:T(8,128)(2,1)S(1)}, bf16[48,3072]{1,0:T(8,128)(2,1)S(1)}, u32[]{:S(2)}, u32[]{:S(2)}) collective-permute-start(bf16[48,3072]{1,0:T(8,128)(2,1)S(1)} %multiply_convert_fusion), channel_id=1, source_target_pairs={{0,64},{64,0},{1,65},{65,1},{2,66},{66,2},{3,67},{67,3},{4,68},{68... | collective-permute-start | bytes 884744 | tf_op jit(solution)/shard_map/ppermute | solution.py:66
  122.3 1.3 slice_add_fusion
  123.7 2.3 %collective-permute-start.3 = (bf16[64,3072]{1,0:T(8,128)(2,1)S(1)}, bf16[64,3072]{1,0:T(8,128)(2,1)}, u32[]{:S(2)}, u32[]{:S(2)}) collective-permute-start(bf16[64,3072]{1,0:T(8,128)(2,1)S(1)} %slice.61), channel_id=1, source_target_pairs={{0,32},{32,0},{1,33},{33,1},{2,34},{34,2},{3,35},{35,3},{4,36},{36... | collective-permute-start | bytes 1179656 | tf_op jit(solution)/shard_map/ppermute | solution.py:75
  126.0 2.9 %collective-permute-done.4 = bf16[48,3072]{1,0:T(8,128)(2,1)S(1)} collective-permute-done((bf16[48,3072]{1,0:T(8,128)(2,1)S(1)}, bf16[48,3072]{1,0:T(8,128)(2,1)S(1)}, u32[]{:S(2)}, u32[]{:S(2)}) %collective-permute-start.4) | collective-permute-done | bytes 294944 | tf_op jit(solution)/shard_map/ppermute | solution.py:66
  129.0 0.9 pad_maximum_fusion.2
  129.9 7.0 %collective-permute-done.3 = bf16[64,3072]{1,0:T(8,128)(2,1)} collective-permute-done((bf16[64,3072]{1,0:T(8,128)(2,1)S(1)}, bf16[64,3072]{1,0:T(8,128)(2,1)}, u32[]{:S(2)}, u32[]{:S(2)}) %collective-permute-start.3) | collective-permute-done | bytes 393248 | tf_op jit(solution)/shard_map/ppermute | solution.py:75
  136.9 1.1 fusion.12
  138.1 23.5 %all_to_all.10 = bf16[16,4,3072]{2,1,0:T(4,128)(2,1)S(1)} all-to-all(bf16[16,4,3072]{2,1,0:T(4,128)(2,1)S(1)} %reshape.37), channel_id=1, replica_groups=mesh['x'=4,'yh'=2,'yl'=2,'z'=16,'core'=2] {'z'}, dimensions={0} | all-to-all | bytes 786432 | tf_op jit(solution)/shard_map/all_to_all | solution.py:78
  162.8 4.3 %all-gather.3.cloned.1.call-done = bf16[8,48,3072]{2,1,0:T(8,128)(2,1)} async-done(((bf16[2,48,3072]{2,1,0:T(8,128)(2,1)}), bf16[8,48,3072]{2,1,0:T(8,128)(2,1)}) %all-gather.3.cloned.1.call-update) | async-done | bytes 2359312 | tf_op jit(solution)/shard_map/all_gather | solution.py:69
  167.0 3.2 %fusion.38 = (bf16[8,1,24,3072]{3,2,1,0:T(8,128)(2,1)}, bf16[8,1,24,3072]{3,2,1,0:T(8,128)(2,1)}) fusion(bf16[8,2,24,3072]{3,2,1,0:T(8,128)(2,1)} %bitcast.26), kind=kLoop, calls=%fused_computation.62 | loop fusion | bytes 4718592 | tf_op jit(solution)/shard_map/slice | solution.py:71
  (40 shorter events, 7.2 us)
Async XLA Ops:
  7.2 64.7 %copy-start = (bf16[3072,192]{0,1:T(8,128)(2,1)S(1)}, bf16[3072,192]{0,1:T(8,128)(2,1)}, u32[]{:S(2)}) copy-start(bf16[3072,192]{0,1:T(8,128)(2,1)} %param.7) | copy-start | bytes 3538948
  44.8 13.2 %collective-permute-start = (bf16[64,6144]{1,0:T(8,128)(2,1)S(1)}, bf16[64,6144]{1,0:T(8,128)(2,1)S(1)}, u32[]{:S(2)}, u32[]{:S(2)}) collective-permute-start(bf16[64,6144]{1,0:T(8,128)(2,1)S(1)} %reshape.41), channel_id=1, source_target_pairs={{0,32},{32,0},{1,33},{33,1},{2,34},{34,2},{3,35},{35,3},{4,36},{36... | collective-permute-start | bytes 2359304 | tf_op jit(solution)/shard_map/ppermute | solution.py:41
  58.1 13.6 %collective-permute-start.1 = (bf16[128,6144]{1,0:T(8,128)(2,1)S(1)}, bf16[128,6144]{1,0:T(8,128)(2,1)S(1)}, u32[]{:S(2)}, u32[]{:S(2)}) collective-permute-start(bf16[128,6144]{1,0:T(8,128)(2,1)S(1)} %pad_maximum_fusion.1), channel_id=1, source_target_pairs={{0,1},{1,0},{2,3},{3,2},{4,5},{5,4},{6,7},{7,6},{8,9},{9,8},{10,11... | collective-permute-start | bytes 4718600 | tf_op jit(solution)/shard_map/ppermute | solution.py:42
  72.6 1.3 copy-start.7
  74.5 0.6 copy-start.4
  76.8 41.1 %all-to-all-start.1 = ((bf16[8,48,3072]{2,1,0:T(8,128)(2,1)}), bf16[8,48,3072]{2,1,0:T(8,128)(2,1)S(1)}, u32[]{:S(2)}, u32[]{:S(2)}) async-start(bf16[8,48,3072]{2,1,0:T(8,128)(2,1)} %bitcast.23), calls=%async_computation.1 | async-start | bytes 4718592 | tf_op jit(solution)/shard_map/all_to_all | solution.py:64
  83.5 83.5 %all-gather.3.cloned.1.call-start = ((), (), s32[]{:S(2)}) async-start(), calls=%async_computation.2 | async-start | bytes 2949120 | tf_op jit(solution)/shard_map/all_gather | solution.py:69
  85.0 1.6 copy-start.1
  87.7 34.6 %collective-permute-start.2 = (bf16[128,3072]{1,0:T(8,128)(2,1)}, bf16[128,3072]{1,0:T(8,128)(2,1)}, u32[]{:S(2)}, u32[]{:S(2)}) collective-permute-start(bf16[128,3072]{1,0:T(8,128)(2,1)} %slice.60), channel_id=1, source_target_pairs={{0,1},{1,0},{2,3},{3,2},{4,5},{5,4},{6,7},{7,6},{8,9},{9,8},{10,11... | collective-permute-start | bytes 2359304 | tf_op jit(solution)/shard_map/ppermute | solution.py:75
  117.9 4.3 %copy-start.2 = (f32[256,3072]{1,0:T(8,128)S(1)}, f32[256,3072]{1,0:T(8,128)}, u32[]{:S(2)}) copy-start(f32[256,3072]{1,0:T(8,128)} %copy-done.1) | copy-start | bytes 9437188
  118.3 10.6 %collective-permute-start.4 = (bf16[48,3072]{1,0:T(8,128)(2,1)S(1)}, bf16[48,3072]{1,0:T(8,128)(2,1)S(1)}, u32[]{:S(2)}, u32[]{:S(2)}) collective-permute-start(bf16[48,3072]{1,0:T(8,128)(2,1)S(1)} %multiply_convert_fusion), channel_id=1, source_target_pairs={{0,64},{64,0},{1,65},{65,1},{2,66},{66,2},{3,67},{67,3},{4,68},{68... | collective-permute-start | bytes 884744 | tf_op jit(solution)/shard_map/ppermute | solution.py:66
  123.7 13.2 %collective-permute-start.3 = (bf16[64,3072]{1,0:T(8,128)(2,1)S(1)}, bf16[64,3072]{1,0:T(8,128)(2,1)}, u32[]{:S(2)}, u32[]{:S(2)}) collective-permute-start(bf16[64,3072]{1,0:T(8,128)(2,1)S(1)} %slice.61), channel_id=1, source_target_pairs={{0,32},{32,0},{1,33},{33,1},{2,34},{34,2},{3,35},{35,3},{4,36},{36... | collective-permute-start | bytes 1179656 | tf_op jit(solution)/shard_map/ppermute | solution.py:75
  129.9 31.9 %copy-start.3 = (bf16[4,3072]{1,0:T(4,128)(2,1)S(1)}, bf16[4,3072]{1,0:T(4,128)(2,1)}, u32[]{:S(2)}) copy-start(bf16[4,3072]{1,0:T(4,128)(2,1)} %param.5) | copy-start | bytes 73732
  129.9 31.9 %copy-start.5 = (f32[3072]{0:T(1024)S(1)}, f32[3072]{0:T(1024)}, u32[]{:S(2)}) copy-start(f32[3072]{0:T(1024)} %param.6) | copy-start | bytes 36868
  129.9 32.1 %copy-start.6 = (bf16[4,3072]{1,0:T(4,128)(2,1)S(1)}, bf16[4,3072]{1,0:T(4,128)(2,1)}, u32[]{:S(2)}) copy-start(bf16[4,3072]{1,0:T(4,128)(2,1)} %param.9) | copy-start | bytes 73732
Sparse Core Ops, SparseCore 0:
  130.0 37.0 all-gather.2

commit v2 on v1

--- a/solution.py
+++ b/solution.py
@@ -21,6 +21,10 @@
         1.0 + 3.0 * 0.044715 * value * value
     )
     return gelu, derivative
+
+
+def take(pairs, at):
+    return lax.dynamic_index_in_dim(pairs, at, 1, False, allow_negative_indices=False)
 
 
 def body(inputs, gain, w_in, w_out, cotangent):
@@ -53,30 +57,44 @@
     part_out = lax.dot_general(
         activated, grad_all, contract_first, preferred_element_type=jnp.float32
     ).astype(jnp.bfloat16)
+    parts = jnp.concatenate([part_in, part_out], axis=0).reshape(n_dp, -1, width)
+    parts, hidden_grad = lax.optimization_barrier((parts, hidden_grad))
+    parts = lax.all_to_all(parts, DP, 0, 0, tiled=True)
+
     whole_sum = lax.dot_general(
         hidden_grad, w_in, contract_last, preferred_element_type=jnp.float32
     )
-
-    block = hidden_units // n_dp
-    parts = jnp.stack(
-        [part_in.reshape(n_dp, block, width), part_out.reshape(n_dp, block, width)], axis=1
-    ).reshape(n_dp, 2 * block, width)
-    parts = lax.all_to_all(parts, DP, 0, 0, tiled=True)
-    mine = (jnp.sum(parts.astype(jnp.float32), axis=0) / n_dp).astype(jnp.bfloat16)
-    other = lax.ppermute(mine, "yh", SWAP)
-    first = lax.axis_index("yh") == 0
-    pair = jnp.stack([jnp.where(first, mine, other), jnp.where(first, other, mine)])
-    spread = lax.all_gather(pair, "x", axis=0, tiled=True).reshape(n_dp, 2, block, width)
-    grad_in = spread[:, 0].reshape(hidden_units, width).T
-    grad_out = spread[:, 1].reshape(hidden_units, width)
-
-    for axis in ("core", "yl"):
-        half = whole_sum.shape[0] // 2
-        away = lax.ppermute(whole_sum[half:].astype(jnp.bfloat16), axis, SWAP)
-        whole_sum = whole_sum[:half] + away.astype(jnp.float32)
-    terms = whole_sum.astype(jnp.bfloat16).reshape(n_z, rows, width)
-    terms = lax.all_to_all(terms, "z", 0, 0, tiled=True)
-    normed_grad = jnp.sum(terms.astype(jnp.float32), axis=0)
+    quarter = whole_sum.shape[0] // 4
+    size = quarter // 1
+    both_swapped = [(k, k ^ 3) for k in range(4)]
+    routes = (("yl", SWAP), ("core", SWAP), (("yl", "core"), both_swapped))
+    total = whole_sum[:quarter]
+    for k, (axis, pairs) in enumerate(routes, 1):
+        away = whole_sum[k * quarter : (k + 1) * quarter].astype(jnp.bfloat16)
+        away = [lax.ppermute(away[c : c + size], axis, pairs) for c in range(0, quarter, size)]
+        total = total + jnp.concatenate(away).astype(jnp.float32)
+    whole_sum = total
+    at = lax.axis_index("z").astype(jnp.uint32)
+    step, bit_at = 1, 0
+    while step < n_z:
+        if step == 2:
+            parts, _ = lax.optimization_barrier((parts, whole_sum))
+            mine = (jnp.sum(parts.astype(jnp.float32), axis=0) / n_dp).astype(jnp.bfloat16)
+            spread = jnp.broadcast_to(mine[None], (n_dp, *mine.shape))
+            spread, whole_sum = lax.optimization_barrier((spread, whole_sum))
+            spread = lax.all_to_all(spread, DP, 0, 0, tiled=True)
+        bit = (at >> bit_at) & 1
+        pairs = whole_sum.reshape(-1, 2, rows, width)
+        send = take(pairs, bit ^ 1).reshape(-1, width)
+        keep = take(pairs, bit).reshape(-1, width)
+        partners = [(z, z ^ step) for z in range(n_z)]
+        away = lax.ppermute(send.astype(jnp.bfloat16), "z", partners)
+        whole_sum = keep + away.astype(jnp.float32)
+        step, bit_at = 2 * step, bit_at + 1
+    normed_grad = whole_sum
+    spread = spread.reshape(2, hidden_units, width)
+    grad_in = spread[0].T
+    grad_out = spread[1]
     scaled = normed_grad * gain[None, :]
     first_mean = jnp.mean(scaled, axis=1, keepdims=True)
     second_mean = jnp.mean(scaled * normal, axis=1, keepdims=True)

time: 179 us -> 186 us (1.039)
  the two profiles are of different devices: /device:TPU:1 before, /device:TPU:24 now
where the time goes in v2:
time: 186 us; the launch traced here: 184 us
  starting transfers between devices  54.2 us (29%)
  waiting for transfers between devices  42.3 us (23%)
  blocking collectives  40.1 us (22%)
  local copies, waits for them, and re-layouts  26.4 us (14%)
  other arithmetic  15.8 us (8%)
  matrix products  4.62 us (2%)
    all_gather x1, blocking collectives, body(): both = lax.all_gather(both, 'z', axis=0, tiled=True)  40.1 us
    all_to_all x1, starting transfers between devices, body(): spread = lax.all_to_all(spread, DP, 0, 0, tiled=True)  19 us
    ppermute x4, starting transfers between devices, body(): away = lax.ppermute(send.astype(jnp.bfloat16), 'z', partners)  15.5 us
    ppermute x3, waiting for transfers between devices, body(): lax.ppermute(away[c:c + size], axis, pairs)  13.6 us
    ppermute x4, waiting for transfers between devices, body(): away = lax.ppermute(send.astype(jnp.bfloat16), 'z', partners)  12.9 us
    ppermute x1, waiting for transfers between devices, body(): both = jnp.concatenate([both, lax.ppermute(both, 'yl', SWAP)], axis=0)  11.5 us
    ppermute x3, starting transfers between devices, body(): lax.ppermute(away[c:c + size], axis, pairs)  7.86 us
    convert_element_type x7, local copies, waits for them, and re-layouts, body(): away = lax.ppermute(send.astype(jnp.bfloat16), 'z', partners)  7.85 us
  transfers between devices with their start and end apart: 11, of which 7 were waited for; matrix products, arithmetic and copies ran while one was open for 16% of the time, Pallas kernels for 0%

profile of v2, /device:TPU:24, one launch (start us, length us, event | category | flops | bytes accessed | tf_op | source)
XLA Modules:
  0.0 184.3 jit_solution(8746987358983210707)
XLA Ops:
  4.8 40.1 %all-gather = bf16[16,4,6144]{2,1,0:T(4,128)(2,1)S(1)} all-gather(bf16[1,4,6144]{2,1,0:T(4,128)(2,1)S(1)} %maximum_bitcast_fusion), channel_id=1, replica_groups=mesh['x'=4,'yh'=2,'yl'=2,'z'=16,'core'=2] {'z'}, dimensions={0}, use_global_device_ids=true | all-gather | bytes 835584 | tf_op jit(solution)/shard_map/all_gather | solution.py:44
  45.1 2.7 %collective-permute-start = (bf16[64,6144]{1,0:T(8,128)(2,1)S(1)}, bf16[64,6144]{1,0:T(8,128)(2,1)S(1)}, u32[]{:S(2)}, u32[]{:S(2)}) collective-permute-start(bf16[64,6144]{1,0:T(8,128)(2,1)S(1)} %reshape.90), channel_id=1, source_target_pairs={{0,32},{32,0},{1,33},{33,1},{2,34},{34,2},{3,35},{35,3},{4,36},{36... | collective-permute-start | bytes 2359304 | tf_op jit(solution)/shard_map/ppermute | solution.py:45
  47.7 11.5 %collective-permute-done = bf16[64,6144]{1,0:T(8,128)(2,1)S(1)} collective-permute-done((bf16[64,6144]{1,0:T(8,128)(2,1)S(1)}, bf16[64,6144]{1,0:T(8,128)(2,1)S(1)}, u32[]{:S(2)}, u32[]{:S(2)}) %collective-permute-start) | collective-permute-done | bytes 786464 | tf_op jit(solution)/shard_map/ppermute | solution.py:45
  59.3 1.9 %collective-permute-start.1 = (bf16[128,6144]{1,0:T(8,128)(2,1)S(1)}, bf16[128,6144]{1,0:T(8,128)(2,1)S(1)}, u32[]{:S(2)}, u32[]{:S(2)}) collective-permute-start(bf16[128,6144]{1,0:T(8,128)(2,1)S(1)} %pad_maximum_fusion.1), channel_id=1, source_target_pairs={{0,1},{1,0},{2,3},{3,2},{4,5},{5,4},{6,7},{7,6},{8,9},{9,8},{10,11... | collective-permute-start | bytes 4718600 | tf_op jit(solution)/shard_map/ppermute | solution.py:46
  61.4 3.3 %collective-permute-done.1 = bf16[128,6144]{1,0:T(8,128)(2,1)S(1)} collective-permute-done((bf16[128,6144]{1,0:T(8,128)(2,1)S(1)}, bf16[128,6144]{1,0:T(8,128)(2,1)S(1)}, u32[]{:S(2)}, u32[]{:S(2)}) %collective-permute-start.1) | collective-permute-done | bytes 1572896 | tf_op jit(solution)/shard_map/ppermute | solution.py:46
  68.9 2.2 %fusion.44 = (bf16[256,3072]{1,0:T(8,128)(2,1)S(1)}, f32[256,3072]{1,0:T(8,128)}) fusion(bf16[256,192]{0,1:T(8,128)(2,1)S(1)} %fusion.9, bf16[3072,192]{0,1:T(8,128)(2,1)S(1)} %copy-done), kind=kOutput, calls=%fused_computation.71 | convolution fusion | flops 302776320 | bytes 5996544 | tf_op jit(solution)/shard_map/dot_general | solution.py:64
  72.2 2.4 %collective-permute-start.4 = (bf16[64,3072]{1,0:T(8,128)(2,1)}, bf16[64,3072]{1,0:T(8,128)(2,1)}, u32[]{:S(2)}, u32[]{:S(2)}) collective-permute-start(bf16[64,3072]{1,0:T(8,128)(2,1)} %get-tuple-element.18), channel_id=1, source_target_pairs={{0,33},{1,32},{32,1},{33,0},{2,35},{3,34},{34,3},{35,2},{4,37},{5,... | collective-permute-start | bytes 1179656 | tf_op jit(solution)/shard_map/ppermute | solution.py:74
  74.6 2.3 %collective-permute-start.3 = (bf16[64,3072]{1,0:T(8,128)(2,1)}, bf16[64,3072]{1,0:T(8,128)(2,1)}, u32[]{:S(2)}, u32[]{:S(2)}) collective-permute-start(bf16[64,3072]{1,0:T(8,128)(2,1)} %get-tuple-element.19), channel_id=1, source_target_pairs={{0,1},{1,0},{2,3},{3,2},{4,5},{5,4},{6,7},{7,6},{8,9},{9,8},{10,11... | collective-permute-start | bytes 1179656 | tf_op jit(solution)/shard_map/ppermute | solution.py:74
  76.9 3.2 %collective-permute-start.2 = (bf16[64,3072]{1,0:T(8,128)(2,1)}, bf16[64,3072]{1,0:T(8,128)(2,1)}, u32[]{:S(2)}, u32[]{:S(2)}) collective-permute-start(bf16[64,3072]{1,0:T(8,128)(2,1)} %get-tuple-element.17), channel_id=1, source_target_pairs={{0,32},{32,0},{1,33},{33,1},{2,34},{34,2},{3,35},{35,3},{4,36},{36... | collective-permute-start | bytes 1179656 | tf_op jit(solution)/shard_map/ppermute | solution.py:74
  80.1 7.3 %all-to-all-start = ((bf16[8,48,3072]{2,1,0:T(8,128)(2,1)}), bf16[8,48,3072]{2,1,0:T(8,128)(2,1)S(1)}, u32[]{:S(2)}, u32[]{:S(2)}) async-start(bf16[8,48,3072]{2,1,0:T(8,128)(2,1)} %bitcast.1), calls=%async_computation | async-start | bytes 4718592 | tf_op jit(solution)/shard_map/all_to_all | solution.py:62
  87.4 13.6 %collective-permute-done.2 = bf16[64,3072]{1,0:T(8,128)(2,1)} collective-permute-done((bf16[64,3072]{1,0:T(8,128)(2,1)}, bf16[64,3072]{1,0:T(8,128)(2,1)}, u32[]{:S(2)}, u32[]{:S(2)}) %collective-permute-start.2) | collective-permute-done | bytes 393248 | tf_op jit(solution)/shard_map/ppermute | solution.py:74
  101.0 2.5 %fusion.13 = f32[64,3072]{1,0:T(8,128)} fusion(f32[256,3072]{1,0:T(8,128)} %get-tuple-element.21, bf16[64,3072]{1,0:T(8,128)(2,1)} %collective-permute-done.4, bf16[64,3072]{1,0:T(8,128)(2,1)} %collective-permute-done.3, bf16[64,3072]{1,0:T(8,128)(2,1)} %collective-permute-done.2), kind=kLoop, calls=%fused_computation.15 | loop fusion | flops 1179648 | bytes 2752512 | tf_op jit(solution)/shard_map/add | solution.py:75
  103.5 2.2 %reshape.81 = f32[8,2,4,3072]{3,2,1,0:T(4,128)} reshape(f32[64,3072]{1,0:T(8,128)} %fusion.13) | data formatting | bytes 1572864 | tf_op jit(solution)/shard_map/reshape | solution.py:87
  109.1 1.9 %collective-permute-start.5 = (bf16[32,3072]{1,0:T(8,128)(2,1)}, bf16[32,3072]{1,0:T(8,128)(2,1)}, u32[]{:S(2)}, u32[]{:S(2)}) collective-permute-start(bf16[32,3072]{1,0:T(8,128)(2,1)} %convert_element_type.97), channel_id=1, source_target_pairs={{0,2},{2,0},{4,6},{6,4},{8,10},{10,8},{12,14},{14,12},{16,18},{18,... | collective-permute-start | bytes 589832 | tf_op jit(solution)/shard_map/ppermute | solution.py:91
  111.0 1.8 constant_dynamic-slice_fusion.2
  112.8 1.9 %reshape.82 = f32[32,3072]{1,0:T(8,128)} reshape(f32[8,1,4,3072]{3,2,1,0:T(4,128)} %constant_dynamic-slice_fusion.2) | data formatting | bytes 786432 | tf_op jit(solution)/shard_map/reshape | solution.py:89
  114.7 2.8 %collective-permute-done.5 = bf16[32,3072]{1,0:T(8,128)(2,1)} collective-permute-done((bf16[32,3072]{1,0:T(8,128)(2,1)}, bf16[32,3072]{1,0:T(8,128)(2,1)}, u32[]{:S(2)}, u32[]{:S(2)}) %collective-permute-start.5) | collective-permute-done | bytes 196640 | tf_op jit(solution)/shard_map/ppermute | solution.py:91
  117.5 1.8 convert_add_fusion
  123.3 2.1 %collective-permute-start.6 = (bf16[16,3072]{1,0:T(8,128)(2,1)}, bf16[16,3072]{1,0:T(8,128)(2,1)}, u32[]{:S(2)}, u32[]{:S(2)}) collective-permute-start(bf16[16,3072]{1,0:T(8,128)(2,1)} %convert_element_type.102), channel_id=1, source_target_pairs={{0,4},{2,6},{4,0},{6,2},{8,12},{10,14},{12,8},{14,10},{16,20},{18,... | collective-permute-start | bytes 294920 | tf_op jit(solution)/shard_map/ppermute | solution.py:91
  126.2 19.0 %all-to-all-start.1 = ((bf16[8,48,3072]{2,1,0:T(8,128)(2,1)}), bf16[8,48,3072]{2,1,0:T(8,128)(2,1)S(1)}, u32[]{:S(2)}, u32[]{:S(2)}) async-start(bf16[8,48,3072]{2,1,0:T(8,128)(2,1)} %broadcast_in_dim.2), calls=%async_computation.1 | async-start | bytes 4718592 | tf_op jit(solution)/shard_map/all_to_all | solution.py:85
  151.5 4.5 %collective-permute-start.7 = (bf16[8,3072]{1,0:T(8,128)(2,1)}, bf16[8,3072]{1,0:T(8,128)(2,1)}, u32[]{:S(2)}, u32[]{:S(2)}) collective-permute-start(bf16[8,3072]{1,0:T(8,128)(2,1)} %convert_element_type.105), channel_id=1, source_target_pairs={{0,8},{2,10},{4,12},{6,14},{8,0},{10,2},{12,4},{14,6},{16,24},{18,... | collective-permute-start | bytes 147464 | tf_op jit(solution)/shard_map/ppermute | solution.py:91
  159.1 2.7 %collective-permute-done.7 = bf16[8,3072]{1,0:T(8,128)(2,1)} collective-permute-done((bf16[8,3072]{1,0:T(8,128)(2,1)}, bf16[8,3072]{1,0:T(8,128)(2,1)}, u32[]{:S(2)}, u32[]{:S(2)}) %collective-permute-start.7) | collective-permute-done | bytes 49184 | tf_op jit(solution)/shard_map/ppermute | solution.py:91
  165.6 7.0 %collective-permute-start.8 = (bf16[4,3072]{1,0:T(4,128)(2,1)S(1)}, bf16[4,3072]{1,0:T(4,128)(2,1)S(1)}, u32[]{:S(2)}, u32[]{:S(2)}) collective-permute-start(bf16[4,3072]{1,0:T(4,128)(2,1)S(1)} %fusion.36), channel_id=1, source_target_pairs={{0,16},{2,18},{4,20},{6,22},{8,24},{10,26},{12,28},{14,30},{16,0},... | collective-permute-start | bytes 73736 | tf_op jit(solution)/shard_map/ppermute | solution.py:91
  172.6 7.5 %collective-permute-done.8 = bf16[4,3072]{1,0:T(4,128)(2,1)S(1)} collective-permute-done((bf16[4,3072]{1,0:T(4,128)(2,1)S(1)}, bf16[4,3072]{1,0:T(4,128)(2,1)S(1)}, u32[]{:S(2)}, u32[]{:S(2)}) %collective-permute-start.8) | collective-permute-done | bytes 24608 | tf_op jit(solution)/shard_map/ppermute | solution.py:91
  (55 shorter events, 35.5 us)
Async XLA Ops:
  0.6 64.1 %copy-start = (bf16[3072,192]{0,1:T(8,128)(2,1)S(1)}, bf16[3072,192]{0,1:T(8,128)(2,1)}, u32[]{:S(2)}) copy-start(bf16[3072,192]{0,1:T(8,128)(2,1)} %param.7) | copy-start | bytes 3538948
  2.6 0.6 copy-start.3
  45.1 14.1 %collective-permute-start = (bf16[64,6144]{1,0:T(8,128)(2,1)S(1)}, bf16[64,6144]{1,0:T(8,128)(2,1)S(1)}, u32[]{:S(2)}, u32[]{:S(2)}) collective-permute-start(bf16[64,6144]{1,0:T(8,128)(2,1)S(1)} %reshape.90), channel_id=1, source_target_pairs={{0,32},{32,0},{1,33},{33,1},{2,34},{34,2},{3,35},{35,3},{4,36},{36... | collective-permute-start | bytes 2359304 | tf_op jit(solution)/shard_map/ppermute | solution.py:45
  59.3 5.3 %collective-permute-start.1 = (bf16[128,6144]{1,0:T(8,128)(2,1)S(1)}, bf16[128,6144]{1,0:T(8,128)(2,1)S(1)}, u32[]{:S(2)}, u32[]{:S(2)}) collective-permute-start(bf16[128,6144]{1,0:T(8,128)(2,1)S(1)} %pad_maximum_fusion.1), channel_id=1, source_target_pairs={{0,1},{1,0},{2,3},{3,2},{4,5},{5,4},{6,7},{7,6},{8,9},{9,8},{10,11... | collective-permute-start | bytes 4718600 | tf_op jit(solution)/shard_map/ppermute | solution.py:46
  64.8 1.3 copy-start.4
  72.2 15.2 %collective-permute-start.4 = (bf16[64,3072]{1,0:T(8,128)(2,1)}, bf16[64,3072]{1,0:T(8,128)(2,1)}, u32[]{:S(2)}, u32[]{:S(2)}) collective-permute-start(bf16[64,3072]{1,0:T(8,128)(2,1)} %get-tuple-element.18), channel_id=1, source_target_pairs={{0,33},{1,32},{32,1},{33,0},{2,35},{3,34},{34,3},{35,2},{4,37},{5,... | collective-permute-start | bytes 1179656 | tf_op jit(solution)/shard_map/ppermute | solution.py:74
  74.6 12.8 %collective-permute-start.3 = (bf16[64,3072]{1,0:T(8,128)(2,1)}, bf16[64,3072]{1,0:T(8,128)(2,1)}, u32[]{:S(2)}, u32[]{:S(2)}) collective-permute-start(bf16[64,3072]{1,0:T(8,128)(2,1)} %get-tuple-element.19), channel_id=1, source_target_pairs={{0,1},{1,0},{2,3},{3,2},{4,5},{5,4},{6,7},{7,6},{8,9},{9,8},{10,11... | collective-permute-start | bytes 1179656 | tf_op jit(solution)/shard_map/ppermute | solution.py:74
  76.9 24.1 %collective-permute-start.2 = (bf16[64,3072]{1,0:T(8,128)(2,1)}, bf16[64,3072]{1,0:T(8,128)(2,1)}, u32[]{:S(2)}, u32[]{:S(2)}) collective-permute-start(bf16[64,3072]{1,0:T(8,128)(2,1)} %get-tuple-element.17), channel_id=1, source_target_pairs={{0,32},{32,0},{1,33},{33,1},{2,34},{34,2},{3,35},{35,3},{4,36},{36... | collective-permute-start | bytes 1179656 | tf_op jit(solution)/shard_map/ppermute | solution.py:74
  80.1 40.3 %all-to-all-start = ((bf16[8,48,3072]{2,1,0:T(8,128)(2,1)}), bf16[8,48,3072]{2,1,0:T(8,128)(2,1)S(1)}, u32[]{:S(2)}, u32[]{:S(2)}) async-start(bf16[8,48,3072]{2,1,0:T(8,128)(2,1)} %bitcast.1), calls=%async_computation | async-start | bytes 4718592 | tf_op jit(solution)/shard_map/all_to_all | solution.py:62
  109.1 8.3 %collective-permute-start.5 = (bf16[32,3072]{1,0:T(8,128)(2,1)}, bf16[32,3072]{1,0:T(8,128)(2,1)}, u32[]{:S(2)}, u32[]{:S(2)}) collective-permute-start(bf16[32,3072]{1,0:T(8,128)(2,1)} %convert_element_type.97), channel_id=1, source_target_pairs={{0,2},{2,0},{4,6},{6,4},{8,10},{10,8},{12,14},{14,12},{16,18},{18,... | collective-permute-start | bytes 589832 | tf_op jit(solution)/shard_map/ppermute | solution.py:91
  120.7 1.8 copy-start.1
  123.3 21.9 %collective-permute-start.6 = (bf16[16,3072]{1,0:T(8,128)(2,1)}, bf16[16,3072]{1,0:T(8,128)(2,1)}, u32[]{:S(2)}, u32[]{:S(2)}) collective-permute-start(bf16[16,3072]{1,0:T(8,128)(2,1)} %convert_element_type.102), channel_id=1, source_target_pairs={{0,4},{2,6},{4,0},{6,2},{8,12},{10,14},{12,8},{14,10},{16,20},{18,... | collective-permute-start | bytes 294920 | tf_op jit(solution)/shard_map/ppermute | solution.py:91
  126.2 53.9 %copy-start.2 = (f32[3072]{0:T(1024)S(1)}, f32[3072]{0:T(1024)}, u32[]{:S(2)}) copy-start(f32[3072]{0:T(1024)} %param.6) | copy-start | bytes 36868
  126.2 56.5 %all-to-all-start.1 = ((bf16[8,48,3072]{2,1,0:T(8,128)(2,1)}), bf16[8,48,3072]{2,1,0:T(8,128)(2,1)S(1)}, u32[]{:S(2)}, u32[]{:S(2)}) async-start(bf16[8,48,3072]{2,1,0:T(8,128)(2,1)} %broadcast_in_dim.2), calls=%async_computation.1 | async-start | bytes 4718592 | tf_op jit(solution)/shard_map/all_to_all | solution.py:85
  151.5 10.2 %collective-permute-start.7 = (bf16[8,3072]{1,0:T(8,128)(2,1)}, bf16[8,3072]{1,0:T(8,128)(2,1)}, u32[]{:S(2)}, u32[]{:S(2)}) collective-permute-start(bf16[8,3072]{1,0:T(8,128)(2,1)} %convert_element_type.105), channel_id=1, source_target_pairs={{0,8},{2,10},{4,12},{6,14},{8,0},{10,2},{12,4},{14,6},{16,24},{18,... | collective-permute-start | bytes 147464 | tf_op jit(solution)/shard_map/ppermute | solution.py:91
  165.6 14.4 %collective-permute-start.8 = (bf16[4,3072]{1,0:T(4,128)(2,1)S(1)}, bf16[4,3072]{1,0:T(4,128)(2,1)S(1)}, u32[]{:S(2)}, u32[]{:S(2)}) collective-permute-start(bf16[4,3072]{1,0:T(4,128)(2,1)S(1)} %fusion.36), channel_id=1, source_target_pairs={{0,16},{2,18},{4,20},{6,22},{8,24},{10,26},{12,28},{14,30},{16,0},... | collective-permute-start | bytes 73736 | tf_op jit(solution)/shard_map/ppermute | solution.py:91

commit v3 on v1

--- a/solution.py
+++ b/solution.py
@@ -23,9 +23,32 @@
     return gelu, derivative
 
 
+STAGES = (("core", 1), ("z", 1), ("yl", 1), ("z", 2), ("z", 4), ("z", 8))
+
+
+def partner(axis, step):
+    return [(at, at ^ step) for at in range(lax.axis_size(axis))]
+
+
+def stage_order(rows, n_z):
+    at = lax.broadcasted_iota(jnp.int32, (4 * n_z * rows, 4 * n_z * rows), 0)
+    column = lax.broadcasted_iota(jnp.int32, at.shape, 1)
+    old = at % rows
+    far = jnp.zeros_like(at)
+    block = at.shape[0]
+    for axis, step in STAGES:
+        block //= 2
+        bit = (at // block) % 2
+        if axis == "z":
+            far = far + bit * step
+        else:
+            old = old + bit * (n_z * rows * (2 if axis == "core" else 1))
+    old = old + (far ^ lax.axis_index("z")) * rows
+    return (old == column).astype(jnp.bfloat16)
+
+
 def body(inputs, gain, w_in, w_out, cotangent):
     rows, width = inputs.shape
-    hidden_units = w_out.shape[0]
     n_dp = lax.axis_size(DP)
     n_z = lax.axis_size("z")
     widened = inputs.astype(jnp.float32)
@@ -47,36 +70,41 @@
     activated = gelu.astype(jnp.bfloat16)
     act_grad = lax.dot_general(grad_all, w_out, contract_last, preferred_element_type=jnp.float32)
     hidden_grad = (act_grad * derivative).astype(jnp.bfloat16)
+    order = stage_order(rows, n_z)
+    ordered = jnp.dot(order, hidden_grad, preferred_element_type=jnp.float32).astype(jnp.bfloat16)
+    half = ordered.shape[0] // 2
+    send = lax.dot_general(
+        ordered[half:], w_in, contract_last, preferred_element_type=jnp.float32
+    ).astype(jnp.bfloat16)
+
+    activated, hidden_grad, send = lax.optimization_barrier((activated, hidden_grad, send))
     part_in = lax.dot_general(
         hidden_grad, normed_all, contract_first, preferred_element_type=jnp.float32
     ).astype(jnp.bfloat16)
     part_out = lax.dot_general(
         activated, grad_all, contract_first, preferred_element_type=jnp.float32
     ).astype(jnp.bfloat16)
-    whole_sum = lax.dot_general(
-        hidden_grad, w_in, contract_last, preferred_element_type=jnp.float32
-    )
+    parts = jnp.concatenate([part_in, part_out], axis=0).reshape(n_dp, -1, width)
+    parts, ordered = lax.optimization_barrier((parts, ordered))
+    parts = lax.all_to_all(parts, DP, 0, 0, tiled=True)
 
-    block = hidden_units // n_dp
-    parts = jnp.stack(
-        [part_in.reshape(n_dp, block, width), part_out.reshape(n_dp, block, width)], axis=1
-    ).reshape(n_dp, 2 * block, width)
-    parts = lax.all_to_all(parts, DP, 0, 0, tiled=True)
-    mine = (jnp.sum(parts.astype(jnp.float32), axis=0) / n_dp).astype(jnp.bfloat16)
-    other = lax.ppermute(mine, "yh", SWAP)
-    first = lax.axis_index("yh") == 0
-    pair = jnp.stack([jnp.where(first, mine, other), jnp.where(first, other, mine)])
-    spread = lax.all_gather(pair, "x", axis=0, tiled=True).reshape(n_dp, 2, block, width)
-    grad_in = spread[:, 0].reshape(hidden_units, width).T
-    grad_out = spread[:, 1].reshape(hidden_units, width)
-
-    for axis in ("core", "yl"):
-        half = whole_sum.shape[0] // 2
-        away = lax.ppermute(whole_sum[half:].astype(jnp.bfloat16), axis, SWAP)
-        whole_sum = whole_sum[:half] + away.astype(jnp.float32)
-    terms = whole_sum.astype(jnp.bfloat16).reshape(n_z, rows, width)
-    terms = lax.all_to_all(terms, "z", 0, 0, tiled=True)
-    normed_grad = jnp.sum(terms.astype(jnp.float32), axis=0)
+    keep = lax.dot_general(ordered[:half], w_in, contract_last, preferred_element_type=jnp.float32)
+    for k, (axis, step) in enumerate(STAGES):
+        away = lax.ppermute(send, axis, partner(axis, step))
+        half = half // 2
+        total = keep + away.astype(jnp.float32)
+        if k == 2:
+            parts, _ = lax.optimization_barrier((parts, total))
+            mine = (jnp.sum(parts.astype(jnp.float32), axis=0) / n_dp).astype(jnp.bfloat16)
+            spread = jnp.broadcast_to(mine[None], (n_dp, *mine.shape))
+        if k == 2:
+            spread, total = lax.optimization_barrier((spread, total))
+            spread = lax.all_to_all(spread, DP, 0, 0, tiled=True)
+        keep, send = total[:half], total[half:].astype(jnp.bfloat16)
+    normed_grad = total
+    spread = spread.reshape(2, -1, width)
+    grad_in = spread[0].T
+    grad_out = spread[1]
     scaled = normed_grad * gain[None, :]
     first_mean = jnp.mean(scaled, axis=1, keepdims=True)
     second_mean = jnp.mean(scaled * normal, axis=1, keepdims=True)

time: 179 us -> 164 us (0.916)
  blocking collectives: 57.4 us -> 33.9 us
  starting transfers between devices: 29.3 us -> 43.5 us
  between operations: 14.3 us -> 0.97 us
  waiting for transfers between devices: 54.8 us -> 61.4 us
  matrix products: 3.86 us -> 6.48 us
    ppermute x3 -> x6, waiting for transfers between devices: 9.89 us -> 40.1 us  [body(): away = lax.ppermute(send, axis, partner(axis, step))]
    all_to_all x1, waiting for transfers between devices: 27.7 us -> 3.04 us  [body(): parts = lax.all_to_all(parts, DP, 0, 0, tiled=True)]
    all_to_all x1 -> x0, blocking collectives: 23.5 us -> none  [body(): terms = lax.all_to_all(terms, 'z', 0, 0, tiled=True)]
    ppermute x3 -> x6, starting transfers between devices: 8.8 us -> 18.3 us  [body(): away = lax.ppermute(send, axis, partner(axis, step))]
    all_to_all x0 -> x1, waiting for transfers between devices: none -> 5.54 us  [body(): spread = lax.all_to_all(spread, DP, 0, 0, tiled=True)]
    all_to_all x0 -> x1, starting transfers between devices: none -> 4.79 us  [body(): spread = lax.all_to_all(spread, DP, 0, 0, tiled=True)]
    all_gather x1 -> x0, waiting for transfers between devices: 4.29 us -> none  [body(): lax.all_gather(pair, 'x', axis=0, tiled=True).reshape(n_dp, 2, block, width)]
    dot_general x1 -> x3, matrix products: 1.49 us -> 4.12 us  [the longest x1 1.55 us: body(): lax.dot_general(ordered[:half], w_in, contract_last, preferred_element_ty...]
  transfers between devices with their start and end apart: 7 -> 10, of which waited for: 6 -> 9; matrix products, arithmetic and copies ran while one was open for 4% -> 5% of each run, Pallas kernels for 0% -> 0%
where the time goes in v3:
time: 164 us; the launch traced here: 163 us
  waiting for transfers between devices  61.4 us (37%)
  starting transfers between devices  43.5 us (27%)
  blocking collectives  33.9 us (21%)
  other arithmetic  9.96 us (6%)
  local copies, waits for them, and re-layouts  6.52 us (4%)
  matrix products  6.48 us (4%)
    ppermute x6, waiting for transfers between devices, body(): away = lax.ppermute(send, axis, partner(axis, step))  40.1 us
    all_gather x1, blocking collectives, body(): both = lax.all_gather(both, 'z', axis=0, tiled=True)  33.9 us
    ppermute x6, starting transfers between devices, body(): away = lax.ppermute(send, axis, partner(axis, step))  18.3 us
    ppermute x1, starting transfers between devices, body(): both = jnp.concatenate([both, lax.ppermute(both, 'core', SWAP)], axis=0)  10.6 us
    ppermute x1, waiting for transfers between devices, body(): both = jnp.concatenate([both, lax.ppermute(both, 'yl', SWAP)], axis=0)  9.86 us
    all_to_all x1, starting transfers between devices, body(): parts = lax.all_to_all(parts, DP, 0, 0, tiled=True)  6.65 us
    all_to_all x1, waiting for transfers between devices, body(): spread = lax.all_to_all(spread, DP, 0, 0, tiled=True)  5.54 us
    all_to_all x1, starting transfers between devices, body(): spread = lax.all_to_all(spread, DP, 0, 0, tiled=True)  4.79 us
  transfers between devices with their start and end apart: 10, of which 9 were waited for; matrix products, arithmetic and copies ran while one was open for 5% of the time, Pallas kernels for 0%

profile of v3, /device:TPU:1, one launch (start us, length us, event | category | flops | bytes accessed | tf_op | source)
XLA Modules:
  0.0 162.8 jit_solution(5363280298442298010)
XLA Ops:
  4.7 33.9 %all-gather = bf16[16,4,6144]{2,1,0:T(4,128)(2,1)S(1)} all-gather(bf16[1,4,6144]{2,1,0:T(4,128)(2,1)S(1)} %maximum_bitcast_fusion), channel_id=1, replica_groups=mesh['x'=4,'yh'=2,'yl'=2,'z'=16,'core'=2] {'z'}, dimensions={0}, use_global_device_ids=true | all-gather | bytes 835584 | tf_op jit(solution)/shard_map/all_gather | solution.py:63
  38.8 3.2 %collective-permute-start = (bf16[64,6144]{1,0:T(8,128)(2,1)S(1)}, bf16[64,6144]{1,0:T(8,128)(2,1)S(1)}, u32[]{:S(2)}, u32[]{:S(2)}) collective-permute-start(bf16[64,6144]{1,0:T(8,128)(2,1)S(1)} %reshape.42), channel_id=1, source_target_pairs={{0,32},{32,0},{1,33},{33,1},{2,34},{34,2},{3,35},{35,3},{4,36},{36... | collective-permute-start | bytes 2359304 | tf_op jit(solution)/shard_map/ppermute | solution.py:64
  42.1 9.9 %collective-permute-done = bf16[64,6144]{1,0:T(8,128)(2,1)S(1)} collective-permute-done((bf16[64,6144]{1,0:T(8,128)(2,1)S(1)}, bf16[64,6144]{1,0:T(8,128)(2,1)S(1)}, u32[]{:S(2)}, u32[]{:S(2)}) %collective-permute-start) | collective-permute-done | bytes 786464 | tf_op jit(solution)/shard_map/ppermute | solution.py:64
  52.1 10.6 %collective-permute-start.1 = (bf16[128,6144]{1,0:T(8,128)(2,1)S(1)}, bf16[128,6144]{1,0:T(8,128)(2,1)S(1)}, u32[]{:S(2)}, u32[]{:S(2)}) collective-permute-start(bf16[128,6144]{1,0:T(8,128)(2,1)S(1)} %pad_maximum_fusion.1), channel_id=1, source_target_pairs={{0,1},{1,0},{2,3},{3,2},{4,5},{5,4},{6,7},{7,6},{8,9},{9,8},{10,11... | collective-permute-start | bytes 4718600 | tf_op jit(solution)/shard_map/ppermute | solution.py:65
  62.8 2.9 %collective-permute-done.1 = bf16[128,6144]{1,0:T(8,128)(2,1)S(1)} collective-permute-done((bf16[128,6144]{1,0:T(8,128)(2,1)S(1)}, bf16[128,6144]{1,0:T(8,128)(2,1)S(1)}, u32[]{:S(2)}, u32[]{:S(2)}) %collective-permute-start.1) | collective-permute-done | bytes 1572896 | tf_op jit(solution)/shard_map/ppermute | solution.py:65
  70.4 2.2 %collective-permute-start.2 = (bf16[128,3072]{1,0:T(8,128)(2,1)}, bf16[128,3072]{1,0:T(8,128)(2,1)}, u32[]{:S(2)}, u32[]{:S(2)}) collective-permute-start(bf16[128,3072]{1,0:T(8,128)(2,1)} %convolution_convert_fusion.2), channel_id=1, source_target_pairs={{0,1},{1,0},{2,3},{3,2},{4,5},{5,4},{6,7},{7,6},{8,9},{9,8},{10,11... | collective-permute-start | bytes 2359304 | tf_op jit(solution)/shard_map/ppermute | solution.py:93
  73.6 1.6 pad_maximum_fusion
  75.2 6.6 %all-to-all-start = ((bf16[8,48,3072]{2,1,0:T(8,128)(2,1)}), bf16[8,48,3072]{2,1,0:T(8,128)(2,1)S(1)}, u32[]{:S(2)}, u32[]{:S(2)}) async-start(bf16[8,48,3072]{2,1,0:T(8,128)(2,1)} %bitcast.14), calls=%async_computation | async-start | bytes 4718592 | tf_op jit(solution)/shard_map/all_to_all | solution.py:89
  83.5 1.9 %collective-permute-start.3 = (bf16[64,3072]{1,0:T(8,128)(2,1)S(1)}, bf16[64,3072]{1,0:T(8,128)(2,1)S(1)}, u32[]{:S(2)}, u32[]{:S(2)}) collective-permute-start(bf16[64,3072]{1,0:T(8,128)(2,1)S(1)} %slice.121), channel_id=1, source_target_pairs={{0,2},{2,0},{4,6},{6,4},{8,10},{10,8},{12,14},{14,12},{16,18},{18,... | collective-permute-start | bytes 1179656 | tf_op jit(solution)/shard_map/ppermute | solution.py:93
  85.4 10.2 %collective-permute-done.3 = bf16[64,3072]{1,0:T(8,128)(2,1)S(1)} collective-permute-done((bf16[64,3072]{1,0:T(8,128)(2,1)S(1)}, bf16[64,3072]{1,0:T(8,128)(2,1)S(1)}, u32[]{:S(2)}, u32[]{:S(2)}) %collective-permute-start.3) | collective-permute-done | bytes 393248 | tf_op jit(solution)/shard_map/ppermute | solution.py:93
  95.7 2.4 %collective-permute-start.4 = (bf16[32,3072]{1,0:T(8,128)(2,1)S(1)}, bf16[32,3072]{1,0:T(8,128)(2,1)S(1)}, u32[]{:S(2)}, u32[]{:S(2)}) collective-permute-start(bf16[32,3072]{1,0:T(8,128)(2,1)S(1)} %slice.122), channel_id=1, source_target_pairs={{0,32},{32,0},{1,33},{33,1},{2,34},{34,2},{3,35},{35,3},{4,36},{36... | collective-permute-start | bytes 589832 | tf_op jit(solution)/shard_map/ppermute | solution.py:93
  98.1 14.6 %collective-permute-done.4 = bf16[32,3072]{1,0:T(8,128)(2,1)S(1)} collective-permute-done((bf16[32,3072]{1,0:T(8,128)(2,1)S(1)}, bf16[32,3072]{1,0:T(8,128)(2,1)S(1)}, u32[]{:S(2)}, u32[]{:S(2)}) %collective-permute-start.4) | collective-permute-done | bytes 196640 | tf_op jit(solution)/shard_map/ppermute | solution.py:93
  113.4 3.0 %all-to-all-done = bf16[8,48,3072]{2,1,0:T(8,128)(2,1)S(1)} async-done(((bf16[8,48,3072]{2,1,0:T(8,128)(2,1)}), bf16[8,48,3072]{2,1,0:T(8,128)(2,1)S(1)}, u32[]{:S(2)}, u32[]{:S(2)}) %all-to-all-start) | async-done | bytes 2359328 | tf_op jit(solution)/shard_map/all_to_all | solution.py:89
  116.8 1.7 %broadcast_in_dim.2 = bf16[8,48,3072]{2,1,0:T(8,128)(2,1)} broadcast(bf16[48,3072]{1,0:T(8,128)(2,1)S(1)} %multiply_convert_fusion), dimensions={1,2} | broadcast | bytes 2654208 | tf_op jit(solution)/shard_map/broadcast_in_dim | solution.py:99
  118.5 1.6 slice.123
  120.1 2.0 %collective-permute-start.5 = (bf16[16,3072]{1,0:T(8,128)(2,1)}, bf16[16,3072]{1,0:T(8,128)(2,1)}, u32[]{:S(2)}, u32[]{:S(2)}) collective-permute-start(bf16[16,3072]{1,0:T(8,128)(2,1)} %slice.123), channel_id=1, source_target_pairs={{0,4},{2,6},{4,0},{6,2},{8,12},{10,14},{12,8},{14,10},{16,20},{18,... | collective-permute-start | bytes 294920 | tf_op jit(solution)/shard_map/ppermute | solution.py:93
  122.2 4.8 %all-to-all-start.1 = ((bf16[8,48,3072]{2,1,0:T(8,128)(2,1)}), bf16[8,48,3072]{2,1,0:T(8,128)(2,1)S(1)}, u32[]{:S(2)}, u32[]{:S(2)}) async-start(bf16[8,48,3072]{2,1,0:T(8,128)(2,1)} %broadcast_in_dim.2), calls=%async_computation.1 | async-start | bytes 4718592 | tf_op jit(solution)/shard_map/all_to_all | solution.py:102
  127.0 1.6 collective-permute-done.5
  129.5 4.2 %collective-permute-start.6 = (bf16[8,3072]{1,0:T(8,128)(2,1)S(1)}, bf16[8,3072]{1,0:T(8,128)(2,1)S(1)}, u32[]{:S(2)}, u32[]{:S(2)}) collective-permute-start(bf16[8,3072]{1,0:T(8,128)(2,1)S(1)} %slice.124), channel_id=1, source_target_pairs={{0,8},{2,10},{4,12},{6,14},{8,0},{10,2},{12,4},{14,6},{16,24},{18,... | collective-permute-start | bytes 147464 | tf_op jit(solution)/shard_map/ppermute | solution.py:93
  133.7 6.1 %collective-permute-done.6 = bf16[8,3072]{1,0:T(8,128)(2,1)S(1)} collective-permute-done((bf16[8,3072]{1,0:T(8,128)(2,1)S(1)}, bf16[8,3072]{1,0:T(8,128)(2,1)S(1)}, u32[]{:S(2)}, u32[]{:S(2)}) %collective-permute-start.6) | collective-permute-done | bytes 49184 | tf_op jit(solution)/shard_map/ppermute | solution.py:93
  139.8 5.6 %collective-permute-start.7 = (bf16[4,3072]{1,0:T(4,128)(2,1)S(1)}, bf16[4,3072]{1,0:T(4,128)(2,1)S(1)}, u32[]{:S(2)}, u32[]{:S(2)}) collective-permute-start(bf16[4,3072]{1,0:T(4,128)(2,1)S(1)} %slice.125), channel_id=1, source_target_pairs={{0,16},{2,18},{4,20},{6,22},{8,24},{10,26},{12,28},{14,30},{16,0},... | collective-permute-start | bytes 73736 | tf_op jit(solution)/shard_map/ppermute | solution.py:93
  145.4 7.7 %collective-permute-done.7 = bf16[4,3072]{1,0:T(4,128)(2,1)S(1)} collective-permute-done((bf16[4,3072]{1,0:T(4,128)(2,1)S(1)}, bf16[4,3072]{1,0:T(4,128)(2,1)S(1)}, u32[]{:S(2)}, u32[]{:S(2)}) %collective-permute-start.7) | collective-permute-done | bytes 24608 | tf_op jit(solution)/shard_map/ppermute | solution.py:93
  155.6 5.5 %all-to-all-done.1 = bf16[8,48,3072]{2,1,0:T(8,128)(2,1)S(1)} async-done(((bf16[8,48,3072]{2,1,0:T(8,128)(2,1)}), bf16[8,48,3072]{2,1,0:T(8,128)(2,1)S(1)}, u32[]{:S(2)}, u32[]{:S(2)}) %all-to-all-start.1) | async-done | bytes 2359328 | tf_op jit(solution)/shard_map/all_to_all | solution.py:102
  161.1 1.6 %fusion.97 = (bf16[4,48,3072]{2,1,0:T(8,128)(2,1)}, bf16[4,48,3072]{2,1,0:T(8,128)(2,1)}) fusion(bf16[8,48,3072]{2,1,0:T(8,128)(2,1)S(1)} %all-to-all-done.1), kind=kLoop, calls=%fused_computation.177 | loop fusion | bytes 4718592 | tf_op jit(solution)/shard_map/slice | solution.py:107
  (54 shorter events, 16.5 us)
Async XLA Ops:
  0.6 65.2 %copy-start = (bf16[3072,192]{0,1:T(8,128)(2,1)S(1)}, bf16[3072,192]{0,1:T(8,128)(2,1)}, u32[]{:S(2)}) copy-start(bf16[3072,192]{0,1:T(8,128)(2,1)} %param.7) | copy-start | bytes 3538948
  2.6 0.5 copy-start.3
  38.8 13.2 %collective-permute-start = (bf16[64,6144]{1,0:T(8,128)(2,1)S(1)}, bf16[64,6144]{1,0:T(8,128)(2,1)S(1)}, u32[]{:S(2)}, u32[]{:S(2)}) collective-permute-start(bf16[64,6144]{1,0:T(8,128)(2,1)S(1)} %reshape.42), channel_id=1, source_target_pairs={{0,32},{32,0},{1,33},{33,1},{2,34},{34,2},{3,35},{35,3},{4,36},{36... | collective-permute-start | bytes 2359304 | tf_op jit(solution)/shard_map/ppermute | solution.py:64
  52.1 13.6 %collective-permute-start.1 = (bf16[128,6144]{1,0:T(8,128)(2,1)S(1)}, bf16[128,6144]{1,0:T(8,128)(2,1)S(1)}, u32[]{:S(2)}, u32[]{:S(2)}) collective-permute-start(bf16[128,6144]{1,0:T(8,128)(2,1)S(1)} %pad_maximum_fusion.1), channel_id=1, source_target_pairs={{0,1},{1,0},{2,3},{3,2},{4,5},{5,4},{6,7},{7,6},{8,9},{9,8},{10,11... | collective-permute-start | bytes 4718600 | tf_op jit(solution)/shard_map/ppermute | solution.py:65
  65.8 1.3 copy-start.4
  69.1 1.3 copy-start.2
  70.4 11.5 %collective-permute-start.2 = (bf16[128,3072]{1,0:T(8,128)(2,1)}, bf16[128,3072]{1,0:T(8,128)(2,1)}, u32[]{:S(2)}, u32[]{:S(2)}) collective-permute-start(bf16[128,3072]{1,0:T(8,128)(2,1)} %convolution_convert_fusion.2), channel_id=1, source_target_pairs={{0,1},{1,0},{2,3},{3,2},{4,5},{5,4},{6,7},{7,6},{8,9},{9,8},{10,11... | collective-permute-start | bytes 2359304 | tf_op jit(solution)/shard_map/ppermute | solution.py:93
  75.2 41.2 %all-to-all-start = ((bf16[8,48,3072]{2,1,0:T(8,128)(2,1)}), bf16[8,48,3072]{2,1,0:T(8,128)(2,1)S(1)}, u32[]{:S(2)}, u32[]{:S(2)}) async-start(bf16[8,48,3072]{2,1,0:T(8,128)(2,1)} %bitcast.14), calls=%async_computation | async-start | bytes 4718592 | tf_op jit(solution)/shard_map/all_to_all | solution.py:89
  83.5 12.1 %collective-permute-start.3 = (bf16[64,3072]{1,0:T(8,128)(2,1)S(1)}, bf16[64,3072]{1,0:T(8,128)(2,1)S(1)}, u32[]{:S(2)}, u32[]{:S(2)}) collective-permute-start(bf16[64,3072]{1,0:T(8,128)(2,1)S(1)} %slice.121), channel_id=1, source_target_pairs={{0,2},{2,0},{4,6},{6,4},{8,10},{10,8},{12,14},{14,12},{16,18},{18,... | collective-permute-start | bytes 1179656 | tf_op jit(solution)/shard_map/ppermute | solution.py:93
  95.7 16.9 %collective-permute-start.4 = (bf16[32,3072]{1,0:T(8,128)(2,1)S(1)}, bf16[32,3072]{1,0:T(8,128)(2,1)S(1)}, u32[]{:S(2)}, u32[]{:S(2)}) collective-permute-start(bf16[32,3072]{1,0:T(8,128)(2,1)S(1)} %slice.122), channel_id=1, source_target_pairs={{0,32},{32,0},{1,33},{33,1},{2,34},{34,2},{3,35},{35,3},{4,36},{36... | collective-permute-start | bytes 589832 | tf_op jit(solution)/shard_map/ppermute | solution.py:93
  120.1 33.0 %copy-start.1 = (f32[3072]{0:T(1024)S(1)}, f32[3072]{0:T(1024)}, u32[]{:S(2)}) copy-start(f32[3072]{0:T(1024)} %param.6) | copy-start | bytes 36868
  120.1 8.4 %collective-permute-start.5 = (bf16[16,3072]{1,0:T(8,128)(2,1)}, bf16[16,3072]{1,0:T(8,128)(2,1)}, u32[]{:S(2)}, u32[]{:S(2)}) collective-permute-start(bf16[16,3072]{1,0:T(8,128)(2,1)} %slice.123), channel_id=1, source_target_pairs={{0,4},{2,6},{4,0},{6,2},{8,12},{10,14},{12,8},{14,10},{16,20},{18,... | collective-permute-start | bytes 294920 | tf_op jit(solution)/shard_map/ppermute | solution.py:93
  122.2 39.0 %all-to-all-start.1 = ((bf16[8,48,3072]{2,1,0:T(8,128)(2,1)}), bf16[8,48,3072]{2,1,0:T(8,128)(2,1)S(1)}, u32[]{:S(2)}, u32[]{:S(2)}) async-start(bf16[8,48,3072]{2,1,0:T(8,128)(2,1)} %broadcast_in_dim.2), calls=%async_computation.1 | async-start | bytes 4718592 | tf_op jit(solution)/shard_map/all_to_all | solution.py:102
  129.5 10.3 %collective-permute-start.6 = (bf16[8,3072]{1,0:T(8,128)(2,1)S(1)}, bf16[8,3072]{1,0:T(8,128)(2,1)S(1)}, u32[]{:S(2)}, u32[]{:S(2)}) collective-permute-start(bf16[8,3072]{1,0:T(8,128)(2,1)S(1)} %slice.124), channel_id=1, source_target_pairs={{0,8},{2,10},{4,12},{6,14},{8,0},{10,2},{12,4},{14,6},{16,24},{18,... | collective-permute-start | bytes 147464 | tf_op jit(solution)/shard_map/ppermute | solution.py:93
  139.8 13.3 %collective-permute-start.7 = (bf16[4,3072]{1,0:T(4,128)(2,1)S(1)}, bf16[4,3072]{1,0:T(4,128)(2,1)S(1)}, u32[]{:S(2)}, u32[]{:S(2)}) collective-permute-start(bf16[4,3072]{1,0:T(4,128)(2,1)S(1)} %slice.125), channel_id=1, source_target_pairs={{0,16},{2,18},{4,20},{6,22},{8,24},{10,26},{12,28},{14,30},{16,0},... | collective-permute-start | bytes 73736 | tf_op jit(solution)/shard_map/ppermute | solution.py:93

commit v4 on v3

--- a/solution.py
+++ b/solution.py
@@ -3,14 +3,15 @@
 import jax
 import jax.numpy as jnp
 from jax import lax
+from jax.experimental import pallas as pl
 from jax.sharding import Mesh, PartitionSpec as P
 
 AXES = ("x", "yh", "yl", "z", "core")
 DP = ("x", "yh")
 MP = ("yl", "z", "core")
+STAGES = (("core", 1, 1), ("z", 1, 1), ("yl", 1, 1), ("z", 2, 1), ("z", 4, 1), ("z", 8, 1))
 contract_last = (((1,), (1,)), ((), ()))
 contract_first = (((0,), (0,)), ((), ()))
-SWAP = [(0, 1), (1, 0)]
 
 
 def gelu_both(value):
@@ -23,20 +24,20 @@
     return gelu, derivative
 
 
-STAGES = (("core", 1), ("z", 1), ("yl", 1), ("z", 2), ("z", 4), ("z", 8))
+def swap(rows, axis, step, pieces):
+    pairs = [(at, at ^ step) for at in range(lax.axis_size(axis))]
+    size = rows.shape[0] // pieces
+    moved = [lax.ppermute(rows[k : k + size], axis, pairs) for k in range(0, rows.shape[0], size)]
+    return moved
 
 
-def partner(axis, step):
-    return [(at, at ^ step) for at in range(lax.axis_size(axis))]
-
-
-def stage_order(rows, n_z):
-    at = lax.broadcasted_iota(jnp.int32, (4 * n_z * rows, 4 * n_z * rows), 0)
+def stage_order(rows, n_z, zero):
+    at = lax.broadcasted_iota(jnp.int32, (4 * n_z * rows, 4 * n_z * rows), 0) + zero
     column = lax.broadcasted_iota(jnp.int32, at.shape, 1)
     old = at % rows
     far = jnp.zeros_like(at)
     block = at.shape[0]
-    for axis, step in STAGES:
+    for axis, step, _ in STAGES:
         block //= 2
         bit = (at // block) % 2
         if axis == "z":
@@ -47,22 +48,53 @@
     return (old == column).astype(jnp.bfloat16)
 
 
+def norm_kernel(inputs, gain, cotangent, joined, normal_out, inverse_out):
+    width = inputs.shape[1]
+    widened = inputs[...].astype(jnp.float32)
+    centred = widened - jnp.mean(widened, axis=1, keepdims=True)
+    variance = jnp.mean(centred * centred, axis=1, keepdims=True)
+    inverse = 1.0 / jnp.sqrt(variance + 1e-06)
+    normal = centred * inverse
+    joined[:, :width] = (normal * gain[...]).astype(jnp.bfloat16)
+    joined[:, width:] = cotangent[...]
+    normal_out[...] = normal
+    inverse_out[...] = jnp.broadcast_to(inverse, inverse_out.shape)
+
+
+def join_normed(inputs, gain, cotangent):
+    rows, width = inputs.shape
+    return pl.pallas_call(
+        norm_kernel,
+        out_shape=(
+            jax.ShapeDtypeStruct((rows, 2 * width), jnp.bfloat16),
+            jax.ShapeDtypeStruct((rows, width), jnp.float32),
+            jax.ShapeDtypeStruct((rows, 128), jnp.float32),
+        ),
+        name="norm",
+    )(inputs, gain[None, :], cotangent)
+
+
+def back_kernel(keep, away, normal, inverse, gain, cotangent, result):
+    normal = normal[...]
+    scaled = (keep[...] + away[...].astype(jnp.float32)) * gain[...]
+    first_mean = jnp.mean(scaled, axis=1, keepdims=True)
+    second_mean = jnp.mean(scaled * normal, axis=1, keepdims=True)
+    change = (scaled - first_mean - normal * second_mean) * inverse[:, :1]
+    result[...] = (cotangent[...].astype(jnp.float32) + change).astype(jnp.bfloat16)
+
+
 def body(inputs, gain, w_in, w_out, cotangent):
     rows, width = inputs.shape
     n_dp = lax.axis_size(DP)
     n_z = lax.axis_size("z")
-    widened = inputs.astype(jnp.float32)
-    row_mean = jnp.mean(widened, axis=1, keepdims=True)
-    centred = widened - row_mean
-    variance = jnp.mean(centred * centred, axis=1, keepdims=True)
-    inverse = 1.0 / jnp.sqrt(variance + 1e-06)
-    normal = centred * inverse
-    normed = (normal * gain[None, :]).astype(jnp.bfloat16)
+    joined, normal, inverse = join_normed(inputs, gain, cotangent)
 
-    both = jnp.concatenate([normed, cotangent], axis=1)
-    both = lax.all_gather(both, "z", axis=0, tiled=True)
-    both = jnp.concatenate([both, lax.ppermute(both, "yl", SWAP)], axis=0)
-    both = jnp.concatenate([both, lax.ppermute(both, "core", SWAP)], axis=0)
+    both = lax.all_gather(joined, "z", axis=0, tiled=True)
+    both, zero = lax.optimization_barrier((both, jnp.int32(0)))
+    order = stage_order(rows, n_z, zero)
+    both = jnp.concatenate([both, *swap(both, "yl", 1, 2)], axis=0)
+    both, order = lax.optimization_barrier((both, order))
+    both = jnp.concatenate([both, *swap(both, "core", 1, 1)], axis=0)
     normed_all, grad_all = both[:, :width], both[:, width:]
 
     hidden = jnp.dot(normed_all, w_in, preferred_element_type=jnp.float32)
@@ -70,7 +102,6 @@
     activated = gelu.astype(jnp.bfloat16)
     act_grad = lax.dot_general(grad_all, w_out, contract_last, preferred_element_type=jnp.float32)
     hidden_grad = (act_grad * derivative).astype(jnp.bfloat16)
-    order = stage_order(rows, n_z)
     ordered = jnp.dot(order, hidden_grad, preferred_element_type=jnp.float32).astype(jnp.bfloat16)
     half = ordered.shape[0] // 2
     send = lax.dot_general(
@@ -89,8 +120,10 @@
     parts = lax.all_to_all(parts, DP, 0, 0, tiled=True)
 
     keep = lax.dot_general(ordered[:half], w_in, contract_last, preferred_element_type=jnp.float32)
-    for k, (axis, step) in enumerate(STAGES):
-        away = lax.ppermute(send, axis, partner(axis, step))
+    for k, (axis, step, pieces) in enumerate(STAGES):
+        away = jnp.concatenate(swap(send, axis, step, pieces))
+        if k == len(STAGES) - 1:
+            break
         half = half // 2
         total = keep + away.astype(jnp.float32)
         if k == 2:
@@ -101,15 +134,16 @@
             spread, total = lax.optimization_barrier((spread, total))
             spread = lax.all_to_all(spread, DP, 0, 0, tiled=True)
         keep, send = total[:half], total[half:].astype(jnp.bfloat16)
-    normed_grad = total
     spread = spread.reshape(2, -1, width)
     grad_in = spread[0].T
     grad_out = spread[1]
-    scaled = normed_grad * gain[None, :]
-    first_mean = jnp.mean(scaled, axis=1, keepdims=True)
-    second_mean = jnp.mean(scaled * normal, axis=1, keepdims=True)
-    result = cotangent.astype(jnp.float32) + (scaled - first_mean - normal * second_mean) * inverse
-    return (result.astype(jnp.bfloat16), grad_in, grad_out)
+    input_grad = pl.pallas_call(
+        back_kernel,
+        out_shape=jax.ShapeDtypeStruct(inputs.shape, jnp.bfloat16),
+        cost_estimate=pl.CostEstimate(flops=0, bytes_accessed=0, transcendentals=0),
+        name="norm_back",
+    )(keep, away, normal, inverse, gain[None, :], cotangent)
+    return (input_grad, grad_in, grad_out)
 
 
 def solution(mesh):

time: 164 us -> 160 us (0.976)
  waiting for transfers between devices: 61.4 us -> 47.9 us
  starting transfers between devices: 43.5 us -> 48.3 us
  Pallas kernels: 0 us -> 3.32 us
    ppermute x8 -> x9, waiting for transfers between devices: 52.9 us -> 44.9 us  [swap(): lax.ppermute(rows[k:k + size], axis, pairs)]
    all_to_all x1, waiting for transfers between devices: 5.54 us -> 0.01 us  [body(): spread = lax.all_to_all(spread, DP, 0, 0, tiled=True)]
    ppermute x8 -> x9, starting transfers between devices: 32.1 us -> 36.9 us  [swap(): lax.ppermute(rows[k:k + size], axis, pairs)]
    pallas_call x0 -> x2, Pallas kernels: none -> 3.32 us  [the longest x1 1.74 us: join_normed(): pl.pallas_call(norm_kernel, out_shape=(jax.ShapeDtypeStruct((rows, 2 * wi...]
    reduce_sum x3 -> x0, other arithmetic: 2.9 us -> none  [the longest x1 0.98 us: body(): first_mean = jnp.mean(scaled, axis=1, keepdims=True)]
    and x4, other arithmetic: 0.03 us -> 1.77 us  [stage_order(): bit = at // block % 2]
  transfers between devices with their start and end apart: 10 -> 11, of which waited for: 9 -> 8; matrix products, arithmetic and copies ran while one was open for 5% -> 9% of each run, Pallas kernels for 0% -> 1%
where the time goes in v4:
time: 160 us; the launch traced here: 158 us
  starting transfers between devices  48.3 us (30%)
  waiting for transfers between devices  47.9 us (30%)
  blocking collectives  34.2 us (21%)
  other arithmetic  10.9 us (7%)
  local copies, waits for them, and re-layouts  6.66 us (4%)
  matrix products  5.43 us (3%)
  Pallas kernels  3.32 us (2%)
    ppermute x9, waiting for transfers between devices, swap(): lax.ppermute(rows[k:k + size], axis, pairs)  44.9 us
    ppermute x9, starting transfers between devices, swap(): lax.ppermute(rows[k:k + size], axis, pairs)  36.9 us
    all_gather x1, blocking collectives, body(): both = lax.all_gather(joined, 'z', axis=0, tiled=True)  34.2 us
    all_to_all x1, starting transfers between devices, body(): parts = lax.all_to_all(parts, DP, 0, 0, tiled=True)  6.63 us
    all_to_all x1, starting transfers between devices, body(): spread = lax.all_to_all(spread, DP, 0, 0, tiled=True)  4.77 us
  transfers between devices with their start and end apart: 11, of which 8 were waited for; matrix products, arithmetic and copies ran while one was open for 9% of the time, Pallas kernels for 1%

profile of v4, /device:TPU:1, one launch (start us, length us, event | category | flops | bytes accessed | tf_op | source)
XLA Modules:
  0.0 157.7 jit_solution(3805455919979561020)
XLA Ops:
  0.6 1.7 %norm.1 = (bf16[4,6144]{1,0:T(4,128)(2,1)}, f32[4,3072]{1,0:T(4,128)}, f32[4,128]{1,0:T(4,128)}) custom-call(bf16[4,3072]{1,0:T(4,128)(2,1)} %inputs.1, f32[1,3072]{1,0:T(1,128)} %bitcast.19, bf16[4,3072]{1,0:T(4,128)(2,1)} %cotangent.3), custom_call_target="tpu_custom_call" | custom-call | tf_op jit(solution)/shard_map/norm/pallas_call | solution.py:66
  2.4 34.2 %all-gather = bf16[16,4,6144]{2,1,0:T(4,128)(2,1)S(1)} all-gather(bf16[1,4,6144]{2,1,0:T(4,128)(2,1)} %bitcast.18), channel_id=1, replica_groups=mesh['x'=4,'yh'=2,'yl'=2,'z'=16,'core'=2] {'z'}, dimensions={0}, use_global_device_ids=true | all-gather | bytes 835584 | tf_op jit(solution)/shard_map/all_gather | solution.py:92
  36.8 3.2 %collective-permute-start = (bf16[32,6144]{1,0:T(8,128)(2,1)S(1)}, bf16[32,6144]{1,0:T(8,128)(2,1)S(1)}, u32[]{:S(2)}, u32[]{:S(2)}) collective-permute-start(bf16[32,6144]{1,0:T(8,128)(2,1)S(1)} %get-tuple-element.35), channel_id=1, source_target_pairs={{0,32},{32,0},{1,33},{33,1},{2,34},{34,2},{3,35},{35,3},{4,36},{36... | collective-permute-start | bytes 1179656 | tf_op jit(solution)/shard_map/ppermute | solution.py:30
  40.0 2.1 %collective-permute-start.1 = (bf16[32,6144]{1,0:T(8,128)(2,1)S(1)}, bf16[32,6144]{1,0:T(8,128)(2,1)S(1)}, u32[]{:S(2)}, u32[]{:S(2)}) collective-permute-start(bf16[32,6144]{1,0:T(8,128)(2,1)S(1)} %get-tuple-element.36), channel_id=1, source_target_pairs={{0,32},{32,0},{1,33},{33,1},{2,34},{34,2},{3,35},{35,3},{4,36},{36... | collective-permute-start | bytes 1179656 | tf_op jit(solution)/shard_map/ppermute | solution.py:30
  46.8 2.3 %fusion.32 = bf16[256,256]{1,0:T(8,128)(2,1)S(1)} fusion(s32[]{:T(128)S(6)} %axis_index.15, s32[256]{0:T(256)} %get-tuple-element.45, s32[256]{0:T(256)} %get-tuple-element.52, s32[256]{0:T(256)} %get-tuple-element.46, s32[256]{0:T(256)} %get-tuple-element.53, s32[256]{0:T(256)S(1)} %get-tuple-element.47, s32[256]{0:T(256)} %get-tuple-element.54, ...), kind=kLoop, calls=%fused_computation.73 | loop fusion | flops 5767168 | bytes 147204 | tf_op jit(solution)/shard_map/convert_element_type | solution.py:48
  50.1 10.6 %collective-permute-start.2 = (bf16[128,6144]{1,0:T(8,128)(2,1)S(1)}, bf16[128,6144]{1,0:T(8,128)(2,1)S(1)}, u32[]{:S(2)}, u32[]{:S(2)}) collective-permute-start(bf16[128,6144]{1,0:T(8,128)(2,1)S(1)} %pad_maximum_fusion.1), channel_id=1, source_target_pairs={{0,1},{1,0},{2,3},{3,2},{4,5},{5,4},{6,7},{7,6},{8,9},{9,8},{10,11... | collective-permute-start | bytes 4718600 | tf_op jit(solution)/shard_map/ppermute | solution.py:30
  60.8 2.9 %collective-permute-done.2 = bf16[128,6144]{1,0:T(8,128)(2,1)S(1)} collective-permute-done((bf16[128,6144]{1,0:T(8,128)(2,1)S(1)}, bf16[128,6144]{1,0:T(8,128)(2,1)S(1)}, u32[]{:S(2)}, u32[]{:S(2)}) %collective-permute-start.2) | collective-permute-done | bytes 1572896 | tf_op jit(solution)/shard_map/ppermute | solution.py:30
  67.3 2.3 %collective-permute-start.3 = (bf16[128,3072]{1,0:T(8,128)(2,1)}, bf16[128,3072]{1,0:T(8,128)(2,1)}, u32[]{:S(2)}, u32[]{:S(2)}) collective-permute-start(bf16[128,3072]{1,0:T(8,128)(2,1)} %convolution_convert_fusion.2), channel_id=1, source_target_pairs={{0,1},{1,0},{2,3},{3,2},{4,5},{5,4},{6,7},{7,6},{8,9},{9,8},{10,11... | collective-permute-start | bytes 2359304 | tf_op jit(solution)/shard_map/ppermute | solution.py:30
  70.6 1.6 %pad_maximum_fusion = bf16[384,3072]{1,0:T(8,128)(2,1)} fusion(bf16[192,3072]{1,0:T(8,128)(2,1)S(1)} %convolution_convert_fusion, bf16[192,3072]{1,0:T(8,128)(2,1)S(1)} %convolution_convert_fusion.1), kind=kLoop, calls=%fused_computation.4 | loop fusion | flops 4718592 | bytes 4718592 | tf_op jit(solution)/shard_map/concatenate | solution.py:118
  72.2 6.6 %all-to-all-start = ((bf16[8,48,3072]{2,1,0:T(8,128)(2,1)}), bf16[8,48,3072]{2,1,0:T(8,128)(2,1)S(1)}, u32[]{:S(2)}, u32[]{:S(2)}) async-start(bf16[8,48,3072]{2,1,0:T(8,128)(2,1)} %bitcast.15), calls=%async_computation | async-start | bytes 4718592 | tf_op jit(solution)/shard_map/all_to_all | solution.py:120
  80.5 1.9 %collective-permute-start.4 = (bf16[64,3072]{1,0:T(8,128)(2,1)S(1)}, bf16[64,3072]{1,0:T(8,128)(2,1)S(1)}, u32[]{:S(2)}, u32[]{:S(2)}) collective-permute-start(bf16[64,3072]{1,0:T(8,128)(2,1)S(1)} %slice.120), channel_id=1, source_target_pairs={{0,2},{2,0},{4,6},{6,4},{8,10},{10,8},{12,14},{14,12},{16,18},{18,... | collective-permute-start | bytes 1179656 | tf_op jit(solution)/shard_map/ppermute | solution.py:30
  82.4 10.2 %collective-permute-done.4 = bf16[64,3072]{1,0:T(8,128)(2,1)S(1)} collective-permute-done((bf16[64,3072]{1,0:T(8,128)(2,1)S(1)}, bf16[64,3072]{1,0:T(8,128)(2,1)S(1)}, u32[]{:S(2)}, u32[]{:S(2)}) %collective-permute-start.4) | collective-permute-done | bytes 393248 | tf_op jit(solution)/shard_map/ppermute | solution.py:30
  92.8 2.3 %collective-permute-start.5 = (bf16[32,3072]{1,0:T(8,128)(2,1)S(1)}, bf16[32,3072]{1,0:T(8,128)(2,1)S(1)}, u32[]{:S(2)}, u32[]{:S(2)}) collective-permute-start(bf16[32,3072]{1,0:T(8,128)(2,1)S(1)} %slice.121), channel_id=1, source_target_pairs={{0,32},{32,0},{1,33},{33,1},{2,34},{34,2},{3,35},{35,3},{4,36},{36... | collective-permute-start | bytes 589832 | tf_op jit(solution)/shard_map/ppermute | solution.py:30
  95.1 14.5 %collective-permute-done.5 = bf16[32,3072]{1,0:T(8,128)(2,1)S(1)} collective-permute-done((bf16[32,3072]{1,0:T(8,128)(2,1)S(1)}, bf16[32,3072]{1,0:T(8,128)(2,1)S(1)}, u32[]{:S(2)}, u32[]{:S(2)}) %collective-permute-start.5) | collective-permute-done | bytes 196640 | tf_op jit(solution)/shard_map/ppermute | solution.py:30
  110.4 3.0 %all-to-all-done = bf16[8,48,3072]{2,1,0:T(8,128)(2,1)S(1)} async-done(((bf16[8,48,3072]{2,1,0:T(8,128)(2,1)}), bf16[8,48,3072]{2,1,0:T(8,128)(2,1)S(1)}, u32[]{:S(2)}, u32[]{:S(2)}) %all-to-all-start) | async-done | bytes 2359328 | tf_op jit(solution)/shard_map/all_to_all | solution.py:120
  113.8 1.7 %broadcast_in_dim.5 = bf16[8,48,3072]{2,1,0:T(8,128)(2,1)} broadcast(bf16[48,3072]{1,0:T(8,128)(2,1)S(1)} %multiply_convert_fusion), dimensions={1,2} | broadcast | bytes 2654208 | tf_op jit(solution)/shard_map/broadcast_in_dim | solution.py:132
  115.5 4.8 %all-to-all-start.1 = ((bf16[8,48,3072]{2,1,0:T(8,128)(2,1)}), bf16[8,48,3072]{2,1,0:T(8,128)(2,1)S(1)}, u32[]{:S(2)}, u32[]{:S(2)}) async-start(bf16[8,48,3072]{2,1,0:T(8,128)(2,1)} %broadcast_in_dim.5), calls=%async_computation.1 | async-start | bytes 4718592 | tf_op jit(solution)/shard_map/all_to_all | solution.py:135
  121.3 1.9 %collective-permute-start.6 = (bf16[16,3072]{1,0:T(8,128)(2,1)S(1)}, bf16[16,3072]{1,0:T(8,128)(2,1)S(1)}, u32[]{:S(2)}, u32[]{:S(2)}) collective-permute-start(bf16[16,3072]{1,0:T(8,128)(2,1)S(1)} %slice.122), channel_id=1, source_target_pairs={{0,4},{2,6},{4,0},{6,2},{8,12},{10,14},{12,8},{14,10},{16,20},{18,... | collective-permute-start | bytes 294920 | tf_op jit(solution)/shard_map/ppermute | solution.py:30
  123.2 6.7 %collective-permute-done.6 = bf16[16,3072]{1,0:T(8,128)(2,1)S(1)} collective-permute-done((bf16[16,3072]{1,0:T(8,128)(2,1)S(1)}, bf16[16,3072]{1,0:T(8,128)(2,1)S(1)}, u32[]{:S(2)}, u32[]{:S(2)}) %collective-permute-start.6) | collective-permute-done | bytes 98336 | tf_op jit(solution)/shard_map/ppermute | solution.py:30
  130.8 3.7 %collective-permute-start.7 = (bf16[8,3072]{1,0:T(8,128)(2,1)S(1)}, bf16[8,3072]{1,0:T(8,128)(2,1)S(1)}, u32[]{:S(2)}, u32[]{:S(2)}) collective-permute-start(bf16[8,3072]{1,0:T(8,128)(2,1)S(1)} %slice.123), channel_id=1, source_target_pairs={{0,8},{2,10},{4,12},{6,14},{8,0},{10,2},{12,4},{14,6},{16,24},{18,... | collective-permute-start | bytes 147464 | tf_op jit(solution)/shard_map/ppermute | solution.py:30
  134.5 6.0 %collective-permute-done.7 = bf16[8,3072]{1,0:T(8,128)(2,1)S(1)} collective-permute-done((bf16[8,3072]{1,0:T(8,128)(2,1)S(1)}, bf16[8,3072]{1,0:T(8,128)(2,1)S(1)}, u32[]{:S(2)}, u32[]{:S(2)}) %collective-permute-start.7) | collective-permute-done | bytes 49184 | tf_op jit(solution)/shard_map/ppermute | solution.py:30
  140.5 8.9 %collective-permute-start.8 = (bf16[4,3072]{1,0:T(4,128)(2,1)S(1)}, bf16[4,3072]{1,0:T(4,128)(2,1)S(1)}, u32[]{:S(2)}, u32[]{:S(2)}) collective-permute-start(bf16[4,3072]{1,0:T(4,128)(2,1)S(1)} %slice.124), channel_id=1, source_target_pairs={{0,16},{2,18},{4,20},{6,22},{8,24},{10,26},{12,28},{14,30},{16,0},... | collective-permute-start | bytes 73736 | tf_op jit(solution)/shard_map/ppermute | solution.py:30
  150.1 3.7 %collective-permute-done.8.away = bf16[4,3072]{1,0:T(4,128)(2,1)S(1)} collective-permute-done((bf16[4,3072]{1,0:T(4,128)(2,1)S(1)}, bf16[4,3072]{1,0:T(4,128)(2,1)S(1)}, u32[]{:S(2)}, u32[]{:S(2)}) %collective-permute-start.8) | collective-permute-done | bytes 24608 | tf_op jit(solution)/shard_map/ppermute | solution.py:30
  156.0 1.6 %fusion.45 = (bf16[4,48,3072]{2,1,0:T(8,128)(2,1)}, bf16[4,48,3072]{2,1,0:T(8,128)(2,1)}) fusion(bf16[8,48,3072]{2,1,0:T(8,128)(2,1)S(1)} %all-to-all-done.1), kind=kLoop, calls=%fused_computation.121 | loop fusion | bytes 4718592 | tf_op jit(solution)/shard_map/slice | solution.py:139
  (48 shorter events, 18.2 us)
Async XLA Ops:
  0.6 63.2 %copy-start = (bf16[3072,192]{0,1:T(8,128)(2,1)S(1)}, bf16[3072,192]{0,1:T(8,128)(2,1)}, u32[]{:S(2)}) copy-start(bf16[3072,192]{0,1:T(8,128)(2,1)} %param.7) | copy-start | bytes 3538948
  36.8 12.4 %collective-permute-start = (bf16[32,6144]{1,0:T(8,128)(2,1)S(1)}, bf16[32,6144]{1,0:T(8,128)(2,1)S(1)}, u32[]{:S(2)}, u32[]{:S(2)}) collective-permute-start(bf16[32,6144]{1,0:T(8,128)(2,1)S(1)} %get-tuple-element.35), channel_id=1, source_target_pairs={{0,32},{32,0},{1,33},{33,1},{2,34},{34,2},{3,35},{35,3},{4,36},{36... | collective-permute-start | bytes 1179656 | tf_op jit(solution)/shard_map/ppermute | solution.py:30
  40.0 10.0 %collective-permute-start.1 = (bf16[32,6144]{1,0:T(8,128)(2,1)S(1)}, bf16[32,6144]{1,0:T(8,128)(2,1)S(1)}, u32[]{:S(2)}, u32[]{:S(2)}) collective-permute-start(bf16[32,6144]{1,0:T(8,128)(2,1)S(1)} %get-tuple-element.36), channel_id=1, source_target_pairs={{0,32},{32,0},{1,33},{33,1},{2,34},{34,2},{3,35},{35,3},{4,36},{36... | collective-permute-start | bytes 1179656 | tf_op jit(solution)/shard_map/ppermute | solution.py:30
  50.1 13.6 %collective-permute-start.2 = (bf16[128,6144]{1,0:T(8,128)(2,1)S(1)}, bf16[128,6144]{1,0:T(8,128)(2,1)S(1)}, u32[]{:S(2)}, u32[]{:S(2)}) collective-permute-start(bf16[128,6144]{1,0:T(8,128)(2,1)S(1)} %pad_maximum_fusion.1), channel_id=1, source_target_pairs={{0,1},{1,0},{2,3},{3,2},{4,5},{5,4},{6,7},{7,6},{8,9},{9,8},{10,11... | collective-permute-start | bytes 4718600 | tf_op jit(solution)/shard_map/ppermute | solution.py:30
  63.9 1.3 copy-start.3
  66.1 4.1 %copy-start.1 = (bf16[256,192]{0,1:T(8,128)(2,1)}, bf16[256,192]{0,1:T(8,128)(2,1)S(1)}, u32[]{:S(2)}) copy-start(bf16[256,192]{0,1:T(8,128)(2,1)S(1)} %convolution_convert_fusion.3) | copy-start | bytes 294916
  67.3 11.5 %collective-permute-start.3 = (bf16[128,3072]{1,0:T(8,128)(2,1)}, bf16[128,3072]{1,0:T(8,128)(2,1)}, u32[]{:S(2)}, u32[]{:S(2)}) collective-permute-start(bf16[128,3072]{1,0:T(8,128)(2,1)} %convolution_convert_fusion.2), channel_id=1, source_target_pairs={{0,1},{1,0},{2,3},{3,2},{4,5},{5,4},{6,7},{7,6},{8,9},{9,8},{10,11... | collective-permute-start | bytes 2359304 | tf_op jit(solution)/shard_map/ppermute | solution.py:30
  72.2 41.2 %all-to-all-start = ((bf16[8,48,3072]{2,1,0:T(8,128)(2,1)}), bf16[8,48,3072]{2,1,0:T(8,128)(2,1)S(1)}, u32[]{:S(2)}, u32[]{:S(2)}) async-start(bf16[8,48,3072]{2,1,0:T(8,128)(2,1)} %bitcast.15), calls=%async_computation | async-start | bytes 4718592 | tf_op jit(solution)/shard_map/all_to_all | solution.py:120
  80.5 12.2 %collective-permute-start.4 = (bf16[64,3072]{1,0:T(8,128)(2,1)S(1)}, bf16[64,3072]{1,0:T(8,128)(2,1)S(1)}, u32[]{:S(2)}, u32[]{:S(2)}) collective-permute-start(bf16[64,3072]{1,0:T(8,128)(2,1)S(1)} %slice.120), channel_id=1, source_target_pairs={{0,2},{2,0},{4,6},{6,4},{8,10},{10,8},{12,14},{14,12},{16,18},{18,... | collective-permute-start | bytes 1179656 | tf_op jit(solution)/shard_map/ppermute | solution.py:30
  92.8 16.9 %collective-permute-start.5 = (bf16[32,3072]{1,0:T(8,128)(2,1)S(1)}, bf16[32,3072]{1,0:T(8,128)(2,1)S(1)}, u32[]{:S(2)}, u32[]{:S(2)}) collective-permute-start(bf16[32,3072]{1,0:T(8,128)(2,1)S(1)} %slice.121), channel_id=1, source_target_pairs={{0,32},{32,0},{1,33},{33,1},{2,34},{34,2},{3,35},{35,3},{4,36},{36... | collective-permute-start | bytes 589832 | tf_op jit(solution)/shard_map/ppermute | solution.py:30
  115.5 40.5 %all-to-all-start.1 = ((bf16[8,48,3072]{2,1,0:T(8,128)(2,1)}), bf16[8,48,3072]{2,1,0:T(8,128)(2,1)S(1)}, u32[]{:S(2)}, u32[]{:S(2)}) async-start(bf16[8,48,3072]{2,1,0:T(8,128)(2,1)} %broadcast_in_dim.5), calls=%async_computation.1 | async-start | bytes 4718592 | tf_op jit(solution)/shard_map/all_to_all | solution.py:135
  121.3 8.6 %collective-permute-start.6 = (bf16[16,3072]{1,0:T(8,128)(2,1)S(1)}, bf16[16,3072]{1,0:T(8,128)(2,1)S(1)}, u32[]{:S(2)}, u32[]{:S(2)}) collective-permute-start(bf16[16,3072]{1,0:T(8,128)(2,1)S(1)} %slice.122), channel_id=1, source_target_pairs={{0,4},{2,6},{4,0},{6,2},{8,12},{10,14},{12,8},{14,10},{16,20},{18,... | collective-permute-start | bytes 294920 | tf_op jit(solution)/shard_map/ppermute | solution.py:30
  130.8 9.7 %collective-permute-start.7 = (bf16[8,3072]{1,0:T(8,128)(2,1)S(1)}, bf16[8,3072]{1,0:T(8,128)(2,1)S(1)}, u32[]{:S(2)}, u32[]{:S(2)}) collective-permute-start(bf16[8,3072]{1,0:T(8,128)(2,1)S(1)} %slice.123), channel_id=1, source_target_pairs={{0,8},{2,10},{4,12},{6,14},{8,0},{10,2},{12,4},{14,6},{16,24},{18,... | collective-permute-start | bytes 147464 | tf_op jit(solution)/shard_map/ppermute | solution.py:30
  140.5 13.3 %collective-permute-start.8 = (bf16[4,3072]{1,0:T(4,128)(2,1)S(1)}, bf16[4,3072]{1,0:T(4,128)(2,1)S(1)}, u32[]{:S(2)}, u32[]{:S(2)}) collective-permute-start(bf16[4,3072]{1,0:T(4,128)(2,1)S(1)} %slice.124), channel_id=1, source_target_pairs={{0,16},{2,18},{4,20},{6,22},{8,24},{10,26},{12,28},{14,30},{16,0},... | collective-permute-start | bytes 73736 | tf_op jit(solution)/shard_map/ppermute | solution.py:30
  153.8 0.6 copy-start.2

commit v5 on v4

--- a/solution.py
+++ b/solution.py
@@ -9,7 +9,7 @@
 AXES = ("x", "yh", "yl", "z", "core")
 DP = ("x", "yh")
 MP = ("yl", "z", "core")
-STAGES = (("core", 1, 1), ("z", 1, 1), ("yl", 1, 1), ("z", 2, 1), ("z", 4, 1), ("z", 8, 1))
+STAGES = (("core", (1,)), ("z", (1, 2,)), ("yl", (1,)), ("z", (4, 8,)))
 contract_last = (((1,), (1,)), ((), ()))
 contract_first = (((0,), (0,)), ((), ()))
 
@@ -24,11 +24,8 @@
     return gelu, derivative
 
 
-def swap(rows, axis, step, pieces):
-    pairs = [(at, at ^ step) for at in range(lax.axis_size(axis))]
-    size = rows.shape[0] // pieces
-    moved = [lax.ppermute(rows[k : k + size], axis, pairs) for k in range(0, rows.shape[0], size)]
-    return moved
+def swap(rows, axis, step):
+    return lax.ppermute(rows, axis, [(at, at ^ step) for at in range(lax.axis_size(axis))])
 
 
 def stage_order(rows, n_z, zero):
@@ -37,13 +34,14 @@
     old = at % rows
     far = jnp.zeros_like(at)
     block = at.shape[0]
-    for axis, step, _ in STAGES:
-        block //= 2
-        bit = (at // block) % 2
-        if axis == "z":
-            far = far + bit * step
-        else:
-            old = old + bit * (n_z * rows * (2 if axis == "core" else 1))
+    for axis, bits in STAGES:
+        for step in reversed(bits):
+            block //= 2
+            bit = (at // block) % 2
+            if axis == "z":
+                far = far + bit * step
+            else:
+                old = old + bit * (n_z * rows * (2 if axis == "core" else 1))
     old = old + (far ^ lax.axis_index("z")) * rows
     return (old == column).astype(jnp.bfloat16)
 
@@ -74,9 +72,13 @@
     )(inputs, gain[None, :], cotangent)
 
 
-def back_kernel(keep, away, normal, inverse, gain, cotangent, result):
+def back_kernel(keep, normal, inverse, gain, cotangent, *rest):
+    *aways, result = rest
     normal = normal[...]
-    scaled = (keep[...] + away[...].astype(jnp.float32)) * gain[...]
+    terms = keep[...]
+    for away in aways:
+        terms = terms + away[...].astype(jnp.float32)
+    scaled = terms * gain[...]
     first_mean = jnp.mean(scaled, axis=1, keepdims=True)
     second_mean = jnp.mean(scaled * normal, axis=1, keepdims=True)
     change = (scaled - first_mean - normal * second_mean) * inverse[:, :1]
@@ -92,9 +94,9 @@
     both = lax.all_gather(joined, "z", axis=0, tiled=True)
     both, zero = lax.optimization_barrier((both, jnp.int32(0)))
     order = stage_order(rows, n_z, zero)
-    both = jnp.concatenate([both, *swap(both, "yl", 1, 2)], axis=0)
+    both = jnp.concatenate([both, swap(both, "yl", 1)], axis=0)
     both, order = lax.optimization_barrier((both, order))
-    both = jnp.concatenate([both, *swap(both, "core", 1, 1)], axis=0)
+    both = jnp.concatenate([both, swap(both, "core", 1)], axis=0)
     normed_all, grad_all = both[:, :width], both[:, width:]
 
     hidden = jnp.dot(normed_all, w_in, preferred_element_type=jnp.float32)
@@ -120,12 +122,13 @@
     parts = lax.all_to_all(parts, DP, 0, 0, tiled=True)
 
     keep = lax.dot_general(ordered[:half], w_in, contract_last, preferred_element_type=jnp.float32)
-    for k, (axis, step, pieces) in enumerate(STAGES):
-        away = jnp.concatenate(swap(send, axis, step, pieces))
+    sends = [send]
+    for k, (axis, bits) in enumerate(STAGES):
+        steps = (*bits, sum(bits))[: len(sends)]
+        aways = [swap(send, axis, step) for send, step in zip(sends, steps)]
         if k == len(STAGES) - 1:
             break
-        half = half // 2
-        total = keep + away.astype(jnp.float32)
+        total = keep + sum(away.astype(jnp.float32) for away in aways)
         if k == 2:
             parts, _ = lax.optimization_barrier((parts, total))
             mine = (jnp.sum(parts.astype(jnp.float32), axis=0) / n_dp).astype(jnp.bfloat16)
@@ -133,7 +136,9 @@
         if k == 2:
             spread, total = lax.optimization_barrier((spread, total))
             spread = lax.all_to_all(spread, DP, 0, 0, tiled=True)
-        keep, send = total[:half], total[half:].astype(jnp.bfloat16)
+        size = total.shape[0] // 2 ** len(STAGES[k + 1][1])
+        keep = total[:size]
+        sends = [total[q : q + size].astype(jnp.bfloat16) for q in range(size, total.shape[0], size)]
     spread = spread.reshape(2, -1, width)
     grad_in = spread[0].T
     grad_out = spread[1]
@@ -142,7 +147,7 @@
         out_shape=jax.ShapeDtypeStruct(inputs.shape, jnp.bfloat16),
         cost_estimate=pl.CostEstimate(flops=0, bytes_accessed=0, transcendentals=0),
         name="norm_back",
-    )(keep, away, normal, inverse, gain[None, :], cotangent)
+    )(keep, normal, inverse, gain[None, :], cotangent, *aways)
     return (input_grad, grad_in, grad_out)
 
 

time: 160 us -> 155 us (0.969)
  other arithmetic: 10.9 us -> 5.17 us
  starting transfers between devices: 48.3 us -> 53.6 us
  waiting for transfers between devices: 47.9 us -> 44.8 us
    ppermute x9 -> x10, waiting for transfers between devices: 44.9 us -> 32.3 us  [swap(): lax.ppermute(rows, axis, [(at, at ^ step) for at in range(lax.axis_size(a...]
    all_to_all x1, waiting for transfers between devices: 0.01 us -> 9.56 us  [body(): spread = lax.all_to_all(spread, DP, 0, 0, tiled=True)]
    ppermute x9 -> x10, starting transfers between devices: 36.9 us -> 42.9 us  [swap(): lax.ppermute(rows, axis, [(at, at ^ step) for at in range(lax.axis_size(a...]
    and x4, other arithmetic: 1.77 us -> 0.05 us  [stage_order(): bit = at // block % 2]
  transfers between devices with their start and end apart: 11 -> 12, of which waited for: 8 -> 9; matrix products, arithmetic and copies ran while one was open for 9% -> 6% of each run, Pallas kernels for 1% -> 1%
where the time goes in v5:
time: 155 us; the launch traced here: 154 us
  starting transfers between devices  53.6 us (35%)
  waiting for transfers between devices  44.8 us (29%)
  blocking collectives  34.2 us (22%)
  local copies, waits for them, and re-layouts  6.58 us (4%)
  matrix products  5.43 us (4%)
  other arithmetic  5.17 us (3%)
  Pallas kernels  3.34 us (2%)
    ppermute x10, starting transfers between devices, swap(): lax.ppermute(rows, axis, [(at, at ^ step) for at in range(lax.axis_size(a...  42.9 us
    all_gather x1, blocking collectives, body(): both = lax.all_gather(joined, 'z', axis=0, tiled=True)  34.2 us
    ppermute x10, waiting for transfers between devices, swap(): lax.ppermute(rows, axis, [(at, at ^ step) for at in range(lax.axis_size(a...  32.3 us
    all_to_all x1, waiting for transfers between devices, body(): spread = lax.all_to_all(spread, DP, 0, 0, tiled=True)  9.56 us
    all_to_all x1, starting transfers between devices, body(): parts = lax.all_to_all(parts, DP, 0, 0, tiled=True)  6.71 us
    all_to_all x1, starting transfers between devices, body(): spread = lax.all_to_all(spread, DP, 0, 0, tiled=True)  4.01 us
  transfers between devices with their start and end apart: 12, of which 9 were waited for; matrix products, arithmetic and copies ran while one was open for 6% of the time, Pallas kernels for 1%

profile of v5, /device:TPU:1, one launch (start us, length us, event | category | flops | bytes accessed | tf_op | source)
XLA Modules:
  0.0 154.0 jit_solution(6118697177186911790)
XLA Ops:
  0.6 1.7 %norm.1 = (bf16[4,6144]{1,0:T(4,128)(2,1)}, f32[4,3072]{1,0:T(4,128)}, f32[4,128]{1,0:T(4,128)}) custom-call(bf16[4,3072]{1,0:T(4,128)(2,1)} %inputs.1, f32[1,3072]{1,0:T(1,128)} %bitcast.18, bf16[4,3072]{1,0:T(4,128)(2,1)} %cotangent.3), custom_call_target="tpu_custom_call" | custom-call | tf_op jit(solution)/shard_map/norm/pallas_call | solution.py:64
  2.4 34.2 %all-gather = bf16[16,4,6144]{2,1,0:T(4,128)(2,1)S(1)} all-gather(bf16[1,4,6144]{2,1,0:T(4,128)(2,1)} %bitcast.20), channel_id=1, replica_groups=mesh['x'=4,'yh'=2,'yl'=2,'z'=16,'core'=2] {'z'}, dimensions={0}, use_global_device_ids=true | all-gather | bytes 835584 | tf_op jit(solution)/shard_map/all_gather | solution.py:94
  36.7 3.2 %collective-permute-start = (bf16[64,6144]{1,0:T(8,128)(2,1)S(1)}, bf16[64,6144]{1,0:T(8,128)(2,1)S(1)}, u32[]{:S(2)}, u32[]{:S(2)}) collective-permute-start(bf16[64,6144]{1,0:T(8,128)(2,1)S(1)} %reshape.20), channel_id=1, source_target_pairs={{0,32},{32,0},{1,33},{33,1},{2,34},{34,2},{3,35},{35,3},{4,36},{36... | collective-permute-start | bytes 2359304 | tf_op jit(solution)/shard_map/ppermute | solution.py:28
  41.4 8.5 %collective-permute-done = bf16[64,6144]{1,0:T(8,128)(2,1)S(1)} collective-permute-done((bf16[64,6144]{1,0:T(8,128)(2,1)S(1)}, bf16[64,6144]{1,0:T(8,128)(2,1)S(1)}, u32[]{:S(2)}, u32[]{:S(2)}) %collective-permute-start) | collective-permute-done | bytes 786464 | tf_op jit(solution)/shard_map/ppermute | solution.py:28
  50.0 10.6 %collective-permute-start.1 = (bf16[128,6144]{1,0:T(8,128)(2,1)S(1)}, bf16[128,6144]{1,0:T(8,128)(2,1)S(1)}, u32[]{:S(2)}, u32[]{:S(2)}) collective-permute-start(bf16[128,6144]{1,0:T(8,128)(2,1)S(1)} %pad_maximum_fusion.1), channel_id=1, source_target_pairs={{0,1},{1,0},{2,3},{3,2},{4,5},{5,4},{6,7},{7,6},{8,9},{9,8},{10,11... | collective-permute-start | bytes 4718600 | tf_op jit(solution)/shard_map/ppermute | solution.py:28
  60.8 2.9 %collective-permute-done.1 = bf16[128,6144]{1,0:T(8,128)(2,1)S(1)} collective-permute-done((bf16[128,6144]{1,0:T(8,128)(2,1)S(1)}, bf16[128,6144]{1,0:T(8,128)(2,1)S(1)}, u32[]{:S(2)}, u32[]{:S(2)}) %collective-permute-start.1) | collective-permute-done | bytes 1572896 | tf_op jit(solution)/shard_map/ppermute | solution.py:28
  67.3 2.3 %collective-permute-start.2 = (bf16[128,3072]{1,0:T(8,128)(2,1)}, bf16[128,3072]{1,0:T(8,128)(2,1)}, u32[]{:S(2)}, u32[]{:S(2)}) collective-permute-start(bf16[128,3072]{1,0:T(8,128)(2,1)} %convolution_convert_fusion.2), channel_id=1, source_target_pairs={{0,1},{1,0},{2,3},{3,2},{4,5},{5,4},{6,7},{7,6},{8,9},{9,8},{10,11... | collective-permute-start | bytes 2359304 | tf_op jit(solution)/shard_map/ppermute | solution.py:28
  72.1 6.7 %all-to-all-start = ((bf16[8,48,3072]{2,1,0:T(8,128)(2,1)}), bf16[8,48,3072]{2,1,0:T(8,128)(2,1)S(1)}, u32[]{:S(2)}, u32[]{:S(2)}) async-start(bf16[8,48,3072]{2,1,0:T(8,128)(2,1)} %bitcast.15), calls=%async_computation | async-start | bytes 4718592 | tf_op jit(solution)/shard_map/all_to_all | solution.py:122
  80.4 1.9 %collective-permute-start.3 = (bf16[32,3072]{1,0:T(8,128)(2,1)S(1)}, bf16[32,3072]{1,0:T(8,128)(2,1)S(1)}, u32[]{:S(2)}, u32[]{:S(2)}) collective-permute-start(bf16[32,3072]{1,0:T(8,128)(2,1)S(1)} %get-tuple-element.35), channel_id=1, source_target_pairs={{0,2},{2,0},{4,6},{6,4},{8,10},{10,8},{12,14},{14,12},{16,18},{18,... | collective-permute-start | bytes 589832 | tf_op jit(solution)/shard_map/ppermute | solution.py:28
  82.4 3.0 %collective-permute-start.5 = (bf16[32,3072]{1,0:T(8,128)(2,1)S(1)}, bf16[32,3072]{1,0:T(8,128)(2,1)S(1)}, u32[]{:S(2)}, u32[]{:S(2)}) collective-permute-start(bf16[32,3072]{1,0:T(8,128)(2,1)S(1)} %get-tuple-element.36), channel_id=1, source_target_pairs={{0,6},{2,4},{4,2},{6,0},{8,14},{10,12},{12,10},{14,8},{16,22},{18,... | collective-permute-start | bytes 589832 | tf_op jit(solution)/shard_map/ppermute | solution.py:28
  85.4 3.5 %collective-permute-start.4 = (bf16[32,3072]{1,0:T(8,128)(2,1)S(1)}, bf16[32,3072]{1,0:T(8,128)(2,1)S(1)}, u32[]{:S(2)}, u32[]{:S(2)}) collective-permute-start(bf16[32,3072]{1,0:T(8,128)(2,1)S(1)} %get-tuple-element.37), channel_id=1, source_target_pairs={{0,4},{2,6},{4,0},{6,2},{8,12},{10,14},{12,8},{14,10},{16,20},{18,... | collective-permute-start | bytes 589832 | tf_op jit(solution)/shard_map/ppermute | solution.py:28
  88.8 3.6 %collective-permute-done.5 = bf16[32,3072]{1,0:T(8,128)(2,1)S(1)} collective-permute-done((bf16[32,3072]{1,0:T(8,128)(2,1)S(1)}, bf16[32,3072]{1,0:T(8,128)(2,1)S(1)}, u32[]{:S(2)}, u32[]{:S(2)}) %collective-permute-start.5) | collective-permute-done | bytes 196640 | tf_op jit(solution)/shard_map/ppermute | solution.py:28
  92.5 11.7 %collective-permute-done.4 = bf16[32,3072]{1,0:T(8,128)(2,1)S(1)} collective-permute-done((bf16[32,3072]{1,0:T(8,128)(2,1)S(1)}, bf16[32,3072]{1,0:T(8,128)(2,1)S(1)}, u32[]{:S(2)}, u32[]{:S(2)}) %collective-permute-start.4) | collective-permute-done | bytes 196640 | tf_op jit(solution)/shard_map/ppermute | solution.py:28
  104.3 2.2 %collective-permute-start.6 = (bf16[16,3072]{1,0:T(8,128)(2,1)S(1)}, bf16[16,3072]{1,0:T(8,128)(2,1)S(1)}, u32[]{:S(2)}, u32[]{:S(2)}) collective-permute-start(bf16[16,3072]{1,0:T(8,128)(2,1)S(1)} %slice.108), channel_id=1, source_target_pairs={{0,32},{32,0},{1,33},{33,1},{2,34},{34,2},{3,35},{35,3},{4,36},{36... | collective-permute-start | bytes 294920 | tf_op jit(solution)/shard_map/ppermute | solution.py:28
  106.5 3.4 %collective-permute-done.6 = bf16[16,3072]{1,0:T(8,128)(2,1)S(1)} collective-permute-done((bf16[16,3072]{1,0:T(8,128)(2,1)S(1)}, bf16[16,3072]{1,0:T(8,128)(2,1)S(1)}, u32[]{:S(2)}, u32[]{:S(2)}) %collective-permute-start.6) | collective-permute-done | bytes 98336 | tf_op jit(solution)/shard_map/ppermute | solution.py:28
  110.6 2.9 %all-to-all-done = bf16[8,48,3072]{2,1,0:T(8,128)(2,1)S(1)} async-done(((bf16[8,48,3072]{2,1,0:T(8,128)(2,1)}), bf16[8,48,3072]{2,1,0:T(8,128)(2,1)S(1)}, u32[]{:S(2)}, u32[]{:S(2)}) %all-to-all-start) | async-done | bytes 2359328 | tf_op jit(solution)/shard_map/all_to_all | solution.py:122
  113.9 1.7 %broadcast_in_dim.5 = bf16[8,48,3072]{2,1,0:T(8,128)(2,1)} broadcast(bf16[48,3072]{1,0:T(8,128)(2,1)S(1)} %multiply_convert_fusion), dimensions={1,2} | broadcast | bytes 2654208 | tf_op jit(solution)/shard_map/broadcast_in_dim | solution.py:135
  115.6 4.0 %all-to-all-start.1 = ((bf16[8,48,3072]{2,1,0:T(8,128)(2,1)}), bf16[8,48,3072]{2,1,0:T(8,128)(2,1)S(1)}, u32[]{:S(2)}, u32[]{:S(2)}) async-start(bf16[8,48,3072]{2,1,0:T(8,128)(2,1)} %broadcast_in_dim.5), calls=%async_computation.1 | async-start | bytes 4718592 | tf_op jit(solution)/shard_map/all_to_all | solution.py:138
  120.6 4.8 %collective-permute-start.9 = (bf16[4,3072]{1,0:T(4,128)(2,1)S(1)}, bf16[4,3072]{1,0:T(4,128)(2,1)}, u32[]{:S(2)}, u32[]{:S(2)}) collective-permute-start(bf16[4,3072]{1,0:T(4,128)(2,1)S(1)} %get-tuple-element.38), channel_id=1, source_target_pairs={{0,24},{2,26},{4,28},{6,30},{8,16},{10,18},{12,20},{14,22},{16,8},... | collective-permute-start | bytes 73736 | tf_op jit(solution)/shard_map/ppermute | solution.py:28
  125.4 5.1 %collective-permute-start.8 = (bf16[4,3072]{1,0:T(4,128)(2,1)S(1)}, bf16[4,3072]{1,0:T(4,128)(2,1)S(1)}, u32[]{:S(2)}, u32[]{:S(2)}) collective-permute-start(bf16[4,3072]{1,0:T(4,128)(2,1)S(1)} %get-tuple-element.39), channel_id=1, source_target_pairs={{0,16},{2,18},{4,20},{6,22},{8,24},{10,26},{12,28},{14,30},{16,0},... | collective-permute-start | bytes 73736 | tf_op jit(solution)/shard_map/ppermute | solution.py:28
  130.5 6.3 %collective-permute-start.7 = (bf16[4,3072]{1,0:T(4,128)(2,1)S(1)}, bf16[4,3072]{1,0:T(4,128)(2,1)S(1)}, u32[]{:S(2)}, u32[]{:S(2)}) collective-permute-start(bf16[4,3072]{1,0:T(4,128)(2,1)S(1)} %get-tuple-element.40), channel_id=1, source_target_pairs={{0,8},{2,10},{4,12},{6,14},{8,0},{10,2},{12,4},{14,6},{16,24},{18,... | collective-permute-start | bytes 73736 | tf_op jit(solution)/shard_map/ppermute | solution.py:28
  138.8 1.7 %collective-permute-done.7.rest_0_ = bf16[4,3072]{1,0:T(4,128)(2,1)S(1)} collective-permute-done((bf16[4,3072]{1,0:T(4,128)(2,1)S(1)}, bf16[4,3072]{1,0:T(4,128)(2,1)S(1)}, u32[]{:S(2)}, u32[]{:S(2)}) %collective-permute-start.7) | collective-permute-done | bytes 24608 | tf_op jit(solution)/shard_map/ppermute | solution.py:28
  142.8 9.6 %all-to-all-done.1 = bf16[8,48,3072]{2,1,0:T(8,128)(2,1)S(1)} async-done(((bf16[8,48,3072]{2,1,0:T(8,128)(2,1)}), bf16[8,48,3072]{2,1,0:T(8,128)(2,1)S(1)}, u32[]{:S(2)}, u32[]{:S(2)}) %all-to-all-start.1) | async-done | bytes 2359328 | tf_op jit(solution)/shard_map/all_to_all | solution.py:138
  152.3 1.6 %fusion.45 = (bf16[4,48,3072]{2,1,0:T(8,128)(2,1)}, bf16[4,48,3072]{2,1,0:T(8,128)(2,1)}) fusion(bf16[8,48,3072]{2,1,0:T(8,128)(2,1)S(1)} %all-to-all-done.1), kind=kLoop, calls=%fused_computation.115 | loop fusion | bytes 4718592 | tf_op jit(solution)/shard_map/slice | solution.py:144
  (48 shorter events, 16.0 us)
Async XLA Ops:
  0.6 63.2 %copy-start = (bf16[3072,192]{0,1:T(8,128)(2,1)S(1)}, bf16[3072,192]{0,1:T(8,128)(2,1)}, u32[]{:S(2)}) copy-start(bf16[3072,192]{0,1:T(8,128)(2,1)} %param.7) | copy-start | bytes 3538948
  36.7 13.2 %collective-permute-start = (bf16[64,6144]{1,0:T(8,128)(2,1)S(1)}, bf16[64,6144]{1,0:T(8,128)(2,1)S(1)}, u32[]{:S(2)}, u32[]{:S(2)}) collective-permute-start(bf16[64,6144]{1,0:T(8,128)(2,1)S(1)} %reshape.20), channel_id=1, source_target_pairs={{0,32},{32,0},{1,33},{33,1},{2,34},{34,2},{3,35},{35,3},{4,36},{36... | collective-permute-start | bytes 2359304 | tf_op jit(solution)/shard_map/ppermute | solution.py:28
  50.0 13.6 %collective-permute-start.1 = (bf16[128,6144]{1,0:T(8,128)(2,1)S(1)}, bf16[128,6144]{1,0:T(8,128)(2,1)S(1)}, u32[]{:S(2)}, u32[]{:S(2)}) collective-permute-start(bf16[128,6144]{1,0:T(8,128)(2,1)S(1)} %pad_maximum_fusion.1), channel_id=1, source_target_pairs={{0,1},{1,0},{2,3},{3,2},{4,5},{5,4},{6,7},{7,6},{8,9},{9,8},{10,11... | collective-permute-start | bytes 4718600 | tf_op jit(solution)/shard_map/ppermute | solution.py:28
  63.8 1.3 copy-start.4
  66.0 1.3 copy-start.1
  67.3 11.5 %collective-permute-start.2 = (bf16[128,3072]{1,0:T(8,128)(2,1)}, bf16[128,3072]{1,0:T(8,128)(2,1)}, u32[]{:S(2)}, u32[]{:S(2)}) collective-permute-start(bf16[128,3072]{1,0:T(8,128)(2,1)} %convolution_convert_fusion.2), channel_id=1, source_target_pairs={{0,1},{1,0},{2,3},{3,2},{4,5},{5,4},{6,7},{7,6},{8,9},{9,8},{10,11... | collective-permute-start | bytes 2359304 | tf_op jit(solution)/shard_map/ppermute | solution.py:28
  72.1 41.4 %all-to-all-start = ((bf16[8,48,3072]{2,1,0:T(8,128)(2,1)}), bf16[8,48,3072]{2,1,0:T(8,128)(2,1)S(1)}, u32[]{:S(2)}, u32[]{:S(2)}) async-start(bf16[8,48,3072]{2,1,0:T(8,128)(2,1)} %bitcast.15), calls=%async_computation | async-start | bytes 4718592 | tf_op jit(solution)/shard_map/all_to_all | solution.py:122
  80.4 8.4 %collective-permute-start.3 = (bf16[32,3072]{1,0:T(8,128)(2,1)S(1)}, bf16[32,3072]{1,0:T(8,128)(2,1)S(1)}, u32[]{:S(2)}, u32[]{:S(2)}) collective-permute-start(bf16[32,3072]{1,0:T(8,128)(2,1)S(1)} %get-tuple-element.35), channel_id=1, source_target_pairs={{0,2},{2,0},{4,6},{6,4},{8,10},{10,8},{12,14},{14,12},{16,18},{18,... | collective-permute-start | bytes 589832 | tf_op jit(solution)/shard_map/ppermute | solution.py:28
  82.4 10.1 %collective-permute-start.5 = (bf16[32,3072]{1,0:T(8,128)(2,1)S(1)}, bf16[32,3072]{1,0:T(8,128)(2,1)S(1)}, u32[]{:S(2)}, u32[]{:S(2)}) collective-permute-start(bf16[32,3072]{1,0:T(8,128)(2,1)S(1)} %get-tuple-element.36), channel_id=1, source_target_pairs={{0,6},{2,4},{4,2},{6,0},{8,14},{10,12},{12,10},{14,8},{16,22},{18,... | collective-permute-start | bytes 589832 | tf_op jit(solution)/shard_map/ppermute | solution.py:28
  85.4 18.8 %collective-permute-start.4 = (bf16[32,3072]{1,0:T(8,128)(2,1)S(1)}, bf16[32,3072]{1,0:T(8,128)(2,1)S(1)}, u32[]{:S(2)}, u32[]{:S(2)}) collective-permute-start(bf16[32,3072]{1,0:T(8,128)(2,1)S(1)} %get-tuple-element.37), channel_id=1, source_target_pairs={{0,4},{2,6},{4,0},{6,2},{8,12},{10,14},{12,8},{14,10},{16,20},{18,... | collective-permute-start | bytes 589832 | tf_op jit(solution)/shard_map/ppermute | solution.py:28
  104.3 5.7 %collective-permute-start.6 = (bf16[16,3072]{1,0:T(8,128)(2,1)S(1)}, bf16[16,3072]{1,0:T(8,128)(2,1)S(1)}, u32[]{:S(2)}, u32[]{:S(2)}) collective-permute-start(bf16[16,3072]{1,0:T(8,128)(2,1)S(1)} %slice.108), channel_id=1, source_target_pairs={{0,32},{32,0},{1,33},{33,1},{2,34},{34,2},{3,35},{35,3},{4,36},{36... | collective-permute-start | bytes 294920 | tf_op jit(solution)/shard_map/ppermute | solution.py:28
  115.6 36.8 %all-to-all-start.1 = ((bf16[8,48,3072]{2,1,0:T(8,128)(2,1)}), bf16[8,48,3072]{2,1,0:T(8,128)(2,1)S(1)}, u32[]{:S(2)}, u32[]{:S(2)}) async-start(bf16[8,48,3072]{2,1,0:T(8,128)(2,1)} %broadcast_in_dim.5), calls=%async_computation.1 | async-start | bytes 4718592 | tf_op jit(solution)/shard_map/all_to_all | solution.py:138
  120.6 17.7 %collective-permute-start.9 = (bf16[4,3072]{1,0:T(4,128)(2,1)S(1)}, bf16[4,3072]{1,0:T(4,128)(2,1)}, u32[]{:S(2)}, u32[]{:S(2)}) collective-permute-start(bf16[4,3072]{1,0:T(4,128)(2,1)S(1)} %get-tuple-element.38), channel_id=1, source_target_pairs={{0,24},{2,26},{4,28},{6,30},{8,16},{10,18},{12,20},{14,22},{16,8},... | collective-permute-start | bytes 73736 | tf_op jit(solution)/shard_map/ppermute | solution.py:28
  125.4 13.4 %collective-permute-start.8 = (bf16[4,3072]{1,0:T(4,128)(2,1)S(1)}, bf16[4,3072]{1,0:T(4,128)(2,1)S(1)}, u32[]{:S(2)}, u32[]{:S(2)}) collective-permute-start(bf16[4,3072]{1,0:T(4,128)(2,1)S(1)} %get-tuple-element.39), channel_id=1, source_target_pairs={{0,16},{2,18},{4,20},{6,22},{8,24},{10,26},{12,28},{14,30},{16,0},... | collective-permute-start | bytes 73736 | tf_op jit(solution)/shard_map/ppermute | solution.py:28
  130.5 10.0 %collective-permute-start.7 = (bf16[4,3072]{1,0:T(4,128)(2,1)S(1)}, bf16[4,3072]{1,0:T(4,128)(2,1)S(1)}, u32[]{:S(2)}, u32[]{:S(2)}) collective-permute-start(bf16[4,3072]{1,0:T(4,128)(2,1)S(1)} %get-tuple-element.40), channel_id=1, source_target_pairs={{0,8},{2,10},{4,12},{6,14},{8,0},{10,2},{12,4},{14,6},{16,24},{18,... | collective-permute-start | bytes 73736 | tf_op jit(solution)/shard_map/ppermute | solution.py:28
  138.8 1.7 %copy-start.2 = (bf16[4,3072]{1,0:T(4,128)(2,1)}, bf16[4,3072]{1,0:T(4,128)(2,1)S(1)}, u32[]{:S(2)}) copy-start(bf16[4,3072]{1,0:T(4,128)(2,1)S(1)} %collective-permute-done.8.rest_1_) | copy-start | bytes 73732
  140.6 0.6 copy-start.3

commit v6 on v5

--- a/solution.py
+++ b/solution.py
@@ -6,10 +6,11 @@
 from jax.experimental import pallas as pl
 from jax.sharding import Mesh, PartitionSpec as P
 
-AXES = ("x", "yh", "yl", "z", "core")
+AXES = ("x", "yh", "yl", "zh", "zl", "core")
 DP = ("x", "yh")
-MP = ("yl", "z", "core")
-STAGES = (("core", (1,)), ("z", (1, 2,)), ("yl", (1,)), ("z", (4, 8,)))
+Z = ("zh", "zl")
+MP = ("yl", *Z, "core")
+STAGES = (("core", (1,)), (Z, (1, 2,)), ("yl", (1,)), (Z, (4, 8,)))
 contract_last = (((1,), (1,)), ((), ()))
 contract_first = (((0,), (0,)), ((), ()))
 
@@ -38,63 +39,62 @@
         for step in reversed(bits):
             block //= 2
             bit = (at // block) % 2
-            if axis == "z":
+            if axis == Z:
                 far = far + bit * step
             else:
                 old = old + bit * (n_z * rows * (2 if axis == "core" else 1))
-    old = old + (far ^ lax.axis_index("z")) * rows
+    old = old + (far % 2) * (n_z // 2 * rows) + (far // 2 ^ lax.axis_index("zh")) * rows
     return (old == column).astype(jnp.bfloat16)
 
 
-def norm_kernel(inputs, gain, cotangent, joined, normal_out, inverse_out):
-    width = inputs.shape[1]
+def normalise(inputs):
     widened = inputs[...].astype(jnp.float32)
     centred = widened - jnp.mean(widened, axis=1, keepdims=True)
     variance = jnp.mean(centred * centred, axis=1, keepdims=True)
     inverse = 1.0 / jnp.sqrt(variance + 1e-06)
-    normal = centred * inverse
+    return centred * inverse, inverse
+
+
+def norm_kernel(inputs, gain, cotangent, joined):
+    width = inputs.shape[1]
+    normal, _ = normalise(inputs)
     joined[:, :width] = (normal * gain[...]).astype(jnp.bfloat16)
     joined[:, width:] = cotangent[...]
-    normal_out[...] = normal
-    inverse_out[...] = jnp.broadcast_to(inverse, inverse_out.shape)
 
 
 def join_normed(inputs, gain, cotangent):
     rows, width = inputs.shape
     return pl.pallas_call(
         norm_kernel,
-        out_shape=(
-            jax.ShapeDtypeStruct((rows, 2 * width), jnp.bfloat16),
-            jax.ShapeDtypeStruct((rows, width), jnp.float32),
-            jax.ShapeDtypeStruct((rows, 128), jnp.float32),
-        ),
+        out_shape=jax.ShapeDtypeStruct((rows, 2 * width), jnp.bfloat16),
         name="norm",
     )(inputs, gain[None, :], cotangent)
 
 
-def back_kernel(keep, normal, inverse, gain, cotangent, *rest):
+def back_kernel(keep, inputs, gain, cotangent, *rest):
     *aways, result = rest
-    normal = normal[...]
+    normal, inverse = normalise(inputs)
     terms = keep[...]
     for away in aways:
         terms = terms + away[...].astype(jnp.float32)
     scaled = terms * gain[...]
     first_mean = jnp.mean(scaled, axis=1, keepdims=True)
     second_mean = jnp.mean(scaled * normal, axis=1, keepdims=True)
-    change = (scaled - first_mean - normal * second_mean) * inverse[:, :1]
+    change = (scaled - first_mean - normal * second_mean) * inverse
     result[...] = (cotangent[...].astype(jnp.float32) + change).astype(jnp.bfloat16)
 
 
 def body(inputs, gain, w_in, w_out, cotangent):
     rows, width = inputs.shape
     n_dp = lax.axis_size(DP)
-    n_z = lax.axis_size("z")
-    joined, normal, inverse = join_normed(inputs, gain, cotangent)
+    n_z = lax.axis_size(Z)
+    joined = join_normed(inputs, gain, cotangent)
 
-    both = lax.all_gather(joined, "z", axis=0, tiled=True)
-    both, zero = lax.optimization_barrier((both, jnp.int32(0)))
+    even = lax.all_gather(joined, "zh", axis=0, tiled=True)
+    even, zero = lax.optimization_barrier((even, jnp.int32(0)))
     order = stage_order(rows, n_z, zero)
-    both = jnp.concatenate([both, swap(both, "yl", 1)], axis=0)
+    odd = swap(even, "zl", 1)
+    both = jnp.concatenate([even, odd, swap(even, "yl", 1), swap(odd, "yl", 1)], axis=0)
     both, order = lax.optimization_barrier((both, order))
     both = jnp.concatenate([both, swap(both, "core", 1)], axis=0)
     normed_all, grad_all = both[:, :width], both[:, width:]
@@ -147,12 +147,12 @@
         out_shape=jax.ShapeDtypeStruct(inputs.shape, jnp.bfloat16),
         cost_estimate=pl.CostEstimate(flops=0, bytes_accessed=0, transcendentals=0),
         name="norm_back",
-    )(keep, normal, inverse, gain[None, :], cotangent, *aways)
+    )(keep, inputs, gain[None, :], cotangent, *aways)
     return (input_grad, grad_in, grad_out)
 
 
 def solution(mesh):
-    fine = Mesh(mesh.devices.reshape(4, 2, 2, 16, 2), AXES)
+    fine = Mesh(mesh.devices.reshape(4, 2, 2, 8, 2, 2), AXES)
     rows, hidden_split = P(DP + MP, None), P(None, MP)
     in_specs = (rows, P(), hidden_split, P(MP, None), rows)
     out_specs = (rows, hidden_split, P(MP, None))

time: 155 us -> 160 us (1.032)
  waiting for transfers between devices: 44.8 us -> 48 us
  starting transfers between devices: 53.6 us -> 56.6 us
  blocking collectives: 34.2 us -> 32 us
    ppermute x10 -> x12, waiting for transfers between devices: 32.3 us -> 35.9 us  [swap(): lax.ppermute(rows, axis, [(at, at ^ step) for at in range(lax.axis_size(a...]
    ppermute x10 -> x12, starting transfers between devices: 42.9 us -> 46.4 us  [swap(): lax.ppermute(rows, axis, [(at, at ^ step) for at in range(lax.axis_size(a...]
    all_gather x1, blocking collectives: 34.2 us -> 32 us  [body(): even = lax.all_gather(joined, 'zh', axis=0, tiled=True)]
  transfers between devices with their start and end apart: 12 -> 14, of which waited for: 9 -> 10; matrix products, arithmetic and copies ran while one was open for 6% -> 6% of each run, Pallas kernels for 1% -> 1%
where the time goes in v6:
time: 160 us; the launch traced here: 158 us
  starting transfers between devices  56.6 us (35%)
  waiting for transfers between devices  48 us (30%)
  blocking collectives  32 us (20%)
  local copies, waits for them, and re-layouts  6.45 us (4%)
  matrix products  5.41 us (3%)
  other arithmetic  5.13 us (3%)
  Pallas kernels  3.53 us (2%)
    ppermute x12, starting transfers between devices, swap(): lax.ppermute(rows, axis, [(at, at ^ step) for at in range(lax.axis_size(a...  46.4 us
    ppermute x12, waiting for transfers between devices, swap(): lax.ppermute(rows, axis, [(at, at ^ step) for at in range(lax.axis_size(a...  35.9 us
    all_gather x1, blocking collectives, body(): even = lax.all_gather(joined, 'zh', axis=0, tiled=True)  32 us
    all_to_all x1, waiting for transfers between devices, body(): spread = lax.all_to_all(spread, DP, 0, 0, tiled=True)  8.99 us
    all_to_all x1, starting transfers between devices, body(): parts = lax.all_to_all(parts, DP, 0, 0, tiled=True)  6.36 us
    all_to_all x1, starting transfers between devices, body(): spread = lax.all_to_all(spread, DP, 0, 0, tiled=True)  3.88 us
  transfers between devices with their start and end apart: 14, of which 10 were waited for; matrix products, arithmetic and copies ran while one was open for 6% of the time, Pallas kernels for 1%

profile of v6, /device:TPU:1, one launch (start us, length us, event | category | flops | bytes accessed | tf_op | source)
XLA Modules:
  0.0 158.2 jit_solution(7911413100622091020)
XLA Ops:
  2.4 32.0 %all-gather = bf16[8,4,6144]{2,1,0:T(4,128)(2,1)S(1)} all-gather(bf16[1,4,6144]{2,1,0:T(4,128)(2,1)} %bitcast.18), channel_id=1, replica_groups=mesh['x'=4,'yh'=2,'yl'=2,'zh'=8,'zl'=2,'core'=2] {'zh'}, dimensions={0}, use_global_device_ids=true | all-gather | bytes 442368 | tf_op jit(solution)/shard_map/all_gather | solution.py:93
  34.5 3.2 %collective-permute-start.1 = (bf16[32,6144]{1,0:T(8,128)(2,1)S(1)}, bf16[32,6144]{1,0:T(8,128)(2,1)S(1)}, u32[]{:S(2)}, u32[]{:S(2)}) collective-permute-start(bf16[32,6144]{1,0:T(8,128)(2,1)S(1)} %reshape.20), channel_id=1, source_target_pairs={{0,32},{32,0},{1,33},{33,1},{2,34},{34,2},{3,35},{35,3},{4,36},{36... | collective-permute-start | bytes 1179656 | tf_op jit(solution)/shard_map/ppermute | solution.py:29
  37.7 2.0 %collective-permute-start = (bf16[32,6144]{1,0:T(8,128)(2,1)S(1)}, bf16[32,6144]{1,0:T(8,128)(2,1)S(1)}, u32[]{:S(2)}, u32[]{:S(2)}) collective-permute-start(bf16[32,6144]{1,0:T(8,128)(2,1)S(1)} %reshape.20), channel_id=1, source_target_pairs={{0,2},{2,0},{1,3},{3,1},{4,6},{6,4},{5,7},{7,5},{8,10},{10,8},{9,1... | collective-permute-start | bytes 1179656 | tf_op jit(solution)/shard_map/ppermute | solution.py:29
  39.9 6.7 %collective-permute-done = bf16[32,6144]{1,0:T(8,128)(2,1)S(1)} collective-permute-done((bf16[32,6144]{1,0:T(8,128)(2,1)S(1)}, bf16[32,6144]{1,0:T(8,128)(2,1)S(1)}, u32[]{:S(2)}, u32[]{:S(2)}) %collective-permute-start) | collective-permute-done | bytes 393248 | tf_op jit(solution)/shard_map/ppermute | solution.py:29
  46.5 1.9 %collective-permute-start.2 = (bf16[32,6144]{1,0:T(8,128)(2,1)S(1)}, bf16[32,6144]{1,0:T(8,128)(2,1)S(1)}, u32[]{:S(2)}, u32[]{:S(2)}) collective-permute-start(bf16[32,6144]{1,0:T(8,128)(2,1)S(1)} %collective-permute-done), channel_id=1, source_target_pairs={{0,32},{32,0},{1,33},{33,1},{2,34},{34,2},{3,35},{35,3},{4,36},{36... | collective-permute-start | bytes 1179656 | tf_op jit(solution)/shard_map/ppermute | solution.py:29
  49.7 5.3 %collective-permute-done.2 = bf16[32,6144]{1,0:T(8,128)(2,1)S(1)} collective-permute-done((bf16[32,6144]{1,0:T(8,128)(2,1)S(1)}, bf16[32,6144]{1,0:T(8,128)(2,1)S(1)}, u32[]{:S(2)}, u32[]{:S(2)}) %collective-permute-start.2) | collective-permute-done | bytes 393248 | tf_op jit(solution)/shard_map/ppermute | solution.py:29
  55.2 10.5 %collective-permute-start.3 = (bf16[128,6144]{1,0:T(8,128)(2,1)S(1)}, bf16[128,6144]{1,0:T(8,128)(2,1)S(1)}, u32[]{:S(2)}, u32[]{:S(2)}) collective-permute-start(bf16[128,6144]{1,0:T(8,128)(2,1)S(1)} %pad_maximum_fusion.1), channel_id=1, source_target_pairs={{0,1},{1,0},{2,3},{3,2},{4,5},{5,4},{6,7},{7,6},{8,9},{9,8},{10,11... | collective-permute-start | bytes 4718600 | tf_op jit(solution)/shard_map/ppermute | solution.py:29
  65.8 2.9 %collective-permute-done.3 = bf16[128,6144]{1,0:T(8,128)(2,1)S(1)} collective-permute-done((bf16[128,6144]{1,0:T(8,128)(2,1)S(1)}, bf16[128,6144]{1,0:T(8,128)(2,1)S(1)}, u32[]{:S(2)}, u32[]{:S(2)}) %collective-permute-start.3) | collective-permute-done | bytes 1572896 | tf_op jit(solution)/shard_map/ppermute | solution.py:29
  72.4 2.3 %collective-permute-start.4 = (bf16[128,3072]{1,0:T(8,128)(2,1)}, bf16[128,3072]{1,0:T(8,128)(2,1)}, u32[]{:S(2)}, u32[]{:S(2)}) collective-permute-start(bf16[128,3072]{1,0:T(8,128)(2,1)} %convolution_convert_fusion.2), channel_id=1, source_target_pairs={{0,1},{1,0},{2,3},{3,2},{4,5},{5,4},{6,7},{7,6},{8,9},{9,8},{10,11... | collective-permute-start | bytes 2359304 | tf_op jit(solution)/shard_map/ppermute | solution.py:29
  77.2 6.4 %all-to-all-start = ((bf16[8,48,3072]{2,1,0:T(8,128)(2,1)}), bf16[8,48,3072]{2,1,0:T(8,128)(2,1)S(1)}, u32[]{:S(2)}, u32[]{:S(2)}) async-start(bf16[8,48,3072]{2,1,0:T(8,128)(2,1)} %bitcast.15), calls=%async_computation | async-start | bytes 4718592 | tf_op jit(solution)/shard_map/all_to_all | solution.py:122
  85.2 2.7 %collective-permute-start.5 = (bf16[32,3072]{1,0:T(8,128)(2,1)S(1)}, bf16[32,3072]{1,0:T(8,128)(2,1)S(1)}, u32[]{:S(2)}, u32[]{:S(2)}) collective-permute-start(bf16[32,3072]{1,0:T(8,128)(2,1)S(1)} %get-tuple-element.29), channel_id=1, source_target_pairs={{0,2},{2,0},{4,6},{6,4},{8,10},{10,8},{12,14},{14,12},{16,18},{18,... | collective-permute-start | bytes 589832 | tf_op jit(solution)/shard_map/ppermute | solution.py:29
  87.9 3.6 %collective-permute-start.7 = (bf16[32,3072]{1,0:T(8,128)(2,1)S(1)}, bf16[32,3072]{1,0:T(8,128)(2,1)S(1)}, u32[]{:S(2)}, u32[]{:S(2)}) collective-permute-start(bf16[32,3072]{1,0:T(8,128)(2,1)S(1)} %get-tuple-element.30), channel_id=1, source_target_pairs={{0,6},{2,4},{4,2},{6,0},{8,14},{10,12},{12,10},{14,8},{16,22},{18,... | collective-permute-start | bytes 589832 | tf_op jit(solution)/shard_map/ppermute | solution.py:29
  91.4 2.1 %collective-permute-start.6 = (bf16[32,3072]{1,0:T(8,128)(2,1)S(1)}, bf16[32,3072]{1,0:T(8,128)(2,1)S(1)}, u32[]{:S(2)}, u32[]{:S(2)}) collective-permute-start(bf16[32,3072]{1,0:T(8,128)(2,1)S(1)} %get-tuple-element.31), channel_id=1, source_target_pairs={{0,4},{2,6},{4,0},{6,2},{8,12},{10,14},{12,8},{14,10},{16,20},{18,... | collective-permute-start | bytes 589832 | tf_op jit(solution)/shard_map/ppermute | solution.py:29
  93.6 5.0 %collective-permute-done.7 = bf16[32,3072]{1,0:T(8,128)(2,1)S(1)} collective-permute-done((bf16[32,3072]{1,0:T(8,128)(2,1)S(1)}, bf16[32,3072]{1,0:T(8,128)(2,1)S(1)}, u32[]{:S(2)}, u32[]{:S(2)}) %collective-permute-start.7) | collective-permute-done | bytes 196640 | tf_op jit(solution)/shard_map/ppermute | solution.py:29
  98.6 9.9 %collective-permute-done.6 = bf16[32,3072]{1,0:T(8,128)(2,1)S(1)} collective-permute-done((bf16[32,3072]{1,0:T(8,128)(2,1)S(1)}, bf16[32,3072]{1,0:T(8,128)(2,1)S(1)}, u32[]{:S(2)}, u32[]{:S(2)}) %collective-permute-start.6) | collective-permute-done | bytes 196640 | tf_op jit(solution)/shard_map/ppermute | solution.py:29
  108.7 1.9 %collective-permute-start.8 = (bf16[16,3072]{1,0:T(8,128)(2,1)S(1)}, bf16[16,3072]{1,0:T(8,128)(2,1)S(1)}, u32[]{:S(2)}, u32[]{:S(2)}) collective-permute-start(bf16[16,3072]{1,0:T(8,128)(2,1)S(1)} %slice.108), channel_id=1, source_target_pairs={{0,32},{32,0},{1,33},{33,1},{2,34},{34,2},{3,35},{35,3},{4,36},{36... | collective-permute-start | bytes 294920 | tf_op jit(solution)/shard_map/ppermute | solution.py:29
  110.6 3.7 %collective-permute-done.8 = bf16[16,3072]{1,0:T(8,128)(2,1)S(1)} collective-permute-done((bf16[16,3072]{1,0:T(8,128)(2,1)S(1)}, bf16[16,3072]{1,0:T(8,128)(2,1)S(1)}, u32[]{:S(2)}, u32[]{:S(2)}) %collective-permute-start.8) | collective-permute-done | bytes 98336 | tf_op jit(solution)/shard_map/ppermute | solution.py:29
  115.0 3.2 %all-to-all-done = bf16[8,48,3072]{2,1,0:T(8,128)(2,1)S(1)} async-done(((bf16[8,48,3072]{2,1,0:T(8,128)(2,1)}), bf16[8,48,3072]{2,1,0:T(8,128)(2,1)S(1)}, u32[]{:S(2)}, u32[]{:S(2)}) %all-to-all-start) | async-done | bytes 2359328 | tf_op jit(solution)/shard_map/all_to_all | solution.py:122
  120.3 3.9 %all-to-all-start.1 = ((bf16[8,48,3072]{2,1,0:T(8,128)(2,1)}), bf16[8,48,3072]{2,1,0:T(8,128)(2,1)S(1)}, u32[]{:S(2)}, u32[]{:S(2)}) async-start(bf16[8,48,3072]{2,1,0:T(8,128)(2,1)} %broadcast_in_dim.5), calls=%async_computation.1 | async-start | bytes 4718592 | tf_op jit(solution)/shard_map/all_to_all | solution.py:138
  125.1 5.3 %collective-permute-start.11 = (bf16[4,3072]{1,0:T(4,128)(2,1)S(1)}, bf16[4,3072]{1,0:T(4,128)(2,1)}, u32[]{:S(2)}, u32[]{:S(2)}) collective-permute-start(bf16[4,3072]{1,0:T(4,128)(2,1)S(1)} %get-tuple-element.32), channel_id=1, source_target_pairs={{0,24},{2,26},{4,28},{6,30},{8,16},{10,18},{12,20},{14,22},{16,8},... | collective-permute-start | bytes 73736 | tf_op jit(solution)/shard_map/ppermute | solution.py:29
  130.4 6.5 %collective-permute-start.10 = (bf16[4,3072]{1,0:T(4,128)(2,1)S(1)}, bf16[4,3072]{1,0:T(4,128)(2,1)S(1)}, u32[]{:S(2)}, u32[]{:S(2)}) collective-permute-start(bf16[4,3072]{1,0:T(4,128)(2,1)S(1)} %get-tuple-element.33), channel_id=1, source_target_pairs={{0,16},{2,18},{4,20},{6,22},{8,24},{10,26},{12,28},{14,30},{16,0},... | collective-permute-start | bytes 73736 | tf_op jit(solution)/shard_map/ppermute | solution.py:29
  137.0 4.4 %collective-permute-start.9 = (bf16[4,3072]{1,0:T(4,128)(2,1)S(1)}, bf16[4,3072]{1,0:T(4,128)(2,1)}, u32[]{:S(2)}, u32[]{:S(2)}) collective-permute-start(bf16[4,3072]{1,0:T(4,128)(2,1)S(1)} %get-tuple-element.34), channel_id=1, source_target_pairs={{0,8},{2,10},{4,12},{6,14},{8,0},{10,2},{12,4},{14,6},{16,24},{18,... | collective-permute-start | bytes 73736 | tf_op jit(solution)/shard_map/ppermute | solution.py:29
  145.7 1.8 %norm_back.1 = bf16[4,3072]{1,0:T(4,128)(2,1)} custom-call(f32[4,3072]{1,0:T(4,128)} %slice.67.keep, bf16[4,3072]{1,0:T(4,128)(2,1)} %inputs.3, f32[1,3072]{1,0:T(1,128)} %bitcast.20, bf16[4,3072]{1,0:T(4,128)(2,1)} %cotangent.3, bf16[4,3072]{1,0:T(4,128)(2,1)} %collective-permute-done.9.rest_0_, bf16[4,3072]{1,0:T(4,128)(2,1)} %copy-done.2, ...), custom_call_target="tpu_custom_call" | custom-call | tf_op jit(solution)/shard_map/norm_back/pallas_call | solution.py:145
  147.5 9.0 %all-to-all-done.1 = bf16[8,48,3072]{2,1,0:T(8,128)(2,1)S(1)} async-done(((bf16[8,48,3072]{2,1,0:T(8,128)(2,1)}), bf16[8,48,3072]{2,1,0:T(8,128)(2,1)S(1)}, u32[]{:S(2)}, u32[]{:S(2)}) %all-to-all-start.1) | async-done | bytes 2359328 | tf_op jit(solution)/shard_map/all_to_all | solution.py:138
  (50 shorter events, 21.0 us)
Async XLA Ops:
  0.6 68.3 %copy-start = (bf16[3072,192]{0,1:T(8,128)(2,1)S(1)}, bf16[3072,192]{0,1:T(8,128)(2,1)}, u32[]{:S(2)}) copy-start(bf16[3072,192]{0,1:T(8,128)(2,1)} %param.7) | copy-start | bytes 3538948
  34.5 15.2 %collective-permute-start.1 = (bf16[32,6144]{1,0:T(8,128)(2,1)S(1)}, bf16[32,6144]{1,0:T(8,128)(2,1)S(1)}, u32[]{:S(2)}, u32[]{:S(2)}) collective-permute-start(bf16[32,6144]{1,0:T(8,128)(2,1)S(1)} %reshape.20), channel_id=1, source_target_pairs={{0,32},{32,0},{1,33},{33,1},{2,34},{34,2},{3,35},{35,3},{4,36},{36... | collective-permute-start | bytes 1179656 | tf_op jit(solution)/shard_map/ppermute | solution.py:29
  37.7 8.8 %collective-permute-start = (bf16[32,6144]{1,0:T(8,128)(2,1)S(1)}, bf16[32,6144]{1,0:T(8,128)(2,1)S(1)}, u32[]{:S(2)}, u32[]{:S(2)}) collective-permute-start(bf16[32,6144]{1,0:T(8,128)(2,1)S(1)} %reshape.20), channel_id=1, source_target_pairs={{0,2},{2,0},{1,3},{3,1},{4,6},{6,4},{5,7},{7,5},{8,10},{10,8},{9,1... | collective-permute-start | bytes 1179656 | tf_op jit(solution)/shard_map/ppermute | solution.py:29
  46.5 8.5 %collective-permute-start.2 = (bf16[32,6144]{1,0:T(8,128)(2,1)S(1)}, bf16[32,6144]{1,0:T(8,128)(2,1)S(1)}, u32[]{:S(2)}, u32[]{:S(2)}) collective-permute-start(bf16[32,6144]{1,0:T(8,128)(2,1)S(1)} %collective-permute-done), channel_id=1, source_target_pairs={{0,32},{32,0},{1,33},{33,1},{2,34},{34,2},{3,35},{35,3},{4,36},{36... | collective-permute-start | bytes 1179656 | tf_op jit(solution)/shard_map/ppermute | solution.py:29
  55.2 13.6 %collective-permute-start.3 = (bf16[128,6144]{1,0:T(8,128)(2,1)S(1)}, bf16[128,6144]{1,0:T(8,128)(2,1)S(1)}, u32[]{:S(2)}, u32[]{:S(2)}) collective-permute-start(bf16[128,6144]{1,0:T(8,128)(2,1)S(1)} %pad_maximum_fusion.1), channel_id=1, source_target_pairs={{0,1},{1,0},{2,3},{3,2},{4,5},{5,4},{6,7},{7,6},{8,9},{9,8},{10,11... | collective-permute-start | bytes 4718600 | tf_op jit(solution)/shard_map/ppermute | solution.py:29
  68.9 1.3 copy-start.3
  71.1 4.1 %copy-start.1 = (bf16[256,192]{0,1:T(8,128)(2,1)}, bf16[256,192]{0,1:T(8,128)(2,1)S(1)}, u32[]{:S(2)}) copy-start(bf16[256,192]{0,1:T(8,128)(2,1)S(1)} %convolution_convert_fusion.3) | copy-start | bytes 294916
  72.4 11.2 %collective-permute-start.4 = (bf16[128,3072]{1,0:T(8,128)(2,1)}, bf16[128,3072]{1,0:T(8,128)(2,1)}, u32[]{:S(2)}, u32[]{:S(2)}) collective-permute-start(bf16[128,3072]{1,0:T(8,128)(2,1)} %convolution_convert_fusion.2), channel_id=1, source_target_pairs={{0,1},{1,0},{2,3},{3,2},{4,5},{5,4},{6,7},{7,6},{8,9},{9,8},{10,11... | collective-permute-start | bytes 2359304 | tf_op jit(solution)/shard_map/ppermute | solution.py:29
  77.2 41.0 %all-to-all-start = ((bf16[8,48,3072]{2,1,0:T(8,128)(2,1)}), bf16[8,48,3072]{2,1,0:T(8,128)(2,1)S(1)}, u32[]{:S(2)}, u32[]{:S(2)}) async-start(bf16[8,48,3072]{2,1,0:T(8,128)(2,1)} %bitcast.15), calls=%async_computation | async-start | bytes 4718592 | tf_op jit(solution)/shard_map/all_to_all | solution.py:122
  85.2 8.4 %collective-permute-start.5 = (bf16[32,3072]{1,0:T(8,128)(2,1)S(1)}, bf16[32,3072]{1,0:T(8,128)(2,1)S(1)}, u32[]{:S(2)}, u32[]{:S(2)}) collective-permute-start(bf16[32,3072]{1,0:T(8,128)(2,1)S(1)} %get-tuple-element.29), channel_id=1, source_target_pairs={{0,2},{2,0},{4,6},{6,4},{8,10},{10,8},{12,14},{14,12},{16,18},{18,... | collective-permute-start | bytes 589832 | tf_op jit(solution)/shard_map/ppermute | solution.py:29
  87.9 10.7 %collective-permute-start.7 = (bf16[32,3072]{1,0:T(8,128)(2,1)S(1)}, bf16[32,3072]{1,0:T(8,128)(2,1)S(1)}, u32[]{:S(2)}, u32[]{:S(2)}) collective-permute-start(bf16[32,3072]{1,0:T(8,128)(2,1)S(1)} %get-tuple-element.30), channel_id=1, source_target_pairs={{0,6},{2,4},{4,2},{6,0},{8,14},{10,12},{12,10},{14,8},{16,22},{18,... | collective-permute-start | bytes 589832 | tf_op jit(solution)/shard_map/ppermute | solution.py:29
  91.4 17.1 %collective-permute-start.6 = (bf16[32,3072]{1,0:T(8,128)(2,1)S(1)}, bf16[32,3072]{1,0:T(8,128)(2,1)S(1)}, u32[]{:S(2)}, u32[]{:S(2)}) collective-permute-start(bf16[32,3072]{1,0:T(8,128)(2,1)S(1)} %get-tuple-element.31), channel_id=1, source_target_pairs={{0,4},{2,6},{4,0},{6,2},{8,12},{10,14},{12,8},{14,10},{16,20},{18,... | collective-permute-start | bytes 589832 | tf_op jit(solution)/shard_map/ppermute | solution.py:29
  108.7 5.7 %collective-permute-start.8 = (bf16[16,3072]{1,0:T(8,128)(2,1)S(1)}, bf16[16,3072]{1,0:T(8,128)(2,1)S(1)}, u32[]{:S(2)}, u32[]{:S(2)}) collective-permute-start(bf16[16,3072]{1,0:T(8,128)(2,1)S(1)} %slice.108), channel_id=1, source_target_pairs={{0,32},{32,0},{1,33},{33,1},{2,34},{34,2},{3,35},{35,3},{4,36},{36... | collective-permute-start | bytes 294920 | tf_op jit(solution)/shard_map/ppermute | solution.py:29
  120.3 36.3 %all-to-all-start.1 = ((bf16[8,48,3072]{2,1,0:T(8,128)(2,1)}), bf16[8,48,3072]{2,1,0:T(8,128)(2,1)S(1)}, u32[]{:S(2)}, u32[]{:S(2)}) async-start(bf16[8,48,3072]{2,1,0:T(8,128)(2,1)} %broadcast_in_dim.5), calls=%async_computation.1 | async-start | bytes 4718592 | tf_op jit(solution)/shard_map/all_to_all | solution.py:138
  125.1 17.7 %collective-permute-start.11 = (bf16[4,3072]{1,0:T(4,128)(2,1)S(1)}, bf16[4,3072]{1,0:T(4,128)(2,1)}, u32[]{:S(2)}, u32[]{:S(2)}) collective-permute-start(bf16[4,3072]{1,0:T(4,128)(2,1)S(1)} %get-tuple-element.32), channel_id=1, source_target_pairs={{0,24},{2,26},{4,28},{6,30},{8,16},{10,18},{12,20},{14,22},{16,8},... | collective-permute-start | bytes 73736 | tf_op jit(solution)/shard_map/ppermute | solution.py:29
  130.4 13.3 %collective-permute-start.10 = (bf16[4,3072]{1,0:T(4,128)(2,1)S(1)}, bf16[4,3072]{1,0:T(4,128)(2,1)S(1)}, u32[]{:S(2)}, u32[]{:S(2)}) collective-permute-start(bf16[4,3072]{1,0:T(4,128)(2,1)S(1)} %get-tuple-element.33), channel_id=1, source_target_pairs={{0,16},{2,18},{4,20},{6,22},{8,24},{10,26},{12,28},{14,30},{16,0},... | collective-permute-start | bytes 73736 | tf_op jit(solution)/shard_map/ppermute | solution.py:29
  137.0 8.8 %collective-permute-start.9 = (bf16[4,3072]{1,0:T(4,128)(2,1)S(1)}, bf16[4,3072]{1,0:T(4,128)(2,1)}, u32[]{:S(2)}, u32[]{:S(2)}) collective-permute-start(bf16[4,3072]{1,0:T(4,128)(2,1)S(1)} %get-tuple-element.34), channel_id=1, source_target_pairs={{0,8},{2,10},{4,12},{6,14},{8,0},{10,2},{12,4},{14,6},{16,24},{18,... | collective-permute-start | bytes 73736 | tf_op jit(solution)/shard_map/ppermute | solution.py:29
  143.7 0.6 copy-start.2

commit v7 on v5

--- a/solution.py
+++ b/solution.py
@@ -94,9 +94,10 @@
     both = lax.all_gather(joined, "z", axis=0, tiled=True)
     both, zero = lax.optimization_barrier((both, jnp.int32(0)))
     order = stage_order(rows, n_z, zero)
-    both = jnp.concatenate([both, swap(both, "yl", 1)], axis=0)
-    both, order = lax.optimization_barrier((both, order))
-    both = jnp.concatenate([both, swap(both, "core", 1)], axis=0)
+    beside = swap(both, "yl", 1)
+    own = swap(both, "core", 1)
+    beside, own, order = lax.optimization_barrier((beside, own, order))
+    both = jnp.concatenate([both, beside, own, swap(beside, "core", 1)], axis=0)
     normed_all, grad_all = both[:, :width], both[:, width:]
 
     hidden = jnp.dot(normed_all, w_in, preferred_element_type=jnp.float32)
@@ -129,11 +130,11 @@
         if k == len(STAGES) - 1:
             break
         total = keep + sum(away.astype(jnp.float32) for away in aways)
-        if k == 2:
+        if k == 1:
             parts, _ = lax.optimization_barrier((parts, total))
             mine = (jnp.sum(parts.astype(jnp.float32), axis=0) / n_dp).astype(jnp.bfloat16)
             spread = jnp.broadcast_to(mine[None], (n_dp, *mine.shape))
-        if k == 2:
+        if k == 1:
             spread, total = lax.optimization_barrier((spread, total))
             spread = lax.all_to_all(spread, DP, 0, 0, tiled=True)
         size = total.shape[0] // 2 ** len(STAGES[k + 1][1])

time: 155 us -> 177 us (1.14)
  the two profiles are of different devices: /device:TPU:1 before, /device:TPU:18 now
where the time goes in v7:
time: 177 us; the launch traced here: 176 us
  waiting for transfers between devices  54.2 us (31%)
  starting transfers between devices  53.8 us (30%)
  blocking collectives  40.4 us (23%)
  other arithmetic  11.2 us (6%)
  local copies, waits for them, and re-layouts  6.55 us (4%)
  matrix products  5.44 us (3%)
  Pallas kernels  3.34 us (2%)
    ppermute x11, waiting for transfers between devices, swap(): lax.ppermute(rows, axis, [(at, at ^ step) for at in range(lax.axis_size(a...  45.2 us
    all_gather x1, blocking collectives, body(): both = lax.all_gather(joined, 'z', axis=0, tiled=True)  40.4 us
    ppermute x11, starting transfers between devices, swap(): lax.ppermute(rows, axis, [(at, at ^ step) for at in range(lax.axis_size(a...  39.4 us
    all_to_all x1, waiting for transfers between devices, body(): parts = lax.all_to_all(parts, DP, 0, 0, tiled=True)  9.02 us
    all_to_all x1, starting transfers between devices, body(): parts = lax.all_to_all(parts, DP, 0, 0, tiled=True)  7.25 us
    all_to_all x1, starting transfers between devices, body(): spread = lax.all_to_all(spread, DP, 0, 0, tiled=True)  7.16 us
  transfers between devices with their start and end apart: 13, of which 6 were waited for; matrix products, arithmetic and copies ran while one was open for 8% of the time, Pallas kernels for 1%

profile of v7, /device:TPU:18, one launch (start us, length us, event | category | flops | bytes accessed | tf_op | source)
XLA Modules:
  0.0 175.9 jit_solution(13234432594260166814)
XLA Ops:
  0.6 1.7 norm.1
  2.4 40.4 %all-gather = bf16[16,4,6144]{2,1,0:T(4,128)(2,1)S(1)} all-gather(bf16[1,4,6144]{2,1,0:T(4,128)(2,1)} %bitcast.20), channel_id=1, replica_groups=mesh['x'=4,'yh'=2,'yl'=2,'z'=16,'core'=2] {'z'}, dimensions={0}, use_global_device_ids=true | all-gather | bytes 835584 | tf_op jit(solution)/shard_map/all_gather | solution.py:94
  43.0 3.2 %collective-permute-start = (bf16[64,6144]{1,0:T(8,128)(2,1)S(1)}, bf16[64,6144]{1,0:T(8,128)(2,1)S(1)}, u32[]{:S(2)}, u32[]{:S(2)}) collective-permute-start(bf16[64,6144]{1,0:T(8,128)(2,1)S(1)} %reshape.20), channel_id=1, source_target_pairs={{0,32},{32,0},{1,33},{33,1},{2,34},{34,2},{3,35},{35,3},{4,36},{36... | collective-permute-start | bytes 2359304 | tf_op jit(solution)/shard_map/ppermute | solution.py:28
  46.2 1.9 %collective-permute-start.1 = (bf16[64,6144]{1,0:T(8,128)(2,1)S(1)}, bf16[64,6144]{1,0:T(8,128)(2,1)S(1)}, u32[]{:S(2)}, u32[]{:S(2)}) collective-permute-start(bf16[64,6144]{1,0:T(8,128)(2,1)S(1)} %reshape.20), channel_id=1, source_target_pairs={{0,1},{1,0},{2,3},{3,2},{4,5},{5,4},{6,7},{7,6},{8,9},{9,8},{10,11... | collective-permute-start | bytes 2359304 | tf_op jit(solution)/shard_map/ppermute | solution.py:28
  53.3 2.3 %fusion.32 = bf16[256,256]{1,0:T(8,128)(2,1)S(1)} fusion(s32[]{:T(128)S(6)} %axis_index.15, s32[256]{0:T(256)S(1)} %get-tuple-element.55, s32[256]{0:T(256)} %get-tuple-element.62, s32[256]{0:T(256)S(1)} %get-tuple-element.56, s32[256]{0:T(256)} %get-tuple-element.63, s32[256]{0:T(256)S(1)} %get-tuple-element.57, s32[256]{0:T(256)} %get-tuple-element.64, ...), kind=kLoop, calls=%fused_computation.69 | loop fusion | flops 5767168 | bytes 147204 | tf_op jit(solution)/shard_map/convert_element_type | solution.py:46
  57.1 1.9 %collective-permute-start.2 = (bf16[64,6144]{1,0:T(8,128)(2,1)S(1)}, bf16[64,6144]{1,0:T(8,128)(2,1)S(1)}, u32[]{:S(2)}, u32[]{:S(2)}) collective-permute-start(bf16[64,6144]{1,0:T(8,128)(2,1)S(1)} %collective-permute-done), channel_id=1, source_target_pairs={{0,1},{1,0},{2,3},{3,2},{4,5},{5,4},{6,7},{7,6},{8,9},{9,8},{10,11... | collective-permute-start | bytes 2359304 | tf_op jit(solution)/shard_map/ppermute | solution.py:28
  59.1 2.1 %collective-permute-done.2 = bf16[64,6144]{1,0:T(8,128)(2,1)S(1)} collective-permute-done((bf16[64,6144]{1,0:T(8,128)(2,1)S(1)}, bf16[64,6144]{1,0:T(8,128)(2,1)S(1)}, u32[]{:S(2)}, u32[]{:S(2)}) %collective-permute-start.2) | collective-permute-done | bytes 786464 | tf_op jit(solution)/shard_map/ppermute | solution.py:28
  65.3 2.0 %collective-permute-start.3 = (bf16[128,3072]{1,0:T(8,128)(2,1)}, bf16[128,3072]{1,0:T(8,128)(2,1)}, u32[]{:S(2)}, u32[]{:S(2)}) collective-permute-start(bf16[128,3072]{1,0:T(8,128)(2,1)} %convolution_convert_fusion.2), channel_id=1, source_target_pairs={{0,1},{1,0},{2,3},{3,2},{4,5},{5,4},{6,7},{7,6},{8,9},{9,8},{10,11... | collective-permute-start | bytes 2359304 | tf_op jit(solution)/shard_map/ppermute | solution.py:28
  69.4 7.2 %all-to-all-start = ((bf16[8,48,3072]{2,1,0:T(8,128)(2,1)}), bf16[8,48,3072]{2,1,0:T(8,128)(2,1)S(1)}, u32[]{:S(2)}, u32[]{:S(2)}) async-start(bf16[8,48,3072]{2,1,0:T(8,128)(2,1)} %bitcast.15), calls=%async_computation | async-start | bytes 4718592 | tf_op jit(solution)/shard_map/all_to_all | solution.py:123
  78.3 1.9 %collective-permute-start.4 = (bf16[32,3072]{1,0:T(8,128)(2,1)S(1)}, bf16[32,3072]{1,0:T(8,128)(2,1)S(1)}, u32[]{:S(2)}, u32[]{:S(2)}) collective-permute-start(bf16[32,3072]{1,0:T(8,128)(2,1)S(1)} %get-tuple-element.39), channel_id=1, source_target_pairs={{0,2},{2,0},{4,6},{6,4},{8,10},{10,8},{12,14},{14,12},{16,18},{18,... | collective-permute-start | bytes 589832 | tf_op jit(solution)/shard_map/ppermute | solution.py:28
  80.2 2.2 %collective-permute-start.5 = (bf16[32,3072]{1,0:T(8,128)(2,1)S(1)}, bf16[32,3072]{1,0:T(8,128)(2,1)S(1)}, u32[]{:S(2)}, u32[]{:S(2)}) collective-permute-start(bf16[32,3072]{1,0:T(8,128)(2,1)S(1)} %get-tuple-element.41), channel_id=1, source_target_pairs={{0,4},{2,6},{4,0},{6,2},{8,12},{10,14},{12,8},{14,10},{16,20},{18,... | collective-permute-start | bytes 589832 | tf_op jit(solution)/shard_map/ppermute | solution.py:28
  82.4 6.0 %collective-permute-start.6 = (bf16[32,3072]{1,0:T(8,128)(2,1)S(1)}, bf16[32,3072]{1,0:T(8,128)(2,1)S(1)}, u32[]{:S(2)}, u32[]{:S(2)}) collective-permute-start(bf16[32,3072]{1,0:T(8,128)(2,1)S(1)} %get-tuple-element.40), channel_id=1, source_target_pairs={{0,6},{2,4},{4,2},{6,0},{8,14},{10,12},{12,10},{14,8},{16,22},{18,... | collective-permute-start | bytes 589832 | tf_op jit(solution)/shard_map/ppermute | solution.py:28
  88.4 10.8 %collective-permute-done.5 = bf16[32,3072]{1,0:T(8,128)(2,1)S(1)} collective-permute-done((bf16[32,3072]{1,0:T(8,128)(2,1)S(1)}, bf16[32,3072]{1,0:T(8,128)(2,1)S(1)}, u32[]{:S(2)}, u32[]{:S(2)}) %collective-permute-start.5) | collective-permute-done | bytes 196640 | tf_op jit(solution)/shard_map/ppermute | solution.py:28
  100.1 9.0 %all-to-all-done = bf16[8,48,3072]{2,1,0:T(8,128)(2,1)S(1)} async-done(((bf16[8,48,3072]{2,1,0:T(8,128)(2,1)}), bf16[8,48,3072]{2,1,0:T(8,128)(2,1)S(1)}, u32[]{:S(2)}, u32[]{:S(2)}) %all-to-all-start) | async-done | bytes 2359328 | tf_op jit(solution)/shard_map/all_to_all | solution.py:123
  109.5 1.7 broadcast_in_dim.5
  111.2 7.2 %all-to-all-start.1 = ((bf16[8,48,3072]{2,1,0:T(8,128)(2,1)}), bf16[8,48,3072]{2,1,0:T(8,128)(2,1)S(1)}, u32[]{:S(2)}, u32[]{:S(2)}) async-start(bf16[8,48,3072]{2,1,0:T(8,128)(2,1)} %broadcast_in_dim.5), calls=%async_computation.1 | async-start | bytes 4718592 | tf_op jit(solution)/shard_map/all_to_all | solution.py:139
  119.3 3.2 %collective-permute-start.7 = (bf16[16,3072]{1,0:T(8,128)(2,1)S(1)}, bf16[16,3072]{1,0:T(8,128)(2,1)S(1)}, u32[]{:S(2)}, u32[]{:S(2)}) collective-permute-start(bf16[16,3072]{1,0:T(8,128)(2,1)S(1)} %slice.108), channel_id=1, source_target_pairs={{0,32},{32,0},{1,33},{33,1},{2,34},{34,2},{3,35},{35,3},{4,36},{36... | collective-permute-start | bytes 294920 | tf_op jit(solution)/shard_map/ppermute | solution.py:28
  122.5 24.3 %collective-permute-done.7 = bf16[16,3072]{1,0:T(8,128)(2,1)S(1)} collective-permute-done((bf16[16,3072]{1,0:T(8,128)(2,1)S(1)}, bf16[16,3072]{1,0:T(8,128)(2,1)S(1)}, u32[]{:S(2)}, u32[]{:S(2)}) %collective-permute-start.7) | collective-permute-done | bytes 98336 | tf_op jit(solution)/shard_map/ppermute | solution.py:28
  147.7 5.4 %collective-permute-start.10 = (bf16[4,3072]{1,0:T(4,128)(2,1)S(1)}, bf16[4,3072]{1,0:T(4,128)(2,1)}, u32[]{:S(2)}, u32[]{:S(2)}) collective-permute-start(bf16[4,3072]{1,0:T(4,128)(2,1)S(1)} %get-tuple-element.42), channel_id=1, source_target_pairs={{0,24},{2,26},{4,28},{6,30},{8,16},{10,18},{12,20},{14,22},{16,8},... | collective-permute-start | bytes 73736 | tf_op jit(solution)/shard_map/ppermute | solution.py:28
  153.2 4.1 %collective-permute-start.8 = (bf16[4,3072]{1,0:T(4,128)(2,1)S(1)}, bf16[4,3072]{1,0:T(4,128)(2,1)S(1)}, u32[]{:S(2)}, u32[]{:S(2)}) collective-permute-start(bf16[4,3072]{1,0:T(4,128)(2,1)S(1)} %get-tuple-element.44), channel_id=1, source_target_pairs={{0,8},{2,10},{4,12},{6,14},{8,0},{10,2},{12,4},{14,6},{16,24},{18,... | collective-permute-start | bytes 73736 | tf_op jit(solution)/shard_map/ppermute | solution.py:28
  157.3 7.5 %collective-permute-start.9 = (bf16[4,3072]{1,0:T(4,128)(2,1)S(1)}, bf16[4,3072]{1,0:T(4,128)(2,1)S(1)}, u32[]{:S(2)}, u32[]{:S(2)}) collective-permute-start(bf16[4,3072]{1,0:T(4,128)(2,1)S(1)} %get-tuple-element.43), channel_id=1, source_target_pairs={{0,16},{2,18},{4,20},{6,22},{8,24},{10,26},{12,28},{14,30},{16,0},... | collective-permute-start | bytes 73736 | tf_op jit(solution)/shard_map/ppermute | solution.py:28
  165.4 6.6 %collective-permute-done.9.rest_1_ = bf16[4,3072]{1,0:T(4,128)(2,1)S(1)} collective-permute-done((bf16[4,3072]{1,0:T(4,128)(2,1)S(1)}, bf16[4,3072]{1,0:T(4,128)(2,1)S(1)}, u32[]{:S(2)}, u32[]{:S(2)}) %collective-permute-start.9) | collective-permute-done | bytes 24608 | tf_op jit(solution)/shard_map/ppermute | solution.py:28
  172.7 1.6 norm_back.1
  174.3 1.6 fusion.46
  (50 shorter events, 19.0 us)
Async XLA Ops:
  0.6 60.7 %copy-start = (bf16[3072,192]{0,1:T(8,128)(2,1)S(1)}, bf16[3072,192]{0,1:T(8,128)(2,1)}, u32[]{:S(2)}) copy-start(bf16[3072,192]{0,1:T(8,128)(2,1)} %param.7) | copy-start | bytes 3538948
  43.0 14.1 %collective-permute-start = (bf16[64,6144]{1,0:T(8,128)(2,1)S(1)}, bf16[64,6144]{1,0:T(8,128)(2,1)S(1)}, u32[]{:S(2)}, u32[]{:S(2)}) collective-permute-start(bf16[64,6144]{1,0:T(8,128)(2,1)S(1)} %reshape.20), channel_id=1, source_target_pairs={{0,32},{32,0},{1,33},{33,1},{2,34},{34,2},{3,35},{35,3},{4,36},{36... | collective-permute-start | bytes 2359304 | tf_op jit(solution)/shard_map/ppermute | solution.py:28
  46.2 10.9 %collective-permute-start.1 = (bf16[64,6144]{1,0:T(8,128)(2,1)S(1)}, bf16[64,6144]{1,0:T(8,128)(2,1)S(1)}, u32[]{:S(2)}, u32[]{:S(2)}) collective-permute-start(bf16[64,6144]{1,0:T(8,128)(2,1)S(1)} %reshape.20), channel_id=1, source_target_pairs={{0,1},{1,0},{2,3},{3,2},{4,5},{5,4},{6,7},{7,6},{8,9},{9,8},{10,11... | collective-permute-start | bytes 2359304 | tf_op jit(solution)/shard_map/ppermute | solution.py:28
  57.1 4.2 %collective-permute-start.2 = (bf16[64,6144]{1,0:T(8,128)(2,1)S(1)}, bf16[64,6144]{1,0:T(8,128)(2,1)S(1)}, u32[]{:S(2)}, u32[]{:S(2)}) collective-permute-start(bf16[64,6144]{1,0:T(8,128)(2,1)S(1)} %collective-permute-done), channel_id=1, source_target_pairs={{0,1},{1,0},{2,3},{3,2},{4,5},{5,4},{6,7},{7,6},{8,9},{9,8},{10,11... | collective-permute-start | bytes 2359304 | tf_op jit(solution)/shard_map/ppermute | solution.py:28
  61.3 1.3 copy-start.4
  63.5 1.3 copy-start.1
  65.3 11.4 %collective-permute-start.3 = (bf16[128,3072]{1,0:T(8,128)(2,1)}, bf16[128,3072]{1,0:T(8,128)(2,1)}, u32[]{:S(2)}, u32[]{:S(2)}) collective-permute-start(bf16[128,3072]{1,0:T(8,128)(2,1)} %convolution_convert_fusion.2), channel_id=1, source_target_pairs={{0,1},{1,0},{2,3},{3,2},{4,5},{5,4},{6,7},{7,6},{8,9},{9,8},{10,11... | collective-permute-start | bytes 2359304 | tf_op jit(solution)/shard_map/ppermute | solution.py:28
  69.4 39.7 %all-to-all-start = ((bf16[8,48,3072]{2,1,0:T(8,128)(2,1)}), bf16[8,48,3072]{2,1,0:T(8,128)(2,1)S(1)}, u32[]{:S(2)}, u32[]{:S(2)}) async-start(bf16[8,48,3072]{2,1,0:T(8,128)(2,1)} %bitcast.15), calls=%async_computation | async-start | bytes 4718592 | tf_op jit(solution)/shard_map/all_to_all | solution.py:123
  78.3 10.1 %collective-permute-start.4 = (bf16[32,3072]{1,0:T(8,128)(2,1)S(1)}, bf16[32,3072]{1,0:T(8,128)(2,1)S(1)}, u32[]{:S(2)}, u32[]{:S(2)}) collective-permute-start(bf16[32,3072]{1,0:T(8,128)(2,1)S(1)} %get-tuple-element.39), channel_id=1, source_target_pairs={{0,2},{2,0},{4,6},{6,4},{8,10},{10,8},{12,14},{14,12},{16,18},{18,... | collective-permute-start | bytes 589832 | tf_op jit(solution)/shard_map/ppermute | solution.py:28
  80.2 19.0 %collective-permute-start.5 = (bf16[32,3072]{1,0:T(8,128)(2,1)S(1)}, bf16[32,3072]{1,0:T(8,128)(2,1)S(1)}, u32[]{:S(2)}, u32[]{:S(2)}) collective-permute-start(bf16[32,3072]{1,0:T(8,128)(2,1)S(1)} %get-tuple-element.41), channel_id=1, source_target_pairs={{0,4},{2,6},{4,0},{6,2},{8,12},{10,14},{12,8},{14,10},{16,20},{18,... | collective-permute-start | bytes 589832 | tf_op jit(solution)/shard_map/ppermute | solution.py:28
  82.4 16.8 %collective-permute-start.6 = (bf16[32,3072]{1,0:T(8,128)(2,1)S(1)}, bf16[32,3072]{1,0:T(8,128)(2,1)S(1)}, u32[]{:S(2)}, u32[]{:S(2)}) collective-permute-start(bf16[32,3072]{1,0:T(8,128)(2,1)S(1)} %get-tuple-element.40), channel_id=1, source_target_pairs={{0,6},{2,4},{4,2},{6,0},{8,14},{10,12},{12,10},{14,8},{16,22},{18,... | collective-permute-start | bytes 589832 | tf_op jit(solution)/shard_map/ppermute | solution.py:28
  111.2 63.1 %all-to-all-start.1 = ((bf16[8,48,3072]{2,1,0:T(8,128)(2,1)}), bf16[8,48,3072]{2,1,0:T(8,128)(2,1)S(1)}, u32[]{:S(2)}, u32[]{:S(2)}) async-start(bf16[8,48,3072]{2,1,0:T(8,128)(2,1)} %broadcast_in_dim.5), calls=%async_computation.1 | async-start | bytes 4718592 | tf_op jit(solution)/shard_map/all_to_all | solution.py:139
  119.3 27.5 %collective-permute-start.7 = (bf16[16,3072]{1,0:T(8,128)(2,1)S(1)}, bf16[16,3072]{1,0:T(8,128)(2,1)S(1)}, u32[]{:S(2)}, u32[]{:S(2)}) collective-permute-start(bf16[16,3072]{1,0:T(8,128)(2,1)S(1)} %slice.108), channel_id=1, source_target_pairs={{0,32},{32,0},{1,33},{33,1},{2,34},{34,2},{3,35},{35,3},{4,36},{36... | collective-permute-start | bytes 294920 | tf_op jit(solution)/shard_map/ppermute | solution.py:28
  147.7 17.7 %collective-permute-start.10 = (bf16[4,3072]{1,0:T(4,128)(2,1)S(1)}, bf16[4,3072]{1,0:T(4,128)(2,1)}, u32[]{:S(2)}, u32[]{:S(2)}) collective-permute-start(bf16[4,3072]{1,0:T(4,128)(2,1)S(1)} %get-tuple-element.42), channel_id=1, source_target_pairs={{0,24},{2,26},{4,28},{6,30},{8,16},{10,18},{12,20},{14,22},{16,8},... | collective-permute-start | bytes 73736 | tf_op jit(solution)/shard_map/ppermute | solution.py:28
  153.2 12.2 %collective-permute-start.8 = (bf16[4,3072]{1,0:T(4,128)(2,1)S(1)}, bf16[4,3072]{1,0:T(4,128)(2,1)S(1)}, u32[]{:S(2)}, u32[]{:S(2)}) collective-permute-start(bf16[4,3072]{1,0:T(4,128)(2,1)S(1)} %get-tuple-element.44), channel_id=1, source_target_pairs={{0,8},{2,10},{4,12},{6,14},{8,0},{10,2},{12,4},{14,6},{16,24},{18,... | collective-permute-start | bytes 73736 | tf_op jit(solution)/shard_map/ppermute | solution.py:28
  157.3 14.7 %collective-permute-start.9 = (bf16[4,3072]{1,0:T(4,128)(2,1)S(1)}, bf16[4,3072]{1,0:T(4,128)(2,1)S(1)}, u32[]{:S(2)}, u32[]{:S(2)}) collective-permute-start(bf16[4,3072]{1,0:T(4,128)(2,1)S(1)} %get-tuple-element.43), channel_id=1, source_target_pairs={{0,16},{2,18},{4,20},{6,22},{8,24},{10,26},{12,28},{14,30},{16,0},... | collective-permute-start | bytes 73736 | tf_op jit(solution)/shard_map/ppermute | solution.py:28
  165.4 6.6 %copy-start.2 = (bf16[4,3072]{1,0:T(4,128)(2,1)}, bf16[4,3072]{1,0:T(4,128)(2,1)S(1)}, u32[]{:S(2)}) copy-start(bf16[4,3072]{1,0:T(4,128)(2,1)S(1)} %collective-permute-done.8.rest_0_) | copy-start | bytes 73732
  172.0 0.6 copy-start.3

commit v8 on v7

--- a/solution.py
+++ b/solution.py
@@ -130,11 +130,11 @@
         if k == len(STAGES) - 1:
             break
         total = keep + sum(away.astype(jnp.float32) for away in aways)
-        if k == 1:
+        if k == 2:
             parts, _ = lax.optimization_barrier((parts, total))
             mine = (jnp.sum(parts.astype(jnp.float32), axis=0) / n_dp).astype(jnp.bfloat16)
             spread = jnp.broadcast_to(mine[None], (n_dp, *mine.shape))
-        if k == 1:
+        if k == 2:
             spread, total = lax.optimization_barrier((spread, total))
             spread = lax.all_to_all(spread, DP, 0, 0, tiled=True)
         size = total.shape[0] // 2 ** len(STAGES[k + 1][1])

time: 177 us -> 154 us (0.87)
  the two profiles are of different devices: /device:TPU:18 before, /device:TPU:1 now
where the time goes in v8:
time: 154 us; the launch traced here: 153 us
  starting transfers between devices  56.8 us (37%)
  waiting for transfers between devices  34.8 us (23%)
  blocking collectives  34.2 us (22%)
  other arithmetic  11.2 us (7%)
  local copies, waits for them, and re-layouts  6.5 us (4%)
  matrix products  5.44 us (4%)
  Pallas kernels  3.34 us (2%)
    ppermute x11, starting transfers between devices, swap(): lax.ppermute(rows, axis, [(at, at ^ step) for at in range(lax.axis_size(a...  46.2 us
    all_gather x1, blocking collectives, body(): both = lax.all_gather(joined, 'z', axis=0, tiled=True)  34.2 us
    ppermute x11, waiting for transfers between devices, swap(): lax.ppermute(rows, axis, [(at, at ^ step) for at in range(lax.axis_size(a...  24.1 us
    all_to_all x1, waiting for transfers between devices, body(): spread = lax.all_to_all(spread, DP, 0, 0, tiled=True)  8.08 us
    all_to_all x1, starting transfers between devices, body(): parts = lax.all_to_all(parts, DP, 0, 0, tiled=True)  6.65 us
    all_to_all x1, starting transfers between devices, body(): spread = lax.all_to_all(spread, DP, 0, 0, tiled=True)  3.95 us
  transfers between devices with their start and end apart: 13, of which 6 were waited for; matrix products, arithmetic and copies ran while one was open for 10% of the time, Pallas kernels for 1%

profile of v8, /device:TPU:1, one launch (start us, length us, event | category | flops | bytes accessed | tf_op | source)
XLA Modules:
  0.0 153.2 jit_solution(11791662643307920080)
XLA Ops:
  0.6 1.7 %norm.1 = (bf16[4,6144]{1,0:T(4,128)(2,1)}, f32[4,3072]{1,0:T(4,128)}, f32[4,128]{1,0:T(4,128)}) custom-call(bf16[4,3072]{1,0:T(4,128)(2,1)} %inputs.1, f32[1,3072]{1,0:T(1,128)} %bitcast.18, bf16[4,3072]{1,0:T(4,128)(2,1)} %cotangent.3), custom_call_target="tpu_custom_call" | custom-call | tf_op jit(solution)/shard_map/norm/pallas_call | solution.py:64
  2.4 34.2 %all-gather = bf16[16,4,6144]{2,1,0:T(4,128)(2,1)S(1)} all-gather(bf16[1,4,6144]{2,1,0:T(4,128)(2,1)} %bitcast.20), channel_id=1, replica_groups=mesh['x'=4,'yh'=2,'yl'=2,'z'=16,'core'=2] {'z'}, dimensions={0}, use_global_device_ids=true | all-gather | bytes 835584 | tf_op jit(solution)/shard_map/all_gather | solution.py:94
  36.7 3.2 %collective-permute-start = (bf16[64,6144]{1,0:T(8,128)(2,1)S(1)}, bf16[64,6144]{1,0:T(8,128)(2,1)S(1)}, u32[]{:S(2)}, u32[]{:S(2)}) collective-permute-start(bf16[64,6144]{1,0:T(8,128)(2,1)S(1)} %reshape.20), channel_id=1, source_target_pairs={{0,32},{32,0},{1,33},{33,1},{2,34},{34,2},{3,35},{35,3},{4,36},{36... | collective-permute-start | bytes 2359304 | tf_op jit(solution)/shard_map/ppermute | solution.py:28
  39.9 9.9 %collective-permute-start.1 = (bf16[64,6144]{1,0:T(8,128)(2,1)S(1)}, bf16[64,6144]{1,0:T(8,128)(2,1)S(1)}, u32[]{:S(2)}, u32[]{:S(2)}) collective-permute-start(bf16[64,6144]{1,0:T(8,128)(2,1)S(1)} %reshape.20), channel_id=1, source_target_pairs={{0,1},{1,0},{2,3},{3,2},{4,5},{5,4},{6,7},{7,6},{8,9},{9,8},{10,11... | collective-permute-start | bytes 2359304 | tf_op jit(solution)/shard_map/ppermute | solution.py:28
  55.1 2.3 %fusion.32 = bf16[256,256]{1,0:T(8,128)(2,1)S(1)} fusion(s32[]{:T(128)S(6)} %axis_index.15, s32[256]{0:T(256)S(1)} %get-tuple-element.53, s32[256]{0:T(256)} %get-tuple-element.60, s32[256]{0:T(256)S(1)} %get-tuple-element.54, s32[256]{0:T(256)} %get-tuple-element.61, s32[256]{0:T(256)S(1)} %get-tuple-element.55, s32[256]{0:T(256)} %get-tuple-element.62, ...), kind=kLoop, calls=%fused_computation.69 | loop fusion | flops 5767168 | bytes 147204 | tf_op jit(solution)/shard_map/convert_element_type | solution.py:46
  57.5 3.0 %collective-permute-start.2 = (bf16[64,6144]{1,0:T(8,128)(2,1)S(1)}, bf16[64,6144]{1,0:T(8,128)(2,1)S(1)}, u32[]{:S(2)}, u32[]{:S(2)}) collective-permute-start(bf16[64,6144]{1,0:T(8,128)(2,1)S(1)} %collective-permute-done), channel_id=1, source_target_pairs={{0,1},{1,0},{2,3},{3,2},{4,5},{5,4},{6,7},{7,6},{8,9},{9,8},{10,11... | collective-permute-start | bytes 2359304 | tf_op jit(solution)/shard_map/ppermute | solution.py:28
  60.6 1.8 %collective-permute-done.2 = bf16[64,6144]{1,0:T(8,128)(2,1)S(1)} collective-permute-done((bf16[64,6144]{1,0:T(8,128)(2,1)S(1)}, bf16[64,6144]{1,0:T(8,128)(2,1)S(1)}, u32[]{:S(2)}, u32[]{:S(2)}) %collective-permute-start.2) | collective-permute-done | bytes 786464 | tf_op jit(solution)/shard_map/ppermute | solution.py:28
  65.9 2.3 %collective-permute-start.3 = (bf16[128,3072]{1,0:T(8,128)(2,1)}, bf16[128,3072]{1,0:T(8,128)(2,1)}, u32[]{:S(2)}, u32[]{:S(2)}) collective-permute-start(bf16[128,3072]{1,0:T(8,128)(2,1)} %convolution_convert_fusion.2), channel_id=1, source_target_pairs={{0,1},{1,0},{2,3},{3,2},{4,5},{5,4},{6,7},{7,6},{8,9},{9,8},{10,11... | collective-permute-start | bytes 2359304 | tf_op jit(solution)/shard_map/ppermute | solution.py:28
  70.7 6.6 %all-to-all-start = ((bf16[8,48,3072]{2,1,0:T(8,128)(2,1)}), bf16[8,48,3072]{2,1,0:T(8,128)(2,1)S(1)}, u32[]{:S(2)}, u32[]{:S(2)}) async-start(bf16[8,48,3072]{2,1,0:T(8,128)(2,1)} %bitcast.15), calls=%async_computation | async-start | bytes 4718592 | tf_op jit(solution)/shard_map/all_to_all | solution.py:123
  79.0 1.9 %collective-permute-start.4 = (bf16[32,3072]{1,0:T(8,128)(2,1)S(1)}, bf16[32,3072]{1,0:T(8,128)(2,1)S(1)}, u32[]{:S(2)}, u32[]{:S(2)}) collective-permute-start(bf16[32,3072]{1,0:T(8,128)(2,1)S(1)} %get-tuple-element.37), channel_id=1, source_target_pairs={{0,2},{2,0},{4,6},{6,4},{8,10},{10,8},{12,14},{14,12},{16,18},{18,... | collective-permute-start | bytes 589832 | tf_op jit(solution)/shard_map/ppermute | solution.py:28
  81.0 1.9 %collective-permute-start.5 = (bf16[32,3072]{1,0:T(8,128)(2,1)S(1)}, bf16[32,3072]{1,0:T(8,128)(2,1)S(1)}, u32[]{:S(2)}, u32[]{:S(2)}) collective-permute-start(bf16[32,3072]{1,0:T(8,128)(2,1)S(1)} %get-tuple-element.39), channel_id=1, source_target_pairs={{0,4},{2,6},{4,0},{6,2},{8,12},{10,14},{12,8},{14,10},{16,20},{18,... | collective-permute-start | bytes 589832 | tf_op jit(solution)/shard_map/ppermute | solution.py:28
  82.9 5.4 %collective-permute-start.6 = (bf16[32,3072]{1,0:T(8,128)(2,1)S(1)}, bf16[32,3072]{1,0:T(8,128)(2,1)S(1)}, u32[]{:S(2)}, u32[]{:S(2)}) collective-permute-start(bf16[32,3072]{1,0:T(8,128)(2,1)S(1)} %get-tuple-element.38), channel_id=1, source_target_pairs={{0,6},{2,4},{4,2},{6,0},{8,14},{10,12},{12,10},{14,8},{16,22},{18,... | collective-permute-start | bytes 589832 | tf_op jit(solution)/shard_map/ppermute | solution.py:28
  88.3 9.9 %collective-permute-done.5 = bf16[32,3072]{1,0:T(8,128)(2,1)S(1)} collective-permute-done((bf16[32,3072]{1,0:T(8,128)(2,1)S(1)}, bf16[32,3072]{1,0:T(8,128)(2,1)S(1)}, u32[]{:S(2)}, u32[]{:S(2)}) %collective-permute-start.5) | collective-permute-done | bytes 196640 | tf_op jit(solution)/shard_map/ppermute | solution.py:28
  98.4 2.4 %collective-permute-start.7 = (bf16[16,3072]{1,0:T(8,128)(2,1)S(1)}, bf16[16,3072]{1,0:T(8,128)(2,1)S(1)}, u32[]{:S(2)}, u32[]{:S(2)}) collective-permute-start(bf16[16,3072]{1,0:T(8,128)(2,1)S(1)} %slice.108), channel_id=1, source_target_pairs={{0,32},{32,0},{1,33},{33,1},{2,34},{34,2},{3,35},{35,3},{4,36},{36... | collective-permute-start | bytes 294920 | tf_op jit(solution)/shard_map/ppermute | solution.py:28
  100.7 7.9 %collective-permute-done.7 = bf16[16,3072]{1,0:T(8,128)(2,1)S(1)} collective-permute-done((bf16[16,3072]{1,0:T(8,128)(2,1)S(1)}, bf16[16,3072]{1,0:T(8,128)(2,1)S(1)}, u32[]{:S(2)}, u32[]{:S(2)}) %collective-permute-start.7) | collective-permute-done | bytes 98336 | tf_op jit(solution)/shard_map/ppermute | solution.py:28
  109.4 2.6 %all-to-all-done = bf16[8,48,3072]{2,1,0:T(8,128)(2,1)S(1)} async-done(((bf16[8,48,3072]{2,1,0:T(8,128)(2,1)}), bf16[8,48,3072]{2,1,0:T(8,128)(2,1)S(1)}, u32[]{:S(2)}, u32[]{:S(2)}) %all-to-all-start) | async-done | bytes 2359328 | tf_op jit(solution)/shard_map/all_to_all | solution.py:123
  112.4 1.7 %broadcast_in_dim.5 = bf16[8,48,3072]{2,1,0:T(8,128)(2,1)} broadcast(bf16[48,3072]{1,0:T(8,128)(2,1)S(1)} %multiply_convert_fusion), dimensions={1,2} | broadcast | bytes 2654208 | tf_op jit(solution)/shard_map/broadcast_in_dim | solution.py:136
  114.1 4.0 %all-to-all-start.1 = ((bf16[8,48,3072]{2,1,0:T(8,128)(2,1)}), bf16[8,48,3072]{2,1,0:T(8,128)(2,1)S(1)}, u32[]{:S(2)}, u32[]{:S(2)}) async-start(bf16[8,48,3072]{2,1,0:T(8,128)(2,1)} %broadcast_in_dim.5), calls=%async_computation.1 | async-start | bytes 4718592 | tf_op jit(solution)/shard_map/all_to_all | solution.py:139
  119.0 5.2 %collective-permute-start.10 = (bf16[4,3072]{1,0:T(4,128)(2,1)S(1)}, bf16[4,3072]{1,0:T(4,128)(2,1)}, u32[]{:S(2)}, u32[]{:S(2)}) collective-permute-start(bf16[4,3072]{1,0:T(4,128)(2,1)S(1)} %get-tuple-element.40), channel_id=1, source_target_pairs={{0,24},{2,26},{4,28},{6,30},{8,16},{10,18},{12,20},{14,22},{16,8},... | collective-permute-start | bytes 73736 | tf_op jit(solution)/shard_map/ppermute | solution.py:28
  124.2 3.7 %collective-permute-start.8 = (bf16[4,3072]{1,0:T(4,128)(2,1)S(1)}, bf16[4,3072]{1,0:T(4,128)(2,1)S(1)}, u32[]{:S(2)}, u32[]{:S(2)}) collective-permute-start(bf16[4,3072]{1,0:T(4,128)(2,1)S(1)} %get-tuple-element.42), channel_id=1, source_target_pairs={{0,8},{2,10},{4,12},{6,14},{8,0},{10,2},{12,4},{14,6},{16,24},{18,... | collective-permute-start | bytes 73736 | tf_op jit(solution)/shard_map/ppermute | solution.py:28
  127.9 7.3 %collective-permute-start.9 = (bf16[4,3072]{1,0:T(4,128)(2,1)S(1)}, bf16[4,3072]{1,0:T(4,128)(2,1)S(1)}, u32[]{:S(2)}, u32[]{:S(2)}) collective-permute-start(bf16[4,3072]{1,0:T(4,128)(2,1)S(1)} %get-tuple-element.41), channel_id=1, source_target_pairs={{0,16},{2,18},{4,20},{6,22},{8,24},{10,26},{12,28},{14,30},{16,0},... | collective-permute-start | bytes 73736 | tf_op jit(solution)/shard_map/ppermute | solution.py:28
  136.8 4.5 %collective-permute-done.9.rest_1_ = bf16[4,3072]{1,0:T(4,128)(2,1)S(1)} collective-permute-done((bf16[4,3072]{1,0:T(4,128)(2,1)S(1)}, bf16[4,3072]{1,0:T(4,128)(2,1)S(1)}, u32[]{:S(2)}, u32[]{:S(2)}) %collective-permute-start.9) | collective-permute-done | bytes 24608 | tf_op jit(solution)/shard_map/ppermute | solution.py:28
  143.5 8.1 %all-to-all-done.1 = bf16[8,48,3072]{2,1,0:T(8,128)(2,1)S(1)} async-done(((bf16[8,48,3072]{2,1,0:T(8,128)(2,1)}), bf16[8,48,3072]{2,1,0:T(8,128)(2,1)S(1)}, u32[]{:S(2)}, u32[]{:S(2)}) %all-to-all-start.1) | async-done | bytes 2359328 | tf_op jit(solution)/shard_map/all_to_all | solution.py:139
  151.5 1.6 %fusion.45 = (bf16[4,48,3072]{2,1,0:T(8,128)(2,1)}, bf16[4,48,3072]{2,1,0:T(8,128)(2,1)}) fusion(bf16[8,48,3072]{2,1,0:T(8,128)(2,1)S(1)} %all-to-all-done.1), kind=kLoop, calls=%fused_computation.116 | loop fusion | bytes 4718592 | tf_op jit(solution)/shard_map/slice | solution.py:145
  (51 shorter events, 19.1 us)
Async XLA Ops:
  0.6 61.8 %copy-start = (bf16[3072,192]{0,1:T(8,128)(2,1)S(1)}, bf16[3072,192]{0,1:T(8,128)(2,1)}, u32[]{:S(2)}) copy-start(bf16[3072,192]{0,1:T(8,128)(2,1)} %param.7) | copy-start | bytes 3538948
  36.7 20.7 %collective-permute-start = (bf16[64,6144]{1,0:T(8,128)(2,1)S(1)}, bf16[64,6144]{1,0:T(8,128)(2,1)S(1)}, u32[]{:S(2)}, u32[]{:S(2)}) collective-permute-start(bf16[64,6144]{1,0:T(8,128)(2,1)S(1)} %reshape.20), channel_id=1, source_target_pairs={{0,32},{32,0},{1,33},{33,1},{2,34},{34,2},{3,35},{35,3},{4,36},{36... | collective-permute-start | bytes 2359304 | tf_op jit(solution)/shard_map/ppermute | solution.py:28
  39.9 17.5 %collective-permute-start.1 = (bf16[64,6144]{1,0:T(8,128)(2,1)S(1)}, bf16[64,6144]{1,0:T(8,128)(2,1)S(1)}, u32[]{:S(2)}, u32[]{:S(2)}) collective-permute-start(bf16[64,6144]{1,0:T(8,128)(2,1)S(1)} %reshape.20), channel_id=1, source_target_pairs={{0,1},{1,0},{2,3},{3,2},{4,5},{5,4},{6,7},{7,6},{8,9},{9,8},{10,11... | collective-permute-start | bytes 2359304 | tf_op jit(solution)/shard_map/ppermute | solution.py:28
  57.5 4.9 %collective-permute-start.2 = (bf16[64,6144]{1,0:T(8,128)(2,1)S(1)}, bf16[64,6144]{1,0:T(8,128)(2,1)S(1)}, u32[]{:S(2)}, u32[]{:S(2)}) collective-permute-start(bf16[64,6144]{1,0:T(8,128)(2,1)S(1)} %collective-permute-done), channel_id=1, source_target_pairs={{0,1},{1,0},{2,3},{3,2},{4,5},{5,4},{6,7},{7,6},{8,9},{9,8},{10,11... | collective-permute-start | bytes 2359304 | tf_op jit(solution)/shard_map/ppermute | solution.py:28
  62.5 1.3 copy-start.4
  64.6 1.3 copy-start.1
  65.9 11.5 %collective-permute-start.3 = (bf16[128,3072]{1,0:T(8,128)(2,1)}, bf16[128,3072]{1,0:T(8,128)(2,1)}, u32[]{:S(2)}, u32[]{:S(2)}) collective-permute-start(bf16[128,3072]{1,0:T(8,128)(2,1)} %convolution_convert_fusion.2), channel_id=1, source_target_pairs={{0,1},{1,0},{2,3},{3,2},{4,5},{5,4},{6,7},{7,6},{8,9},{9,8},{10,11... | collective-permute-start | bytes 2359304 | tf_op jit(solution)/shard_map/ppermute | solution.py:28
  70.7 41.3 %all-to-all-start = ((bf16[8,48,3072]{2,1,0:T(8,128)(2,1)}), bf16[8,48,3072]{2,1,0:T(8,128)(2,1)S(1)}, u32[]{:S(2)}, u32[]{:S(2)}) async-start(bf16[8,48,3072]{2,1,0:T(8,128)(2,1)} %bitcast.15), calls=%async_computation | async-start | bytes 4718592 | tf_op jit(solution)/shard_map/all_to_all | solution.py:123
  79.0 9.3 %collective-permute-start.4 = (bf16[32,3072]{1,0:T(8,128)(2,1)S(1)}, bf16[32,3072]{1,0:T(8,128)(2,1)S(1)}, u32[]{:S(2)}, u32[]{:S(2)}) collective-permute-start(bf16[32,3072]{1,0:T(8,128)(2,1)S(1)} %get-tuple-element.37), channel_id=1, source_target_pairs={{0,2},{2,0},{4,6},{6,4},{8,10},{10,8},{12,14},{14,12},{16,18},{18,... | collective-permute-start | bytes 589832 | tf_op jit(solution)/shard_map/ppermute | solution.py:28
  81.0 17.3 %collective-permute-start.5 = (bf16[32,3072]{1,0:T(8,128)(2,1)S(1)}, bf16[32,3072]{1,0:T(8,128)(2,1)S(1)}, u32[]{:S(2)}, u32[]{:S(2)}) collective-permute-start(bf16[32,3072]{1,0:T(8,128)(2,1)S(1)} %get-tuple-element.39), channel_id=1, source_target_pairs={{0,4},{2,6},{4,0},{6,2},{8,12},{10,14},{12,8},{14,10},{16,20},{18,... | collective-permute-start | bytes 589832 | tf_op jit(solution)/shard_map/ppermute | solution.py:28
  82.9 15.4 %collective-permute-start.6 = (bf16[32,3072]{1,0:T(8,128)(2,1)S(1)}, bf16[32,3072]{1,0:T(8,128)(2,1)S(1)}, u32[]{:S(2)}, u32[]{:S(2)}) collective-permute-start(bf16[32,3072]{1,0:T(8,128)(2,1)S(1)} %get-tuple-element.38), channel_id=1, source_target_pairs={{0,6},{2,4},{4,2},{6,0},{8,14},{10,12},{12,10},{14,8},{16,22},{18,... | collective-permute-start | bytes 589832 | tf_op jit(solution)/shard_map/ppermute | solution.py:28
  98.4 10.3 %collective-permute-start.7 = (bf16[16,3072]{1,0:T(8,128)(2,1)S(1)}, bf16[16,3072]{1,0:T(8,128)(2,1)S(1)}, u32[]{:S(2)}, u32[]{:S(2)}) collective-permute-start(bf16[16,3072]{1,0:T(8,128)(2,1)S(1)} %slice.108), channel_id=1, source_target_pairs={{0,32},{32,0},{1,33},{33,1},{2,34},{34,2},{3,35},{35,3},{4,36},{36... | collective-permute-start | bytes 294920 | tf_op jit(solution)/shard_map/ppermute | solution.py:28
  114.1 37.5 %all-to-all-start.1 = ((bf16[8,48,3072]{2,1,0:T(8,128)(2,1)}), bf16[8,48,3072]{2,1,0:T(8,128)(2,1)S(1)}, u32[]{:S(2)}, u32[]{:S(2)}) async-start(bf16[8,48,3072]{2,1,0:T(8,128)(2,1)} %broadcast_in_dim.5), calls=%async_computation.1 | async-start | bytes 4718592 | tf_op jit(solution)/shard_map/all_to_all | solution.py:139
  119.0 17.7 %collective-permute-start.10 = (bf16[4,3072]{1,0:T(4,128)(2,1)S(1)}, bf16[4,3072]{1,0:T(4,128)(2,1)}, u32[]{:S(2)}, u32[]{:S(2)}) collective-permute-start(bf16[4,3072]{1,0:T(4,128)(2,1)S(1)} %get-tuple-element.40), channel_id=1, source_target_pairs={{0,24},{2,26},{4,28},{6,30},{8,16},{10,18},{12,20},{14,22},{16,8},... | collective-permute-start | bytes 73736 | tf_op jit(solution)/shard_map/ppermute | solution.py:28
  124.2 12.5 %collective-permute-start.8 = (bf16[4,3072]{1,0:T(4,128)(2,1)S(1)}, bf16[4,3072]{1,0:T(4,128)(2,1)S(1)}, u32[]{:S(2)}, u32[]{:S(2)}) collective-permute-start(bf16[4,3072]{1,0:T(4,128)(2,1)S(1)} %get-tuple-element.42), channel_id=1, source_target_pairs={{0,8},{2,10},{4,12},{6,14},{8,0},{10,2},{12,4},{14,6},{16,24},{18,... | collective-permute-start | bytes 73736 | tf_op jit(solution)/shard_map/ppermute | solution.py:28
  127.9 13.3 %collective-permute-start.9 = (bf16[4,3072]{1,0:T(4,128)(2,1)S(1)}, bf16[4,3072]{1,0:T(4,128)(2,1)S(1)}, u32[]{:S(2)}, u32[]{:S(2)}) collective-permute-start(bf16[4,3072]{1,0:T(4,128)(2,1)S(1)} %get-tuple-element.41), channel_id=1, source_target_pairs={{0,16},{2,18},{4,20},{6,22},{8,24},{10,26},{12,28},{14,30},{16,0},... | collective-permute-start | bytes 73736 | tf_op jit(solution)/shard_map/ppermute | solution.py:28
  136.8 4.5 %copy-start.2 = (bf16[4,3072]{1,0:T(4,128)(2,1)}, bf16[4,3072]{1,0:T(4,128)(2,1)S(1)}, u32[]{:S(2)}) copy-start(bf16[4,3072]{1,0:T(4,128)(2,1)S(1)} %collective-permute-done.8.rest_0_) | copy-start | bytes 73732
  141.2 0.6 copy-start.3

commit v9 on v8

--- a/solution.py
+++ b/solution.py
@@ -28,6 +28,10 @@
     return lax.ppermute(rows, axis, [(at, at ^ step) for at in range(lax.axis_size(axis))])
 
 
+def mixed_rings(n_z):
+    return [[2 * z + (z % 2 ^ core) for z in range(n_z)] for core in range(2)]
+
+
 def stage_order(rows, n_z, zero):
     at = lax.broadcasted_iota(jnp.int32, (4 * n_z * rows, 4 * n_z * rows), 0) + zero
     column = lax.broadcasted_iota(jnp.int32, at.shape, 1)
@@ -40,8 +44,11 @@
             bit = (at // block) % 2
             if axis == "z":
                 far = far + bit * step
+            elif axis == "yl":
+                old = old + bit * (n_z * rows)
             else:
-                old = old + bit * (n_z * rows * (2 if axis == "core" else 1))
+                other = bit
+    old = old + (other ^ far % 2) * (2 * n_z * rows)
     old = old + (far ^ lax.axis_index("z")) * rows
     return (old == column).astype(jnp.bfloat16)
 
@@ -91,7 +98,7 @@
     n_z = lax.axis_size("z")
     joined, normal, inverse = join_normed(inputs, gain, cotangent)
 
-    both = lax.all_gather(joined, "z", axis=0, tiled=True)
+    both = lax.all_gather(joined, ("z", "core"), axis_index_groups=mixed_rings(n_z), axis=0, tiled=True)
     both, zero = lax.optimization_barrier((both, jnp.int32(0)))
     order = stage_order(rows, n_z, zero)
     beside = swap(both, "yl", 1)

time: 154 us -> 158 us (1.026)
  waiting for transfers between devices: 34.8 us -> 42.7 us
  starting transfers between devices: 56.8 us -> 49 us
  blocking collectives: 34.2 us -> 38.7 us
    ppermute x11, waiting for transfers between devices: 24.1 us -> 32.2 us  [swap(): lax.ppermute(rows, axis, [(at, at ^ step) for at in range(lax.axis_size(a...]
    ppermute x11, starting transfers between devices: 46.2 us -> 38.4 us  [swap(): lax.ppermute(rows, axis, [(at, at ^ step) for at in range(lax.axis_size(a...]
    all_gather x1, blocking collectives: 34.2 us -> 38.7 us  [body(): lax.all_gather(joined, ('z', 'core'), axis_index_groups=mixed_rings(n_z),...]
  transfers between devices with their start and end apart: 13 -> 13, of which waited for: 6 -> 7; matrix products, arithmetic and copies ran while one was open for 10% -> 10% of each run, Pallas kernels for 1% -> 1%
where the time goes in v9:
time: 158 us
  starting transfers between devices  49 us (31%)
  waiting for transfers between devices  42.7 us (27%)
  blocking collectives  38.7 us (24%)
  other arithmetic  11.2 us (7%)
  local copies, waits for them, and re-layouts  6.5 us (4%)
  matrix products  5.44 us (3%)
  Pallas kernels  3.34 us (2%)
    all_gather x1, blocking collectives, body(): lax.all_gather(joined, ('z', 'core'), axis_index_groups=mixed_rings(n_z),...  38.7 us
    ppermute x11, starting transfers between devices, swap(): lax.ppermute(rows, axis, [(at, at ^ step) for at in range(lax.axis_size(a...  38.4 us
    ppermute x11, waiting for transfers between devices, swap(): lax.ppermute(rows, axis, [(at, at ^ step) for at in range(lax.axis_size(a...  32.2 us
    all_to_all x1, waiting for transfers between devices, body(): spread = lax.all_to_all(spread, DP, 0, 0, tiled=True)  7.88 us
    all_to_all x1, starting transfers between devices, body(): parts = lax.all_to_all(parts, DP, 0, 0, tiled=True)  6.62 us
    all_to_all x1, starting transfers between devices, body(): spread = lax.all_to_all(spread, DP, 0, 0, tiled=True)  3.93 us
  transfers between devices with their start and end apart: 13, of which 7 were waited for; matrix products, arithmetic and copies ran while one was open for 10% of the time, Pallas kernels for 1%

profile of v9, /device:TPU:1, one launch (start us, length us, event | category | flops | bytes accessed | tf_op | source)
XLA Modules:
  0.0 157.6 jit_solution(18372949941637549868)
XLA Ops:
  0.6 1.7 %norm.1 = (bf16[4,6144]{1,0:T(4,128)(2,1)}, f32[4,3072]{1,0:T(4,128)}, f32[4,128]{1,0:T(4,128)}) custom-call(bf16[4,3072]{1,0:T(4,128)(2,1)} %inputs.1, f32[1,3072]{1,0:T(1,128)} %bitcast.18, bf16[4,3072]{1,0:T(4,128)(2,1)} %cotangent.3), custom_call_target="tpu_custom_call" | custom-call | tf_op jit(solution)/shard_map/norm/pallas_call | solution.py:71
  2.4 38.7 %all-gather = bf16[16,4,6144]{2,1,0:T(4,128)(2,1)S(1)} all-gather(bf16[1,4,6144]{2,1,0:T(4,128)(2,1)} %bitcast.20), channel_id=1, replica_groups={{0,3,4,7,8,11,12,15,16,19,20,23,24,27,28,31},{1,2,5,6,9,10,13,14,17,18,..., dimensions={0}, use_global_device_ids=true | all-gather | bytes 835584 | tf_op jit(solution)/shard_map/all_gather | solution.py:101
  41.2 3.2 %collective-permute-start = (bf16[64,6144]{1,0:T(8,128)(2,1)S(1)}, bf16[64,6144]{1,0:T(8,128)(2,1)S(1)}, u32[]{:S(2)}, u32[]{:S(2)}) collective-permute-start(bf16[64,6144]{1,0:T(8,128)(2,1)S(1)} %reshape.20), channel_id=1, source_target_pairs={{0,32},{32,0},{1,33},{33,1},{2,34},{34,2},{3,35},{35,3},{4,36},{36... | collective-permute-start | bytes 2359304 | tf_op jit(solution)/shard_map/ppermute | solution.py:28
  44.4 2.3 %collective-permute-start.1 = (bf16[64,6144]{1,0:T(8,128)(2,1)S(1)}, bf16[64,6144]{1,0:T(8,128)(2,1)S(1)}, u32[]{:S(2)}, u32[]{:S(2)}) collective-permute-start(bf16[64,6144]{1,0:T(8,128)(2,1)S(1)} %reshape.20), channel_id=1, source_target_pairs={{0,1},{1,0},{2,3},{3,2},{4,5},{5,4},{6,7},{7,6},{8,9},{9,8},{10,11... | collective-permute-start | bytes 2359304 | tf_op jit(solution)/shard_map/ppermute | solution.py:28
  52.0 2.3 %fusion.33 = bf16[256,256]{1,0:T(8,128)(2,1)S(1)} fusion(s32[]{:T(128)S(6)} %axis_index.15, s32[256]{0:T(256)S(1)} %get-tuple-element.53, s32[256]{0:T(256)} %get-tuple-element.60, s32[256]{0:T(256)S(1)} %get-tuple-element.54, s32[256]{0:T(256)} %get-tuple-element.61, s32[256]{0:T(256)S(1)} %get-tuple-element.55, s32[256]{0:T(256)} %get-tuple-element.62, ...), kind=kLoop, calls=%fused_computation.73 | loop fusion | flops 6553600 | bytes 147204 | tf_op jit(solution)/shard_map/convert_element_type | solution.py:53
  54.4 7.8 %collective-permute-done = bf16[64,6144]{1,0:T(8,128)(2,1)S(1)} collective-permute-done((bf16[64,6144]{1,0:T(8,128)(2,1)S(1)}, bf16[64,6144]{1,0:T(8,128)(2,1)S(1)}, u32[]{:S(2)}, u32[]{:S(2)}) %collective-permute-start) | collective-permute-done | bytes 786464 | tf_op jit(solution)/shard_map/ppermute | solution.py:28
  62.1 2.8 %collective-permute-start.2 = (bf16[64,6144]{1,0:T(8,128)(2,1)S(1)}, bf16[64,6144]{1,0:T(8,128)(2,1)S(1)}, u32[]{:S(2)}, u32[]{:S(2)}) collective-permute-start(bf16[64,6144]{1,0:T(8,128)(2,1)S(1)} %collective-permute-done), channel_id=1, source_target_pairs={{0,1},{1,0},{2,3},{3,2},{4,5},{5,4},{6,7},{7,6},{8,9},{9,8},{10,11... | collective-permute-start | bytes 2359304 | tf_op jit(solution)/shard_map/ppermute | solution.py:28
  65.1 1.8 %collective-permute-done.2 = bf16[64,6144]{1,0:T(8,128)(2,1)S(1)} collective-permute-done((bf16[64,6144]{1,0:T(8,128)(2,1)S(1)}, bf16[64,6144]{1,0:T(8,128)(2,1)S(1)}, u32[]{:S(2)}, u32[]{:S(2)}) %collective-permute-start.2) | collective-permute-done | bytes 786464 | tf_op jit(solution)/shard_map/ppermute | solution.py:28
  70.4 2.3 %collective-permute-start.3 = (bf16[128,3072]{1,0:T(8,128)(2,1)}, bf16[128,3072]{1,0:T(8,128)(2,1)}, u32[]{:S(2)}, u32[]{:S(2)}) collective-permute-start(bf16[128,3072]{1,0:T(8,128)(2,1)} %convolution_convert_fusion.2), channel_id=1, source_target_pairs={{0,1},{1,0},{2,3},{3,2},{4,5},{5,4},{6,7},{7,6},{8,9},{9,8},{10,11... | collective-permute-start | bytes 2359304 | tf_op jit(solution)/shard_map/ppermute | solution.py:28
  75.3 6.6 %all-to-all-start = ((bf16[8,48,3072]{2,1,0:T(8,128)(2,1)}), bf16[8,48,3072]{2,1,0:T(8,128)(2,1)S(1)}, u32[]{:S(2)}, u32[]{:S(2)}) async-start(bf16[8,48,3072]{2,1,0:T(8,128)(2,1)} %bitcast.15), calls=%async_computation | async-start | bytes 4718592 | tf_op jit(solution)/shard_map/all_to_all | solution.py:130
  83.5 1.9 %collective-permute-start.4 = (bf16[32,3072]{1,0:T(8,128)(2,1)S(1)}, bf16[32,3072]{1,0:T(8,128)(2,1)S(1)}, u32[]{:S(2)}, u32[]{:S(2)}) collective-permute-start(bf16[32,3072]{1,0:T(8,128)(2,1)S(1)} %get-tuple-element.37), channel_id=1, source_target_pairs={{0,2},{2,0},{4,6},{6,4},{8,10},{10,8},{12,14},{14,12},{16,18},{18,... | collective-permute-start | bytes 589832 | tf_op jit(solution)/shard_map/ppermute | solution.py:28
  85.5 1.9 %collective-permute-start.5 = (bf16[32,3072]{1,0:T(8,128)(2,1)S(1)}, bf16[32,3072]{1,0:T(8,128)(2,1)S(1)}, u32[]{:S(2)}, u32[]{:S(2)}) collective-permute-start(bf16[32,3072]{1,0:T(8,128)(2,1)S(1)} %get-tuple-element.39), channel_id=1, source_target_pairs={{0,4},{2,6},{4,0},{6,2},{8,12},{10,14},{12,8},{14,10},{16,20},{18,... | collective-permute-start | bytes 589832 | tf_op jit(solution)/shard_map/ppermute | solution.py:28
  87.4 5.4 %collective-permute-start.6 = (bf16[32,3072]{1,0:T(8,128)(2,1)S(1)}, bf16[32,3072]{1,0:T(8,128)(2,1)S(1)}, u32[]{:S(2)}, u32[]{:S(2)}) collective-permute-start(bf16[32,3072]{1,0:T(8,128)(2,1)S(1)} %get-tuple-element.38), channel_id=1, source_target_pairs={{0,6},{2,4},{4,2},{6,0},{8,14},{10,12},{12,10},{14,8},{16,22},{18,... | collective-permute-start | bytes 589832 | tf_op jit(solution)/shard_map/ppermute | solution.py:28
  92.8 9.9 %collective-permute-done.5 = bf16[32,3072]{1,0:T(8,128)(2,1)S(1)} collective-permute-done((bf16[32,3072]{1,0:T(8,128)(2,1)S(1)}, bf16[32,3072]{1,0:T(8,128)(2,1)S(1)}, u32[]{:S(2)}, u32[]{:S(2)}) %collective-permute-start.5) | collective-permute-done | bytes 196640 | tf_op jit(solution)/shard_map/ppermute | solution.py:28
  102.9 2.3 %collective-permute-start.7 = (bf16[16,3072]{1,0:T(8,128)(2,1)S(1)}, bf16[16,3072]{1,0:T(8,128)(2,1)S(1)}, u32[]{:S(2)}, u32[]{:S(2)}) collective-permute-start(bf16[16,3072]{1,0:T(8,128)(2,1)S(1)} %slice.108), channel_id=1, source_target_pairs={{0,32},{32,0},{1,33},{33,1},{2,34},{34,2},{3,35},{35,3},{4,36},{36... | collective-permute-start | bytes 294920 | tf_op jit(solution)/shard_map/ppermute | solution.py:28
  105.2 8.0 %collective-permute-done.7 = bf16[16,3072]{1,0:T(8,128)(2,1)S(1)} collective-permute-done((bf16[16,3072]{1,0:T(8,128)(2,1)S(1)}, bf16[16,3072]{1,0:T(8,128)(2,1)S(1)}, u32[]{:S(2)}, u32[]{:S(2)}) %collective-permute-start.7) | collective-permute-done | bytes 98336 | tf_op jit(solution)/shard_map/ppermute | solution.py:28
  113.9 2.6 %all-to-all-done = bf16[8,48,3072]{2,1,0:T(8,128)(2,1)S(1)} async-done(((bf16[8,48,3072]{2,1,0:T(8,128)(2,1)}), bf16[8,48,3072]{2,1,0:T(8,128)(2,1)S(1)}, u32[]{:S(2)}, u32[]{:S(2)}) %all-to-all-start) | async-done | bytes 2359328 | tf_op jit(solution)/shard_map/all_to_all | solution.py:130
  116.9 1.7 %broadcast_in_dim.5 = bf16[8,48,3072]{2,1,0:T(8,128)(2,1)} broadcast(bf16[48,3072]{1,0:T(8,128)(2,1)S(1)} %multiply_convert_fusion), dimensions={1,2} | broadcast | bytes 2654208 | tf_op jit(solution)/shard_map/broadcast_in_dim | solution.py:143
  118.6 3.9 %all-to-all-start.1 = ((bf16[8,48,3072]{2,1,0:T(8,128)(2,1)}), bf16[8,48,3072]{2,1,0:T(8,128)(2,1)S(1)}, u32[]{:S(2)}, u32[]{:S(2)}) async-start(bf16[8,48,3072]{2,1,0:T(8,128)(2,1)} %broadcast_in_dim.5), calls=%async_computation.1 | async-start | bytes 4718592 | tf_op jit(solution)/shard_map/all_to_all | solution.py:146
  123.5 5.2 %collective-permute-start.10 = (bf16[4,3072]{1,0:T(4,128)(2,1)S(1)}, bf16[4,3072]{1,0:T(4,128)(2,1)}, u32[]{:S(2)}, u32[]{:S(2)}) collective-permute-start(bf16[4,3072]{1,0:T(4,128)(2,1)S(1)} %get-tuple-element.40), channel_id=1, source_target_pairs={{0,24},{2,26},{4,28},{6,30},{8,16},{10,18},{12,20},{14,22},{16,8},... | collective-permute-start | bytes 73736 | tf_op jit(solution)/shard_map/ppermute | solution.py:28
  128.7 3.9 %collective-permute-start.8 = (bf16[4,3072]{1,0:T(4,128)(2,1)S(1)}, bf16[4,3072]{1,0:T(4,128)(2,1)S(1)}, u32[]{:S(2)}, u32[]{:S(2)}) collective-permute-start(bf16[4,3072]{1,0:T(4,128)(2,1)S(1)} %get-tuple-element.42), channel_id=1, source_target_pairs={{0,8},{2,10},{4,12},{6,14},{8,0},{10,2},{12,4},{14,6},{16,24},{18,... | collective-permute-start | bytes 73736 | tf_op jit(solution)/shard_map/ppermute | solution.py:28
  132.6 7.1 %collective-permute-start.9 = (bf16[4,3072]{1,0:T(4,128)(2,1)S(1)}, bf16[4,3072]{1,0:T(4,128)(2,1)S(1)}, u32[]{:S(2)}, u32[]{:S(2)}) collective-permute-start(bf16[4,3072]{1,0:T(4,128)(2,1)S(1)} %get-tuple-element.41), channel_id=1, source_target_pairs={{0,16},{2,18},{4,20},{6,22},{8,24},{10,26},{12,28},{14,30},{16,0},... | collective-permute-start | bytes 73736 | tf_op jit(solution)/shard_map/ppermute | solution.py:28
  141.2 4.7 %collective-permute-done.9.rest_1_ = bf16[4,3072]{1,0:T(4,128)(2,1)S(1)} collective-permute-done((bf16[4,3072]{1,0:T(4,128)(2,1)S(1)}, bf16[4,3072]{1,0:T(4,128)(2,1)S(1)}, u32[]{:S(2)}, u32[]{:S(2)}) %collective-permute-start.9) | collective-permute-done | bytes 24608 | tf_op jit(solution)/shard_map/ppermute | solution.py:28
  148.1 7.9 %all-to-all-done.1 = bf16[8,48,3072]{2,1,0:T(8,128)(2,1)S(1)} async-done(((bf16[8,48,3072]{2,1,0:T(8,128)(2,1)}), bf16[8,48,3072]{2,1,0:T(8,128)(2,1)S(1)}, u32[]{:S(2)}, u32[]{:S(2)}) %all-to-all-start.1) | async-done | bytes 2359328 | tf_op jit(solution)/shard_map/all_to_all | solution.py:146
  (51 shorter events, 20.8 us)
Async XLA Ops:
  0.6 66.3 %copy-start = (bf16[3072,192]{0,1:T(8,128)(2,1)S(1)}, bf16[3072,192]{0,1:T(8,128)(2,1)}, u32[]{:S(2)}) copy-start(bf16[3072,192]{0,1:T(8,128)(2,1)} %param.7) | copy-start | bytes 3538948
  41.2 20.9 %collective-permute-start = (bf16[64,6144]{1,0:T(8,128)(2,1)S(1)}, bf16[64,6144]{1,0:T(8,128)(2,1)S(1)}, u32[]{:S(2)}, u32[]{:S(2)}) collective-permute-start(bf16[64,6144]{1,0:T(8,128)(2,1)S(1)} %reshape.20), channel_id=1, source_target_pairs={{0,32},{32,0},{1,33},{33,1},{2,34},{34,2},{3,35},{35,3},{4,36},{36... | collective-permute-start | bytes 2359304 | tf_op jit(solution)/shard_map/ppermute | solution.py:28
  44.4 17.7 %collective-permute-start.1 = (bf16[64,6144]{1,0:T(8,128)(2,1)S(1)}, bf16[64,6144]{1,0:T(8,128)(2,1)S(1)}, u32[]{:S(2)}, u32[]{:S(2)}) collective-permute-start(bf16[64,6144]{1,0:T(8,128)(2,1)S(1)} %reshape.20), channel_id=1, source_target_pairs={{0,1},{1,0},{2,3},{3,2},{4,5},{5,4},{6,7},{7,6},{8,9},{9,8},{10,11... | collective-permute-start | bytes 2359304 | tf_op jit(solution)/shard_map/ppermute | solution.py:28
  62.1 4.7 %collective-permute-start.2 = (bf16[64,6144]{1,0:T(8,128)(2,1)S(1)}, bf16[64,6144]{1,0:T(8,128)(2,1)S(1)}, u32[]{:S(2)}, u32[]{:S(2)}) collective-permute-start(bf16[64,6144]{1,0:T(8,128)(2,1)S(1)} %collective-permute-done), channel_id=1, source_target_pairs={{0,1},{1,0},{2,3},{3,2},{4,5},{5,4},{6,7},{7,6},{8,9},{9,8},{10,11... | collective-permute-start | bytes 2359304 | tf_op jit(solution)/shard_map/ppermute | solution.py:28
  66.9 1.3 copy-start.4
  69.1 1.3 copy-start.1
  70.4 11.5 %collective-permute-start.3 = (bf16[128,3072]{1,0:T(8,128)(2,1)}, bf16[128,3072]{1,0:T(8,128)(2,1)}, u32[]{:S(2)}, u32[]{:S(2)}) collective-permute-start(bf16[128,3072]{1,0:T(8,128)(2,1)} %convolution_convert_fusion.2), channel_id=1, source_target_pairs={{0,1},{1,0},{2,3},{3,2},{4,5},{5,4},{6,7},{7,6},{8,9},{9,8},{10,11... | collective-permute-start | bytes 2359304 | tf_op jit(solution)/shard_map/ppermute | solution.py:28
  75.3 41.2 %all-to-all-start = ((bf16[8,48,3072]{2,1,0:T(8,128)(2,1)}), bf16[8,48,3072]{2,1,0:T(8,128)(2,1)S(1)}, u32[]{:S(2)}, u32[]{:S(2)}) async-start(bf16[8,48,3072]{2,1,0:T(8,128)(2,1)} %bitcast.15), calls=%async_computation | async-start | bytes 4718592 | tf_op jit(solution)/shard_map/all_to_all | solution.py:130
  83.5 9.3 %collective-permute-start.4 = (bf16[32,3072]{1,0:T(8,128)(2,1)S(1)}, bf16[32,3072]{1,0:T(8,128)(2,1)S(1)}, u32[]{:S(2)}, u32[]{:S(2)}) collective-permute-start(bf16[32,3072]{1,0:T(8,128)(2,1)S(1)} %get-tuple-element.37), channel_id=1, source_target_pairs={{0,2},{2,0},{4,6},{6,4},{8,10},{10,8},{12,14},{14,12},{16,18},{18,... | collective-permute-start | bytes 589832 | tf_op jit(solution)/shard_map/ppermute | solution.py:28
  85.5 17.3 %collective-permute-start.5 = (bf16[32,3072]{1,0:T(8,128)(2,1)S(1)}, bf16[32,3072]{1,0:T(8,128)(2,1)S(1)}, u32[]{:S(2)}, u32[]{:S(2)}) collective-permute-start(bf16[32,3072]{1,0:T(8,128)(2,1)S(1)} %get-tuple-element.39), channel_id=1, source_target_pairs={{0,4},{2,6},{4,0},{6,2},{8,12},{10,14},{12,8},{14,10},{16,20},{18,... | collective-permute-start | bytes 589832 | tf_op jit(solution)/shard_map/ppermute | solution.py:28
  87.4 15.4 %collective-permute-start.6 = (bf16[32,3072]{1,0:T(8,128)(2,1)S(1)}, bf16[32,3072]{1,0:T(8,128)(2,1)S(1)}, u32[]{:S(2)}, u32[]{:S(2)}) collective-permute-start(bf16[32,3072]{1,0:T(8,128)(2,1)S(1)} %get-tuple-element.38), channel_id=1, source_target_pairs={{0,6},{2,4},{4,2},{6,0},{8,14},{10,12},{12,10},{14,8},{16,22},{18,... | collective-permute-start | bytes 589832 | tf_op jit(solution)/shard_map/ppermute | solution.py:28
  102.9 10.3 %collective-permute-start.7 = (bf16[16,3072]{1,0:T(8,128)(2,1)S(1)}, bf16[16,3072]{1,0:T(8,128)(2,1)S(1)}, u32[]{:S(2)}, u32[]{:S(2)}) collective-permute-start(bf16[16,3072]{1,0:T(8,128)(2,1)S(1)} %slice.108), channel_id=1, source_target_pairs={{0,32},{32,0},{1,33},{33,1},{2,34},{34,2},{3,35},{35,3},{4,36},{36... | collective-permute-start | bytes 294920 | tf_op jit(solution)/shard_map/ppermute | solution.py:28
  118.6 37.4 %all-to-all-start.1 = ((bf16[8,48,3072]{2,1,0:T(8,128)(2,1)}), bf16[8,48,3072]{2,1,0:T(8,128)(2,1)S(1)}, u32[]{:S(2)}, u32[]{:S(2)}) async-start(bf16[8,48,3072]{2,1,0:T(8,128)(2,1)} %broadcast_in_dim.5), calls=%async_computation.1 | async-start | bytes 4718592 | tf_op jit(solution)/shard_map/all_to_all | solution.py:146
  123.5 17.7 %collective-permute-start.10 = (bf16[4,3072]{1,0:T(4,128)(2,1)S(1)}, bf16[4,3072]{1,0:T(4,128)(2,1)}, u32[]{:S(2)}, u32[]{:S(2)}) collective-permute-start(bf16[4,3072]{1,0:T(4,128)(2,1)S(1)} %get-tuple-element.40), channel_id=1, source_target_pairs={{0,24},{2,26},{4,28},{6,30},{8,16},{10,18},{12,20},{14,22},{16,8},... | collective-permute-start | bytes 73736 | tf_op jit(solution)/shard_map/ppermute | solution.py:28
  128.7 12.5 %collective-permute-start.8 = (bf16[4,3072]{1,0:T(4,128)(2,1)S(1)}, bf16[4,3072]{1,0:T(4,128)(2,1)S(1)}, u32[]{:S(2)}, u32[]{:S(2)}) collective-permute-start(bf16[4,3072]{1,0:T(4,128)(2,1)S(1)} %get-tuple-element.42), channel_id=1, source_target_pairs={{0,8},{2,10},{4,12},{6,14},{8,0},{10,2},{12,4},{14,6},{16,24},{18,... | collective-permute-start | bytes 73736 | tf_op jit(solution)/shard_map/ppermute | solution.py:28
  132.6 13.3 %collective-permute-start.9 = (bf16[4,3072]{1,0:T(4,128)(2,1)S(1)}, bf16[4,3072]{1,0:T(4,128)(2,1)S(1)}, u32[]{:S(2)}, u32[]{:S(2)}) collective-permute-start(bf16[4,3072]{1,0:T(4,128)(2,1)S(1)} %get-tuple-element.41), channel_id=1, source_target_pairs={{0,16},{2,18},{4,20},{6,22},{8,24},{10,26},{12,28},{14,30},{16,0},... | collective-permute-start | bytes 73736 | tf_op jit(solution)/shard_map/ppermute | solution.py:28
  141.2 4.7 %copy-start.2 = (bf16[4,3072]{1,0:T(4,128)(2,1)}, bf16[4,3072]{1,0:T(4,128)(2,1)S(1)}, u32[]{:S(2)}) copy-start(bf16[4,3072]{1,0:T(4,128)(2,1)S(1)} %collective-permute-done.8.rest_0_) | copy-start | bytes 73732
  145.9 0.6 copy-start.3

commit v10 on v8

--- a/solution.py
+++ b/solution.py
@@ -100,10 +100,11 @@
     both = jnp.concatenate([both, beside, own, swap(beside, "core", 1)], axis=0)
     normed_all, grad_all = both[:, :width], both[:, width:]
 
+    act_grad = lax.dot_general(grad_all, w_out, contract_last, preferred_element_type=jnp.float32)
+    act_grad, w_in = lax.optimization_barrier((act_grad, w_in))
     hidden = jnp.dot(normed_all, w_in, preferred_element_type=jnp.float32)
     gelu, derivative = gelu_both(hidden)
     activated = gelu.astype(jnp.bfloat16)
-    act_grad = lax.dot_general(grad_all, w_out, contract_last, preferred_element_type=jnp.float32)
     hidden_grad = (act_grad * derivative).astype(jnp.bfloat16)
     ordered = jnp.dot(order, hidden_grad, preferred_element_type=jnp.float32).astype(jnp.bfloat16)
     half = ordered.shape[0] // 2

time: 154 us -> 154 us (level)
  no operation moved by 1% of the time
where the time goes in v10:
time: 154 us; the launch traced here: 153 us
  starting transfers between devices  56.8 us (37%)
  waiting for transfers between devices  34.9 us (23%)
  blocking collectives  34.2 us (22%)
  other arithmetic  11.3 us (7%)
  local copies, waits for them, and re-layouts  5.97 us (4%)
  matrix products  5.37 us (3%)
  Pallas kernels  3.34 us (2%)
    ppermute x11, starting transfers between devices, swap(): lax.ppermute(rows, axis, [(at, at ^ step) for at in range(lax.axis_size(a...  46.2 us
    all_gather x1, blocking collectives, body(): both = lax.all_gather(joined, 'z', axis=0, tiled=True)  34.2 us
    ppermute x11, waiting for transfers between devices, swap(): lax.ppermute(rows, axis, [(at, at ^ step) for at in range(lax.axis_size(a...  24.2 us
    all_to_all x1, waiting for transfers between devices, body(): spread = lax.all_to_all(spread, DP, 0, 0, tiled=True)  8.07 us
    all_to_all x1, starting transfers between devices, body(): parts = lax.all_to_all(parts, DP, 0, 0, tiled=True)  6.65 us
    all_to_all x1, starting transfers between devices, body(): spread = lax.all_to_all(spread, DP, 0, 0, tiled=True)  3.97 us
  transfers between devices with their start and end apart: 13, of which 6 were waited for; matrix products, arithmetic and copies ran while one was open for 10% of the time, Pallas kernels for 1%

profile of v10, /device:TPU:1, one launch (start us, length us, event | category | flops | bytes accessed | tf_op | source)
XLA Modules:
  0.0 152.8 jit_solution(15764116604195033003)
XLA Ops:
  0.6 1.7 %norm.1 = (bf16[4,6144]{1,0:T(4,128)(2,1)}, f32[4,3072]{1,0:T(4,128)}, f32[4,128]{1,0:T(4,128)}) custom-call(bf16[4,3072]{1,0:T(4,128)(2,1)} %inputs.1, f32[1,3072]{1,0:T(1,128)} %bitcast.18, bf16[4,3072]{1,0:T(4,128)(2,1)} %cotangent.3), custom_call_target="tpu_custom_call" | custom-call | tf_op jit(solution)/shard_map/norm/pallas_call | solution.py:64
  2.4 34.2 %all-gather = bf16[16,4,6144]{2,1,0:T(4,128)(2,1)S(1)} all-gather(bf16[1,4,6144]{2,1,0:T(4,128)(2,1)} %bitcast.20), channel_id=1, replica_groups=mesh['x'=4,'yh'=2,'yl'=2,'z'=16,'core'=2] {'z'}, dimensions={0}, use_global_device_ids=true | all-gather | bytes 835584 | tf_op jit(solution)/shard_map/all_gather | solution.py:94
  36.7 3.2 %collective-permute-start = (bf16[64,6144]{1,0:T(8,128)(2,1)S(1)}, bf16[64,6144]{1,0:T(8,128)(2,1)S(1)}, u32[]{:S(2)}, u32[]{:S(2)}) collective-permute-start(bf16[64,6144]{1,0:T(8,128)(2,1)S(1)} %reshape.20), channel_id=1, source_target_pairs={{0,32},{32,0},{1,33},{33,1},{2,34},{34,2},{3,35},{35,3},{4,36},{36... | collective-permute-start | bytes 2359304 | tf_op jit(solution)/shard_map/ppermute | solution.py:28
  39.9 9.9 %collective-permute-start.1 = (bf16[64,6144]{1,0:T(8,128)(2,1)S(1)}, bf16[64,6144]{1,0:T(8,128)(2,1)S(1)}, u32[]{:S(2)}, u32[]{:S(2)}) collective-permute-start(bf16[64,6144]{1,0:T(8,128)(2,1)S(1)} %reshape.20), channel_id=1, source_target_pairs={{0,1},{1,0},{2,3},{3,2},{4,5},{5,4},{6,7},{7,6},{8,9},{9,8},{10,11... | collective-permute-start | bytes 2359304 | tf_op jit(solution)/shard_map/ppermute | solution.py:28
  55.1 2.3 %fusion.26 = bf16[256,256]{1,0:T(8,128)(2,1)S(1)} fusion(s32[]{:T(128)S(6)} %axis_index.15, s32[256]{0:T(256)S(1)} %get-tuple-element.57, s32[256]{0:T(256)} %get-tuple-element.64, s32[256]{0:T(256)S(1)} %get-tuple-element.58, s32[256]{0:T(256)} %get-tuple-element.65, s32[256]{0:T(256)S(1)} %get-tuple-element.59, s32[256]{0:T(256)} %get-tuple-element.66, ...), kind=kLoop, calls=%fused_computation.67 | loop fusion | flops 5767168 | bytes 147204 | tf_op jit(solution)/shard_map/convert_element_type | solution.py:46
  57.5 3.0 %collective-permute-start.2 = (bf16[64,6144]{1,0:T(8,128)(2,1)S(1)}, bf16[64,6144]{1,0:T(8,128)(2,1)S(1)}, u32[]{:S(2)}, u32[]{:S(2)}) collective-permute-start(bf16[64,6144]{1,0:T(8,128)(2,1)S(1)} %collective-permute-done), channel_id=1, source_target_pairs={{0,1},{1,0},{2,3},{3,2},{4,5},{5,4},{6,7},{7,6},{8,9},{9,8},{10,11... | collective-permute-start | bytes 2359304 | tf_op jit(solution)/shard_map/ppermute | solution.py:28
  60.6 1.8 %collective-permute-done.2 = bf16[64,6144]{1,0:T(8,128)(2,1)S(1)} collective-permute-done((bf16[64,6144]{1,0:T(8,128)(2,1)S(1)}, bf16[64,6144]{1,0:T(8,128)(2,1)S(1)}, u32[]{:S(2)}, u32[]{:S(2)}) %collective-permute-start.2) | collective-permute-done | bytes 786464 | tf_op jit(solution)/shard_map/ppermute | solution.py:28
  65.5 2.3 %collective-permute-start.3 = (bf16[128,3072]{1,0:T(8,128)(2,1)}, bf16[128,3072]{1,0:T(8,128)(2,1)}, u32[]{:S(2)}, u32[]{:S(2)}) collective-permute-start(bf16[128,3072]{1,0:T(8,128)(2,1)} %convolution_convert_fusion.2), channel_id=1, source_target_pairs={{0,1},{1,0},{2,3},{3,2},{4,5},{5,4},{6,7},{7,6},{8,9},{9,8},{10,11... | collective-permute-start | bytes 2359304 | tf_op jit(solution)/shard_map/ppermute | solution.py:28
  70.3 6.6 %all-to-all-start = ((bf16[8,48,3072]{2,1,0:T(8,128)(2,1)}), bf16[8,48,3072]{2,1,0:T(8,128)(2,1)S(1)}, u32[]{:S(2)}, u32[]{:S(2)}) async-start(bf16[8,48,3072]{2,1,0:T(8,128)(2,1)} %bitcast.15), calls=%async_computation | async-start | bytes 4718592 | tf_op jit(solution)/shard_map/all_to_all | solution.py:124
  78.6 1.9 %collective-permute-start.4 = (bf16[32,3072]{1,0:T(8,128)(2,1)S(1)}, bf16[32,3072]{1,0:T(8,128)(2,1)S(1)}, u32[]{:S(2)}, u32[]{:S(2)}) collective-permute-start(bf16[32,3072]{1,0:T(8,128)(2,1)S(1)} %get-tuple-element.41), channel_id=1, source_target_pairs={{0,2},{2,0},{4,6},{6,4},{8,10},{10,8},{12,14},{14,12},{16,18},{18,... | collective-permute-start | bytes 589832 | tf_op jit(solution)/shard_map/ppermute | solution.py:28
  80.5 1.9 %collective-permute-start.5 = (bf16[32,3072]{1,0:T(8,128)(2,1)S(1)}, bf16[32,3072]{1,0:T(8,128)(2,1)S(1)}, u32[]{:S(2)}, u32[]{:S(2)}) collective-permute-start(bf16[32,3072]{1,0:T(8,128)(2,1)S(1)} %get-tuple-element.43), channel_id=1, source_target_pairs={{0,4},{2,6},{4,0},{6,2},{8,12},{10,14},{12,8},{14,10},{16,20},{18,... | collective-permute-start | bytes 589832 | tf_op jit(solution)/shard_map/ppermute | solution.py:28
  82.5 5.4 %collective-permute-start.6 = (bf16[32,3072]{1,0:T(8,128)(2,1)S(1)}, bf16[32,3072]{1,0:T(8,128)(2,1)S(1)}, u32[]{:S(2)}, u32[]{:S(2)}) collective-permute-start(bf16[32,3072]{1,0:T(8,128)(2,1)S(1)} %get-tuple-element.42), channel_id=1, source_target_pairs={{0,6},{2,4},{4,2},{6,0},{8,14},{10,12},{12,10},{14,8},{16,22},{18,... | collective-permute-start | bytes 589832 | tf_op jit(solution)/shard_map/ppermute | solution.py:28
  87.9 9.9 %collective-permute-done.5 = bf16[32,3072]{1,0:T(8,128)(2,1)S(1)} collective-permute-done((bf16[32,3072]{1,0:T(8,128)(2,1)S(1)}, bf16[32,3072]{1,0:T(8,128)(2,1)S(1)}, u32[]{:S(2)}, u32[]{:S(2)}) %collective-permute-start.5) | collective-permute-done | bytes 196640 | tf_op jit(solution)/shard_map/ppermute | solution.py:28
  97.9 2.3 %collective-permute-start.7 = (bf16[16,3072]{1,0:T(8,128)(2,1)S(1)}, bf16[16,3072]{1,0:T(8,128)(2,1)S(1)}, u32[]{:S(2)}, u32[]{:S(2)}) collective-permute-start(bf16[16,3072]{1,0:T(8,128)(2,1)S(1)} %slice.104), channel_id=1, source_target_pairs={{0,32},{32,0},{1,33},{33,1},{2,34},{34,2},{3,35},{35,3},{4,36},{36... | collective-permute-start | bytes 294920 | tf_op jit(solution)/shard_map/ppermute | solution.py:28
  100.3 8.0 %collective-permute-done.7 = bf16[16,3072]{1,0:T(8,128)(2,1)S(1)} collective-permute-done((bf16[16,3072]{1,0:T(8,128)(2,1)S(1)}, bf16[16,3072]{1,0:T(8,128)(2,1)S(1)}, u32[]{:S(2)}, u32[]{:S(2)}) %collective-permute-start.7) | collective-permute-done | bytes 98336 | tf_op jit(solution)/shard_map/ppermute | solution.py:28
  109.0 2.6 %all-to-all-done = bf16[8,48,3072]{2,1,0:T(8,128)(2,1)S(1)} async-done(((bf16[8,48,3072]{2,1,0:T(8,128)(2,1)}), bf16[8,48,3072]{2,1,0:T(8,128)(2,1)S(1)}, u32[]{:S(2)}, u32[]{:S(2)}) %all-to-all-start) | async-done | bytes 2359328 | tf_op jit(solution)/shard_map/all_to_all | solution.py:124
  112.0 1.7 %broadcast_in_dim.5 = bf16[8,48,3072]{2,1,0:T(8,128)(2,1)} broadcast(bf16[48,3072]{1,0:T(8,128)(2,1)S(1)} %multiply_convert_fusion), dimensions={1,2} | broadcast | bytes 2654208 | tf_op jit(solution)/shard_map/broadcast_in_dim | solution.py:137
  113.7 4.0 %all-to-all-start.1 = ((bf16[8,48,3072]{2,1,0:T(8,128)(2,1)}), bf16[8,48,3072]{2,1,0:T(8,128)(2,1)S(1)}, u32[]{:S(2)}, u32[]{:S(2)}) async-start(bf16[8,48,3072]{2,1,0:T(8,128)(2,1)} %broadcast_in_dim.5), calls=%async_computation.1 | async-start | bytes 4718592 | tf_op jit(solution)/shard_map/all_to_all | solution.py:140
  118.6 5.2 %collective-permute-start.10 = (bf16[4,3072]{1,0:T(4,128)(2,1)S(1)}, bf16[4,3072]{1,0:T(4,128)(2,1)}, u32[]{:S(2)}, u32[]{:S(2)}) collective-permute-start(bf16[4,3072]{1,0:T(4,128)(2,1)S(1)} %get-tuple-element.46), channel_id=1, source_target_pairs={{0,24},{2,26},{4,28},{6,30},{8,16},{10,18},{12,20},{14,22},{16,8},... | collective-permute-start | bytes 73736 | tf_op jit(solution)/shard_map/ppermute | solution.py:28
  123.8 3.8 %collective-permute-start.8 = (bf16[4,3072]{1,0:T(4,128)(2,1)S(1)}, bf16[4,3072]{1,0:T(4,128)(2,1)S(1)}, u32[]{:S(2)}, u32[]{:S(2)}) collective-permute-start(bf16[4,3072]{1,0:T(4,128)(2,1)S(1)} %get-tuple-element.48), channel_id=1, source_target_pairs={{0,8},{2,10},{4,12},{6,14},{8,0},{10,2},{12,4},{14,6},{16,24},{18,... | collective-permute-start | bytes 73736 | tf_op jit(solution)/shard_map/ppermute | solution.py:28
  127.6 7.3 %collective-permute-start.9 = (bf16[4,3072]{1,0:T(4,128)(2,1)S(1)}, bf16[4,3072]{1,0:T(4,128)(2,1)S(1)}, u32[]{:S(2)}, u32[]{:S(2)}) collective-permute-start(bf16[4,3072]{1,0:T(4,128)(2,1)S(1)} %get-tuple-element.47), channel_id=1, source_target_pairs={{0,16},{2,18},{4,20},{6,22},{8,24},{10,26},{12,28},{14,30},{16,0},... | collective-permute-start | bytes 73736 | tf_op jit(solution)/shard_map/ppermute | solution.py:28
  136.4 4.5 %collective-permute-done.9.rest_1_ = bf16[4,3072]{1,0:T(4,128)(2,1)S(1)} collective-permute-done((bf16[4,3072]{1,0:T(4,128)(2,1)S(1)}, bf16[4,3072]{1,0:T(4,128)(2,1)S(1)}, u32[]{:S(2)}, u32[]{:S(2)}) %collective-permute-start.9) | collective-permute-done | bytes 24608 | tf_op jit(solution)/shard_map/ppermute | solution.py:28
  143.1 8.1 %all-to-all-done.1 = bf16[8,48,3072]{2,1,0:T(8,128)(2,1)S(1)} async-done(((bf16[8,48,3072]{2,1,0:T(8,128)(2,1)}), bf16[8,48,3072]{2,1,0:T(8,128)(2,1)S(1)}, u32[]{:S(2)}, u32[]{:S(2)}) %all-to-all-start.1) | async-done | bytes 2359328 | tf_op jit(solution)/shard_map/all_to_all | solution.py:140
  151.1 1.6 %fusion.41 = (bf16[4,48,3072]{2,1,0:T(8,128)(2,1)}, bf16[4,48,3072]{2,1,0:T(8,128)(2,1)}) fusion(bf16[8,48,3072]{2,1,0:T(8,128)(2,1)S(1)} %all-to-all-done.1), kind=kLoop, calls=%fused_computation.116 | loop fusion | bytes 4718592 | tf_op jit(solution)/shard_map/slice | solution.py:146
  (52 shorter events, 18.7 us)
Async XLA Ops:
  0.6 62.5 %copy-start = (bf16[3072,192]{0,1:T(8,128)(2,1)S(1)}, bf16[3072,192]{0,1:T(8,128)(2,1)}, u32[]{:S(2)}) copy-start(bf16[3072,192]{0,1:T(8,128)(2,1)} %param.7) | copy-start | bytes 3538948
  36.7 20.7 %collective-permute-start = (bf16[64,6144]{1,0:T(8,128)(2,1)S(1)}, bf16[64,6144]{1,0:T(8,128)(2,1)S(1)}, u32[]{:S(2)}, u32[]{:S(2)}) collective-permute-start(bf16[64,6144]{1,0:T(8,128)(2,1)S(1)} %reshape.20), channel_id=1, source_target_pairs={{0,32},{32,0},{1,33},{33,1},{2,34},{34,2},{3,35},{35,3},{4,36},{36... | collective-permute-start | bytes 2359304 | tf_op jit(solution)/shard_map/ppermute | solution.py:28
  39.9 17.5 %collective-permute-start.1 = (bf16[64,6144]{1,0:T(8,128)(2,1)S(1)}, bf16[64,6144]{1,0:T(8,128)(2,1)S(1)}, u32[]{:S(2)}, u32[]{:S(2)}) collective-permute-start(bf16[64,6144]{1,0:T(8,128)(2,1)S(1)} %reshape.20), channel_id=1, source_target_pairs={{0,1},{1,0},{2,3},{3,2},{4,5},{5,4},{6,7},{7,6},{8,9},{9,8},{10,11... | collective-permute-start | bytes 2359304 | tf_op jit(solution)/shard_map/ppermute | solution.py:28
  57.5 4.9 %collective-permute-start.2 = (bf16[64,6144]{1,0:T(8,128)(2,1)S(1)}, bf16[64,6144]{1,0:T(8,128)(2,1)S(1)}, u32[]{:S(2)}, u32[]{:S(2)}) collective-permute-start(bf16[64,6144]{1,0:T(8,128)(2,1)S(1)} %collective-permute-done), channel_id=1, source_target_pairs={{0,1},{1,0},{2,3},{3,2},{4,5},{5,4},{6,7},{7,6},{8,9},{9,8},{10,11... | collective-permute-start | bytes 2359304 | tf_op jit(solution)/shard_map/ppermute | solution.py:28
  60.6 1.9 %copy-start.4 = (bf16[192,3072]{1,0:T(8,128)(2,1)S(1)}, bf16[192,3072]{1,0:T(8,128)(2,1)}, u32[]{:S(2)}) copy-start(bf16[192,3072]{1,0:T(8,128)(2,1)} %param.8) | copy-start | bytes 3538948
  64.2 1.3 copy-start.1
  65.5 11.5 %collective-permute-start.3 = (bf16[128,3072]{1,0:T(8,128)(2,1)}, bf16[128,3072]{1,0:T(8,128)(2,1)}, u32[]{:S(2)}, u32[]{:S(2)}) collective-permute-start(bf16[128,3072]{1,0:T(8,128)(2,1)} %convolution_convert_fusion.2), channel_id=1, source_target_pairs={{0,1},{1,0},{2,3},{3,2},{4,5},{5,4},{6,7},{7,6},{8,9},{9,8},{10,11... | collective-permute-start | bytes 2359304 | tf_op jit(solution)/shard_map/ppermute | solution.py:28
  70.3 41.3 %all-to-all-start = ((bf16[8,48,3072]{2,1,0:T(8,128)(2,1)}), bf16[8,48,3072]{2,1,0:T(8,128)(2,1)S(1)}, u32[]{:S(2)}, u32[]{:S(2)}) async-start(bf16[8,48,3072]{2,1,0:T(8,128)(2,1)} %bitcast.15), calls=%async_computation | async-start | bytes 4718592 | tf_op jit(solution)/shard_map/all_to_all | solution.py:124
  78.6 9.3 %collective-permute-start.4 = (bf16[32,3072]{1,0:T(8,128)(2,1)S(1)}, bf16[32,3072]{1,0:T(8,128)(2,1)S(1)}, u32[]{:S(2)}, u32[]{:S(2)}) collective-permute-start(bf16[32,3072]{1,0:T(8,128)(2,1)S(1)} %get-tuple-element.41), channel_id=1, source_target_pairs={{0,2},{2,0},{4,6},{6,4},{8,10},{10,8},{12,14},{14,12},{16,18},{18,... | collective-permute-start | bytes 589832 | tf_op jit(solution)/shard_map/ppermute | solution.py:28
  80.5 17.3 %collective-permute-start.5 = (bf16[32,3072]{1,0:T(8,128)(2,1)S(1)}, bf16[32,3072]{1,0:T(8,128)(2,1)S(1)}, u32[]{:S(2)}, u32[]{:S(2)}) collective-permute-start(bf16[32,3072]{1,0:T(8,128)(2,1)S(1)} %get-tuple-element.43), channel_id=1, source_target_pairs={{0,4},{2,6},{4,0},{6,2},{8,12},{10,14},{12,8},{14,10},{16,20},{18,... | collective-permute-start | bytes 589832 | tf_op jit(solution)/shard_map/ppermute | solution.py:28
  82.5 15.4 %collective-permute-start.6 = (bf16[32,3072]{1,0:T(8,128)(2,1)S(1)}, bf16[32,3072]{1,0:T(8,128)(2,1)S(1)}, u32[]{:S(2)}, u32[]{:S(2)}) collective-permute-start(bf16[32,3072]{1,0:T(8,128)(2,1)S(1)} %get-tuple-element.42), channel_id=1, source_target_pairs={{0,6},{2,4},{4,2},{6,0},{8,14},{10,12},{12,10},{14,8},{16,22},{18,... | collective-permute-start | bytes 589832 | tf_op jit(solution)/shard_map/ppermute | solution.py:28
  97.9 10.3 %collective-permute-start.7 = (bf16[16,3072]{1,0:T(8,128)(2,1)S(1)}, bf16[16,3072]{1,0:T(8,128)(2,1)S(1)}, u32[]{:S(2)}, u32[]{:S(2)}) collective-permute-start(bf16[16,3072]{1,0:T(8,128)(2,1)S(1)} %slice.104), channel_id=1, source_target_pairs={{0,32},{32,0},{1,33},{33,1},{2,34},{34,2},{3,35},{35,3},{4,36},{36... | collective-permute-start | bytes 294920 | tf_op jit(solution)/shard_map/ppermute | solution.py:28
  113.7 37.5 %all-to-all-start.1 = ((bf16[8,48,3072]{2,1,0:T(8,128)(2,1)}), bf16[8,48,3072]{2,1,0:T(8,128)(2,1)S(1)}, u32[]{:S(2)}, u32[]{:S(2)}) async-start(bf16[8,48,3072]{2,1,0:T(8,128)(2,1)} %broadcast_in_dim.5), calls=%async_computation.1 | async-start | bytes 4718592 | tf_op jit(solution)/shard_map/all_to_all | solution.py:140
  118.6 17.7 %collective-permute-start.10 = (bf16[4,3072]{1,0:T(4,128)(2,1)S(1)}, bf16[4,3072]{1,0:T(4,128)(2,1)}, u32[]{:S(2)}, u32[]{:S(2)}) collective-permute-start(bf16[4,3072]{1,0:T(4,128)(2,1)S(1)} %get-tuple-element.46), channel_id=1, source_target_pairs={{0,24},{2,26},{4,28},{6,30},{8,16},{10,18},{12,20},{14,22},{16,8},... | collective-permute-start | bytes 73736 | tf_op jit(solution)/shard_map/ppermute | solution.py:28
  123.8 12.6 %collective-permute-start.8 = (bf16[4,3072]{1,0:T(4,128)(2,1)S(1)}, bf16[4,3072]{1,0:T(4,128)(2,1)S(1)}, u32[]{:S(2)}, u32[]{:S(2)}) collective-permute-start(bf16[4,3072]{1,0:T(4,128)(2,1)S(1)} %get-tuple-element.48), channel_id=1, source_target_pairs={{0,8},{2,10},{4,12},{6,14},{8,0},{10,2},{12,4},{14,6},{16,24},{18,... | collective-permute-start | bytes 73736 | tf_op jit(solution)/shard_map/ppermute | solution.py:28
  127.6 13.3 %collective-permute-start.9 = (bf16[4,3072]{1,0:T(4,128)(2,1)S(1)}, bf16[4,3072]{1,0:T(4,128)(2,1)S(1)}, u32[]{:S(2)}, u32[]{:S(2)}) collective-permute-start(bf16[4,3072]{1,0:T(4,128)(2,1)S(1)} %get-tuple-element.47), channel_id=1, source_target_pairs={{0,16},{2,18},{4,20},{6,22},{8,24},{10,26},{12,28},{14,30},{16,0},... | collective-permute-start | bytes 73736 | tf_op jit(solution)/shard_map/ppermute | solution.py:28
  136.4 4.5 %copy-start.2 = (bf16[4,3072]{1,0:T(4,128)(2,1)}, bf16[4,3072]{1,0:T(4,128)(2,1)S(1)}, u32[]{:S(2)}) copy-start(bf16[4,3072]{1,0:T(4,128)(2,1)S(1)} %collective-permute-done.8.rest_0_) | copy-start | bytes 73732
  140.9 0.6 copy-start.3

commit v11 on v10

--- a/solution.py
+++ b/solution.py
@@ -47,14 +47,13 @@
 
 
 def norm_kernel(inputs, gain, cotangent, joined, normal_out, inverse_out):
-    width = inputs.shape[1]
     widened = inputs[...].astype(jnp.float32)
     centred = widened - jnp.mean(widened, axis=1, keepdims=True)
     variance = jnp.mean(centred * centred, axis=1, keepdims=True)
     inverse = 1.0 / jnp.sqrt(variance + 1e-06)
     normal = centred * inverse
-    joined[:, :width] = (normal * gain[...]).astype(jnp.bfloat16)
-    joined[:, width:] = cotangent[...]
+    joined[0] = (normal * gain[...]).astype(jnp.bfloat16)
+    joined[1] = cotangent[...]
     normal_out[...] = normal
     inverse_out[...] = jnp.broadcast_to(inverse, inverse_out.shape)
 
@@ -64,7 +63,7 @@
     return pl.pallas_call(
         norm_kernel,
         out_shape=(
-            jax.ShapeDtypeStruct((rows, 2 * width), jnp.bfloat16),
+            jax.ShapeDtypeStruct((2, rows, width), jnp.bfloat16),
             jax.ShapeDtypeStruct((rows, width), jnp.float32),
             jax.ShapeDtypeStruct((rows, 128), jnp.float32),
         ),
@@ -91,14 +90,14 @@
     n_z = lax.axis_size("z")
     joined, normal, inverse = join_normed(inputs, gain, cotangent)
 
-    both = lax.all_gather(joined, "z", axis=0, tiled=True)
+    both = lax.all_gather(joined, "z").transpose(1, 0, 2, 3).reshape(2, -1, width)
     both, zero = lax.optimization_barrier((both, jnp.int32(0)))
     order = stage_order(rows, n_z, zero)
     beside = swap(both, "yl", 1)
     own = swap(both, "core", 1)
     beside, own, order = lax.optimization_barrier((beside, own, order))
-    both = jnp.concatenate([both, beside, own, swap(beside, "core", 1)], axis=0)
-    normed_all, grad_all = both[:, :width], both[:, width:]
+    both = jnp.concatenate([both, beside, own, swap(beside, "core", 1)], axis=1)
+    normed_all, grad_all = both[0], both[1]
 
     act_grad = lax.dot_general(grad_all, w_out, contract_last, preferred_element_type=jnp.float32)
     act_grad, w_in = lax.optimization_barrier((act_grad, w_in))
@@ -113,13 +112,13 @@
     ).astype(jnp.bfloat16)
 
     activated, hidden_grad, send = lax.optimization_barrier((activated, hidden_grad, send))
-    part_in = lax.dot_general(
-        hidden_grad, normed_all, contract_first, preferred_element_type=jnp.float32
-    ).astype(jnp.bfloat16)
-    part_out = lax.dot_general(
-        activated, grad_all, contract_first, preferred_element_type=jnp.float32
-    ).astype(jnp.bfloat16)
-    parts = jnp.concatenate([part_in, part_out], axis=0).reshape(n_dp, -1, width)
+    parts = lax.dot_general(
+        jnp.stack([hidden_grad, activated]),
+        both,
+        (((1,), (1,)), ((0,), (0,))),
+        preferred_element_type=jnp.float32,
+    )
+    parts = parts.astype(jnp.bfloat16).reshape(n_dp, -1, width)
     parts, ordered = lax.optimization_barrier((parts, ordered))
     parts = lax.all_to_all(parts, DP, 0, 0, tiled=True)
 

time: 154 us -> 154 us (level)
  other arithmetic: 11.3 us -> 7.26 us
  starting transfers between devices: 56.8 us -> 59.3 us
    ppermute x11, starting transfers between devices: 46.2 us -> 48.7 us  [swap(): lax.ppermute(rows, axis, [(at, at ^ step) for at in range(lax.axis_size(a...]
    sub x3, other arithmetic: 1.78 us -> 0.03 us  [stage_order(): bit = at // block % 2]
    concatenate x1 -> x0, other arithmetic: 1.56 us -> none  [body(): jnp.concatenate([part_in, part_out], axis=0).reshape(n_dp, -1, width)]
  transfers between devices with their start and end apart: 13 -> 13, of which waited for: 6 -> 6; matrix products, arithmetic and copies ran while one was open for 10% -> 8% of each run, Pallas kernels for 1% -> 1%
where the time goes in v11:
time: 154 us; the launch traced here: 153 us
  starting transfers between devices  59.3 us (39%)
  waiting for transfers between devices  34.8 us (23%)
  blocking collectives  34.2 us (22%)
  other arithmetic  7.26 us (5%)
  local copies, waits for them, and re-layouts  6.88 us (4%)
  matrix products  6.63 us (4%)
  Pallas kernels  3.34 us (2%)
    ppermute x11, starting transfers between devices, swap(): lax.ppermute(rows, axis, [(at, at ^ step) for at in range(lax.axis_size(a...  48.7 us
    all_gather x1, blocking collectives, body(): lax.all_gather(joined, 'z').transpose(1, 0, 2, 3).reshape(2, -1, width)  34.2 us
    ppermute x11, waiting for transfers between devices, swap(): lax.ppermute(rows, axis, [(at, at ^ step) for at in range(lax.axis_size(a...  24.1 us
    all_to_all x1, waiting for transfers between devices, body(): spread = lax.all_to_all(spread, DP, 0, 0, tiled=True)  8.07 us
    all_to_all x1, starting transfers between devices, body(): parts = lax.all_to_all(parts, DP, 0, 0, tiled=True)  6.65 us
    all_to_all x1, starting transfers between devices, body(): spread = lax.all_to_all(spread, DP, 0, 0, tiled=True)  3.97 us
  transfers between devices with their start and end apart: 13, of which 6 were waited for; matrix products, arithmetic and copies ran while one was open for 8% of the time, Pallas kernels for 1%

profile of v11, /device:TPU:1, one launch (start us, length us, event | category | flops | bytes accessed | tf_op | source)
XLA Modules:
  0.0 153.4 jit_solution(14686207203985434152)
XLA Ops:
  0.6 1.7 %norm.1 = (bf16[2,4,3072]{2,1,0:T(4,128)(2,1)}, f32[4,3072]{1,0:T(4,128)}, f32[4,128]{1,0:T(4,128)}) custom-call(bf16[4,3072]{1,0:T(4,128)(2,1)} %inputs.1, f32[1,3072]{1,0:T(1,128)} %bitcast.32, bf16[4,3072]{1,0:T(4,128)(2,1)} %cotangent.3), custom_call_target="tpu_custom_call" | custom-call | tf_op jit(solution)/shard_map/norm/pallas_call | solution.py:63
  2.4 34.2 %all-gather = bf16[32,4,3072]{2,1,0:T(4,128)(2,1)S(1)} all-gather(bf16[2,4,3072]{2,1,0:T(4,128)(2,1)} %get-tuple-element.21), channel_id=2, replica_groups=mesh['x'=4,'yh'=2,'yl'=2,'z'=16,'core'=2] {'z'}, dimensions={0}, use_global_device_ids=true | all-gather | bytes 835584 | tf_op jit(solution)/shard_map/all_gather | solution.py:93
  37.0 3.2 %collective-permute-start = (bf16[2,64,3072]{2,1,0:T(8,128)(2,1)S(1)}, bf16[2,64,3072]{2,1,0:T(8,128)(2,1)S(1)}, u32[]{:S(2)}, u32[]{:S(2)}) collective-permute-start(bf16[2,64,3072]{2,1,0:T(8,128)(2,1)S(1)} %reshape.21), channel_id=1, source_target_pairs={{0,32},{32,0},{1,33},{33,1},{2,34},{34,2},{3,35},{35,3},{4,36},{36... | collective-permute-start | bytes 2359304 | tf_op jit(solution)/shard_map/ppermute | solution.py:28
  40.2 9.9 %collective-permute-start.1 = (bf16[2,64,3072]{2,1,0:T(8,128)(2,1)S(1)}, bf16[2,64,3072]{2,1,0:T(8,128)(2,1)S(1)}, u32[]{:S(2)}, u32[]{:S(2)}) collective-permute-start(bf16[2,64,3072]{2,1,0:T(8,128)(2,1)S(1)} %reshape.21), channel_id=1, source_target_pairs={{0,1},{1,0},{2,3},{3,2},{4,5},{5,4},{6,7},{7,6},{8,9},{9,8},{10,11... | collective-permute-start | bytes 2359304 | tf_op jit(solution)/shard_map/ppermute | solution.py:28
  53.1 2.1 %fusion.22 = bf16[256,256]{1,0:T(8,128)(2,1)S(1)} fusion(s32[]{:T(128)S(6)} %axis_index.15, s32[256]{0:T(256)S(1)} %get-tuple-element.57, s32[256]{0:T(256)S(1)} %get-tuple-element.64, s32[256]{0:T(256)S(1)} %get-tuple-element.58, s32[256]{0:T(256)S(1)} %get-tuple-element.65, s32[256]{0:T(256)S(1)} %get-tuple-element.59, s32[256]{0:T(256)S(1)} %get-tuple-element.66, ...), kind=kLoop, calls=%fused_computation.64 | loop fusion | flops 5767168 | bytes 147204 | tf_op jit(solution)/shard_map/convert_element_type | solution.py:46
  55.2 5.5 %collective-permute-start.2 = (bf16[2,64,3072]{2,1,0:T(8,128)(2,1)S(1)}, bf16[2,64,3072]{2,1,0:T(8,128)(2,1)S(1)}, u32[]{:S(2)}, u32[]{:S(2)}) collective-permute-start(bf16[2,64,3072]{2,1,0:T(8,128)(2,1)S(1)} %collective-permute-done), channel_id=1, source_target_pairs={{0,1},{1,0},{2,3},{3,2},{4,5},{5,4},{6,7},{7,6},{8,9},{9,8},{10,11... | collective-permute-start | bytes 2359304 | tf_op jit(solution)/shard_map/ppermute | solution.py:28
  61.0 1.7 %collective-permute-done.2 = bf16[2,64,3072]{2,1,0:T(8,128)(2,1)S(1)} collective-permute-done((bf16[2,64,3072]{2,1,0:T(8,128)(2,1)S(1)}, bf16[2,64,3072]{2,1,0:T(8,128)(2,1)S(1)}, u32[]{:S(2)}, u32[]{:S(2)}) %collective-permute-start.2) | collective-permute-done | bytes 786464 | tf_op jit(solution)/shard_map/ppermute | solution.py:28
  66.4 2.3 %collective-permute-start.3 = (bf16[128,3072]{1,0:T(8,128)(2,1)}, bf16[128,3072]{1,0:T(8,128)(2,1)}, u32[]{:S(2)}, u32[]{:S(2)}) collective-permute-start(bf16[128,3072]{1,0:T(8,128)(2,1)} %convolution_convert_fusion.1), channel_id=1, source_target_pairs={{0,1},{1,0},{2,3},{3,2},{4,5},{5,4},{6,7},{7,6},{8,9},{9,8},{10,11... | collective-permute-start | bytes 2359304 | tf_op jit(solution)/shard_map/ppermute | solution.py:28
  68.7 2.2 %convolution_convert_fusion = bf16[2,192,3072]{2,1,0:T(8,128)(2,1)} fusion(bf16[2,256,3072]{2,1,0:T(8,128)(2,1)S(1)} %constant_dynamic-update-slice_fusion, bf16[1,256,192]{1,2,0:T(8,128)(2,1)S(1)} %bitcast.31, bf16[1,256,192]{1,2,0:T(8,128)(2,1)S(1)} %bitcast.30), kind=kOutput, calls=%fused_computation.1 | convolution fusion | flops 605257728 | bytes 5701632 | tf_op jit(solution)/shard_map/dot_general | solution.py:115
  70.9 6.6 %all-to-all-start = ((bf16[8,48,3072]{2,1,0:T(8,128)(2,1)}), bf16[8,48,3072]{2,1,0:T(8,128)(2,1)S(1)}, u32[]{:S(2)}, u32[]{:S(2)}) async-start(bf16[8,48,3072]{2,1,0:T(8,128)(2,1)} %bitcast.25), calls=%async_computation | async-start | bytes 4718592 | tf_op jit(solution)/shard_map/all_to_all | solution.py:123
  79.2 1.9 %collective-permute-start.4 = (bf16[32,3072]{1,0:T(8,128)(2,1)S(1)}, bf16[32,3072]{1,0:T(8,128)(2,1)S(1)}, u32[]{:S(2)}, u32[]{:S(2)}) collective-permute-start(bf16[32,3072]{1,0:T(8,128)(2,1)S(1)} %get-tuple-element.41), channel_id=1, source_target_pairs={{0,2},{2,0},{4,6},{6,4},{8,10},{10,8},{12,14},{14,12},{16,18},{18,... | collective-permute-start | bytes 589832 | tf_op jit(solution)/shard_map/ppermute | solution.py:28
  81.1 1.9 %collective-permute-start.5 = (bf16[32,3072]{1,0:T(8,128)(2,1)S(1)}, bf16[32,3072]{1,0:T(8,128)(2,1)S(1)}, u32[]{:S(2)}, u32[]{:S(2)}) collective-permute-start(bf16[32,3072]{1,0:T(8,128)(2,1)S(1)} %get-tuple-element.43), channel_id=1, source_target_pairs={{0,4},{2,6},{4,0},{6,2},{8,12},{10,14},{12,8},{14,10},{16,20},{18,... | collective-permute-start | bytes 589832 | tf_op jit(solution)/shard_map/ppermute | solution.py:28
  83.1 5.4 %collective-permute-start.6 = (bf16[32,3072]{1,0:T(8,128)(2,1)S(1)}, bf16[32,3072]{1,0:T(8,128)(2,1)S(1)}, u32[]{:S(2)}, u32[]{:S(2)}) collective-permute-start(bf16[32,3072]{1,0:T(8,128)(2,1)S(1)} %get-tuple-element.42), channel_id=1, source_target_pairs={{0,6},{2,4},{4,2},{6,0},{8,14},{10,12},{12,10},{14,8},{16,22},{18,... | collective-permute-start | bytes 589832 | tf_op jit(solution)/shard_map/ppermute | solution.py:28
  88.5 10.0 %collective-permute-done.5 = bf16[32,3072]{1,0:T(8,128)(2,1)S(1)} collective-permute-done((bf16[32,3072]{1,0:T(8,128)(2,1)S(1)}, bf16[32,3072]{1,0:T(8,128)(2,1)S(1)}, u32[]{:S(2)}, u32[]{:S(2)}) %collective-permute-start.5) | collective-permute-done | bytes 196640 | tf_op jit(solution)/shard_map/ppermute | solution.py:28
  98.6 2.3 %collective-permute-start.7 = (bf16[16,3072]{1,0:T(8,128)(2,1)S(1)}, bf16[16,3072]{1,0:T(8,128)(2,1)S(1)}, u32[]{:S(2)}, u32[]{:S(2)}) collective-permute-start(bf16[16,3072]{1,0:T(8,128)(2,1)S(1)} %slice.100), channel_id=1, source_target_pairs={{0,32},{32,0},{1,33},{33,1},{2,34},{34,2},{3,35},{35,3},{4,36},{36... | collective-permute-start | bytes 294920 | tf_op jit(solution)/shard_map/ppermute | solution.py:28
  100.9 7.9 %collective-permute-done.7 = bf16[16,3072]{1,0:T(8,128)(2,1)S(1)} collective-permute-done((bf16[16,3072]{1,0:T(8,128)(2,1)S(1)}, bf16[16,3072]{1,0:T(8,128)(2,1)S(1)}, u32[]{:S(2)}, u32[]{:S(2)}) %collective-permute-start.7) | collective-permute-done | bytes 98336 | tf_op jit(solution)/shard_map/ppermute | solution.py:28
  109.5 2.6 %all-to-all-done = bf16[8,48,3072]{2,1,0:T(8,128)(2,1)S(1)} async-done(((bf16[8,48,3072]{2,1,0:T(8,128)(2,1)}), bf16[8,48,3072]{2,1,0:T(8,128)(2,1)S(1)}, u32[]{:S(2)}, u32[]{:S(2)}) %all-to-all-start) | async-done | bytes 2359328 | tf_op jit(solution)/shard_map/all_to_all | solution.py:123
  112.5 1.7 %broadcast_in_dim.5 = bf16[8,48,3072]{2,1,0:T(8,128)(2,1)} broadcast(bf16[48,3072]{1,0:T(8,128)(2,1)S(1)} %multiply_convert_fusion), dimensions={1,2} | broadcast | bytes 2654208 | tf_op jit(solution)/shard_map/broadcast_in_dim | solution.py:136
  114.2 4.0 %all-to-all-start.1 = ((bf16[8,48,3072]{2,1,0:T(8,128)(2,1)}), bf16[8,48,3072]{2,1,0:T(8,128)(2,1)S(1)}, u32[]{:S(2)}, u32[]{:S(2)}) async-start(bf16[8,48,3072]{2,1,0:T(8,128)(2,1)} %broadcast_in_dim.5), calls=%async_computation.1 | async-start | bytes 4718592 | tf_op jit(solution)/shard_map/all_to_all | solution.py:139
  119.2 5.1 %collective-permute-start.10 = (bf16[4,3072]{1,0:T(4,128)(2,1)S(1)}, bf16[4,3072]{1,0:T(4,128)(2,1)}, u32[]{:S(2)}, u32[]{:S(2)}) collective-permute-start(bf16[4,3072]{1,0:T(4,128)(2,1)S(1)} %get-tuple-element.46), channel_id=1, source_target_pairs={{0,24},{2,26},{4,28},{6,30},{8,16},{10,18},{12,20},{14,22},{16,8},... | collective-permute-start | bytes 73736 | tf_op jit(solution)/shard_map/ppermute | solution.py:28
  124.3 3.8 %collective-permute-start.8 = (bf16[4,3072]{1,0:T(4,128)(2,1)S(1)}, bf16[4,3072]{1,0:T(4,128)(2,1)S(1)}, u32[]{:S(2)}, u32[]{:S(2)}) collective-permute-start(bf16[4,3072]{1,0:T(4,128)(2,1)S(1)} %get-tuple-element.48), channel_id=1, source_target_pairs={{0,8},{2,10},{4,12},{6,14},{8,0},{10,2},{12,4},{14,6},{16,24},{18,... | collective-permute-start | bytes 73736 | tf_op jit(solution)/shard_map/ppermute | solution.py:28
  128.1 7.3 %collective-permute-start.9 = (bf16[4,3072]{1,0:T(4,128)(2,1)S(1)}, bf16[4,3072]{1,0:T(4,128)(2,1)S(1)}, u32[]{:S(2)}, u32[]{:S(2)}) collective-permute-start(bf16[4,3072]{1,0:T(4,128)(2,1)S(1)} %get-tuple-element.47), channel_id=1, source_target_pairs={{0,16},{2,18},{4,20},{6,22},{8,24},{10,26},{12,28},{14,30},{16,0},... | collective-permute-start | bytes 73736 | tf_op jit(solution)/shard_map/ppermute | solution.py:28
  136.9 4.5 %collective-permute-done.9.rest_1_ = bf16[4,3072]{1,0:T(4,128)(2,1)S(1)} collective-permute-done((bf16[4,3072]{1,0:T(4,128)(2,1)S(1)}, bf16[4,3072]{1,0:T(4,128)(2,1)S(1)}, u32[]{:S(2)}, u32[]{:S(2)}) %collective-permute-start.9) | collective-permute-done | bytes 24608 | tf_op jit(solution)/shard_map/ppermute | solution.py:28
  143.6 8.1 %all-to-all-done.1 = bf16[8,48,3072]{2,1,0:T(8,128)(2,1)S(1)} async-done(((bf16[8,48,3072]{2,1,0:T(8,128)(2,1)}), bf16[8,48,3072]{2,1,0:T(8,128)(2,1)S(1)}, u32[]{:S(2)}, u32[]{:S(2)}) %all-to-all-start.1) | async-done | bytes 2359328 | tf_op jit(solution)/shard_map/all_to_all | solution.py:139
  (51 shorter events, 16.4 us)
Async XLA Ops:
  0.6 62.8 %copy-start = (bf16[3072,192]{0,1:T(8,128)(2,1)S(1)}, bf16[3072,192]{0,1:T(8,128)(2,1)}, u32[]{:S(2)}) copy-start(bf16[3072,192]{0,1:T(8,128)(2,1)} %param.7) | copy-start | bytes 3538948
  37.0 18.2 %collective-permute-start = (bf16[2,64,3072]{2,1,0:T(8,128)(2,1)S(1)}, bf16[2,64,3072]{2,1,0:T(8,128)(2,1)S(1)}, u32[]{:S(2)}, u32[]{:S(2)}) collective-permute-start(bf16[2,64,3072]{2,1,0:T(8,128)(2,1)S(1)} %reshape.21), channel_id=1, source_target_pairs={{0,32},{32,0},{1,33},{33,1},{2,34},{34,2},{3,35},{35,3},{4,36},{36... | collective-permute-start | bytes 2359304 | tf_op jit(solution)/shard_map/ppermute | solution.py:28
  40.2 15.0 %collective-permute-start.1 = (bf16[2,64,3072]{2,1,0:T(8,128)(2,1)S(1)}, bf16[2,64,3072]{2,1,0:T(8,128)(2,1)S(1)}, u32[]{:S(2)}, u32[]{:S(2)}) collective-permute-start(bf16[2,64,3072]{2,1,0:T(8,128)(2,1)S(1)} %reshape.21), channel_id=1, source_target_pairs={{0,1},{1,0},{2,3},{3,2},{4,5},{5,4},{6,7},{7,6},{8,9},{9,8},{10,11... | collective-permute-start | bytes 2359304 | tf_op jit(solution)/shard_map/ppermute | solution.py:28
  55.2 7.4 %collective-permute-start.2 = (bf16[2,64,3072]{2,1,0:T(8,128)(2,1)S(1)}, bf16[2,64,3072]{2,1,0:T(8,128)(2,1)S(1)}, u32[]{:S(2)}, u32[]{:S(2)}) collective-permute-start(bf16[2,64,3072]{2,1,0:T(8,128)(2,1)S(1)} %collective-permute-done), channel_id=1, source_target_pairs={{0,1},{1,0},{2,3},{3,2},{4,5},{5,4},{6,7},{7,6},{8,9},{9,8},{10,11... | collective-permute-start | bytes 2359304 | tf_op jit(solution)/shard_map/ppermute | solution.py:28
  60.8 1.9 %copy-start.4 = (bf16[192,3072]{1,0:T(8,128)(2,1)S(1)}, bf16[192,3072]{1,0:T(8,128)(2,1)}, u32[]{:S(2)}) copy-start(bf16[192,3072]{1,0:T(8,128)(2,1)} %param.8) | copy-start | bytes 3538948
  64.5 0.7 copy-start.1
  66.4 11.2 %collective-permute-start.3 = (bf16[128,3072]{1,0:T(8,128)(2,1)}, bf16[128,3072]{1,0:T(8,128)(2,1)}, u32[]{:S(2)}, u32[]{:S(2)}) collective-permute-start(bf16[128,3072]{1,0:T(8,128)(2,1)} %convolution_convert_fusion.1), channel_id=1, source_target_pairs={{0,1},{1,0},{2,3},{3,2},{4,5},{5,4},{6,7},{7,6},{8,9},{9,8},{10,11... | collective-permute-start | bytes 2359304 | tf_op jit(solution)/shard_map/ppermute | solution.py:28
  70.9 41.3 %all-to-all-start = ((bf16[8,48,3072]{2,1,0:T(8,128)(2,1)}), bf16[8,48,3072]{2,1,0:T(8,128)(2,1)S(1)}, u32[]{:S(2)}, u32[]{:S(2)}) async-start(bf16[8,48,3072]{2,1,0:T(8,128)(2,1)} %bitcast.25), calls=%async_computation | async-start | bytes 4718592 | tf_op jit(solution)/shard_map/all_to_all | solution.py:123
  79.2 9.3 %collective-permute-start.4 = (bf16[32,3072]{1,0:T(8,128)(2,1)S(1)}, bf16[32,3072]{1,0:T(8,128)(2,1)S(1)}, u32[]{:S(2)}, u32[]{:S(2)}) collective-permute-start(bf16[32,3072]{1,0:T(8,128)(2,1)S(1)} %get-tuple-element.41), channel_id=1, source_target_pairs={{0,2},{2,0},{4,6},{6,4},{8,10},{10,8},{12,14},{14,12},{16,18},{18,... | collective-permute-start | bytes 589832 | tf_op jit(solution)/shard_map/ppermute | solution.py:28
  81.1 17.3 %collective-permute-start.5 = (bf16[32,3072]{1,0:T(8,128)(2,1)S(1)}, bf16[32,3072]{1,0:T(8,128)(2,1)S(1)}, u32[]{:S(2)}, u32[]{:S(2)}) collective-permute-start(bf16[32,3072]{1,0:T(8,128)(2,1)S(1)} %get-tuple-element.43), channel_id=1, source_target_pairs={{0,4},{2,6},{4,0},{6,2},{8,12},{10,14},{12,8},{14,10},{16,20},{18,... | collective-permute-start | bytes 589832 | tf_op jit(solution)/shard_map/ppermute | solution.py:28
  83.1 15.4 %collective-permute-start.6 = (bf16[32,3072]{1,0:T(8,128)(2,1)S(1)}, bf16[32,3072]{1,0:T(8,128)(2,1)S(1)}, u32[]{:S(2)}, u32[]{:S(2)}) collective-permute-start(bf16[32,3072]{1,0:T(8,128)(2,1)S(1)} %get-tuple-element.42), channel_id=1, source_target_pairs={{0,6},{2,4},{4,2},{6,0},{8,14},{10,12},{12,10},{14,8},{16,22},{18,... | collective-permute-start | bytes 589832 | tf_op jit(solution)/shard_map/ppermute | solution.py:28
  98.6 10.3 %collective-permute-start.7 = (bf16[16,3072]{1,0:T(8,128)(2,1)S(1)}, bf16[16,3072]{1,0:T(8,128)(2,1)S(1)}, u32[]{:S(2)}, u32[]{:S(2)}) collective-permute-start(bf16[16,3072]{1,0:T(8,128)(2,1)S(1)} %slice.100), channel_id=1, source_target_pairs={{0,32},{32,0},{1,33},{33,1},{2,34},{34,2},{3,35},{35,3},{4,36},{36... | collective-permute-start | bytes 294920 | tf_op jit(solution)/shard_map/ppermute | solution.py:28
  114.2 37.5 %all-to-all-start.1 = ((bf16[8,48,3072]{2,1,0:T(8,128)(2,1)}), bf16[8,48,3072]{2,1,0:T(8,128)(2,1)S(1)}, u32[]{:S(2)}, u32[]{:S(2)}) async-start(bf16[8,48,3072]{2,1,0:T(8,128)(2,1)} %broadcast_in_dim.5), calls=%async_computation.1 | async-start | bytes 4718592 | tf_op jit(solution)/shard_map/all_to_all | solution.py:139
  119.2 17.7 %collective-permute-start.10 = (bf16[4,3072]{1,0:T(4,128)(2,1)S(1)}, bf16[4,3072]{1,0:T(4,128)(2,1)}, u32[]{:S(2)}, u32[]{:S(2)}) collective-permute-start(bf16[4,3072]{1,0:T(4,128)(2,1)S(1)} %get-tuple-element.46), channel_id=1, source_target_pairs={{0,24},{2,26},{4,28},{6,30},{8,16},{10,18},{12,20},{14,22},{16,8},... | collective-permute-start | bytes 73736 | tf_op jit(solution)/shard_map/ppermute | solution.py:28
  124.3 12.6 %collective-permute-start.8 = (bf16[4,3072]{1,0:T(4,128)(2,1)S(1)}, bf16[4,3072]{1,0:T(4,128)(2,1)S(1)}, u32[]{:S(2)}, u32[]{:S(2)}) collective-permute-start(bf16[4,3072]{1,0:T(4,128)(2,1)S(1)} %get-tuple-element.48), channel_id=1, source_target_pairs={{0,8},{2,10},{4,12},{6,14},{8,0},{10,2},{12,4},{14,6},{16,24},{18,... | collective-permute-start | bytes 73736 | tf_op jit(solution)/shard_map/ppermute | solution.py:28
  128.1 13.3 %collective-permute-start.9 = (bf16[4,3072]{1,0:T(4,128)(2,1)S(1)}, bf16[4,3072]{1,0:T(4,128)(2,1)S(1)}, u32[]{:S(2)}, u32[]{:S(2)}) collective-permute-start(bf16[4,3072]{1,0:T(4,128)(2,1)S(1)} %get-tuple-element.47), channel_id=1, source_target_pairs={{0,16},{2,18},{4,20},{6,22},{8,24},{10,26},{12,28},{14,30},{16,0},... | collective-permute-start | bytes 73736 | tf_op jit(solution)/shard_map/ppermute | solution.py:28
  136.9 4.5 %copy-start.2 = (bf16[4,3072]{1,0:T(4,128)(2,1)}, bf16[4,3072]{1,0:T(4,128)(2,1)S(1)}, u32[]{:S(2)}) copy-start(bf16[4,3072]{1,0:T(4,128)(2,1)S(1)} %collective-permute-done.8.rest_0_) | copy-start | bytes 73732
  141.4 0.6 copy-start.3

commit v12 on v11

--- a/solution.py
+++ b/solution.py
@@ -119,10 +119,10 @@
         preferred_element_type=jnp.float32,
     )
     parts = parts.astype(jnp.bfloat16).reshape(n_dp, -1, width)
-    parts, ordered = lax.optimization_barrier((parts, ordered))
+    parts, upper = lax.optimization_barrier((parts, ordered[:half]))
     parts = lax.all_to_all(parts, DP, 0, 0, tiled=True)
 
-    keep = lax.dot_general(ordered[:half], w_in, contract_last, preferred_element_type=jnp.float32)
+    keep = lax.dot_general(upper, w_in, contract_last, preferred_element_type=jnp.float32)
     sends = [send]
     for k, (axis, bits) in enumerate(STAGES):
         steps = (*bits, sum(bits))[: len(sends)]

time: 154 us -> 154 us (level)
  no operation moved by 1% of the time
where the time goes in v12:
time: 154 us; the launch traced here: 153 us
  starting transfers between devices  59.3 us (39%)
  waiting for transfers between devices  34.9 us (23%)
  blocking collectives  34.2 us (22%)
  other arithmetic  7.24 us (5%)
  local copies, waits for them, and re-layouts  6.85 us (4%)
  matrix products  6.6 us (4%)
  Pallas kernels  3.34 us (2%)
    ppermute x11, starting transfers between devices, swap(): lax.ppermute(rows, axis, [(at, at ^ step) for at in range(lax.axis_size(a...  48.7 us
    all_gather x1, blocking collectives, body(): lax.all_gather(joined, 'z').transpose(1, 0, 2, 3).reshape(2, -1, width)  34.2 us
    ppermute x11, waiting for transfers between devices, swap(): lax.ppermute(rows, axis, [(at, at ^ step) for at in range(lax.axis_size(a...  24.2 us
    all_to_all x1, waiting for transfers between devices, body(): spread = lax.all_to_all(spread, DP, 0, 0, tiled=True)  8.05 us
    all_to_all x1, starting transfers between devices, body(): parts = lax.all_to_all(parts, DP, 0, 0, tiled=True)  6.65 us
    all_to_all x1, starting transfers between devices, body(): spread = lax.all_to_all(spread, DP, 0, 0, tiled=True)  3.95 us
  transfers between devices with their start and end apart: 13, of which 6 were waited for; matrix products, arithmetic and copies ran while one was open for 8% of the time, Pallas kernels for 1%

profile of v12, /device:TPU:1, one launch (start us, length us, event | category | flops | bytes accessed | tf_op | source)
XLA Modules:
  0.0 153.3 jit_solution(1940704683311081368)
XLA Ops:
  0.6 1.7 %norm.1 = (bf16[2,4,3072]{2,1,0:T(4,128)(2,1)}, f32[4,3072]{1,0:T(4,128)}, f32[4,128]{1,0:T(4,128)}) custom-call(bf16[4,3072]{1,0:T(4,128)(2,1)} %inputs.1, f32[1,3072]{1,0:T(1,128)} %bitcast.33, bf16[4,3072]{1,0:T(4,128)(2,1)} %cotangent.3), custom_call_target="tpu_custom_call" | custom-call | tf_op jit(solution)/shard_map/norm/pallas_call | solution.py:63
  2.4 34.2 %all-gather = bf16[32,4,3072]{2,1,0:T(4,128)(2,1)S(1)} all-gather(bf16[2,4,3072]{2,1,0:T(4,128)(2,1)} %get-tuple-element.21), channel_id=2, replica_groups=mesh['x'=4,'yh'=2,'yl'=2,'z'=16,'core'=2] {'z'}, dimensions={0}, use_global_device_ids=true | all-gather | bytes 835584 | tf_op jit(solution)/shard_map/all_gather | solution.py:93
  37.0 3.2 %collective-permute-start = (bf16[2,64,3072]{2,1,0:T(8,128)(2,1)S(1)}, bf16[2,64,3072]{2,1,0:T(8,128)(2,1)S(1)}, u32[]{:S(2)}, u32[]{:S(2)}) collective-permute-start(bf16[2,64,3072]{2,1,0:T(8,128)(2,1)S(1)} %reshape.21), channel_id=1, source_target_pairs={{0,32},{32,0},{1,33},{33,1},{2,34},{34,2},{3,35},{35,3},{4,36},{36... | collective-permute-start | bytes 2359304 | tf_op jit(solution)/shard_map/ppermute | solution.py:28
  40.2 9.9 %collective-permute-start.1 = (bf16[2,64,3072]{2,1,0:T(8,128)(2,1)S(1)}, bf16[2,64,3072]{2,1,0:T(8,128)(2,1)S(1)}, u32[]{:S(2)}, u32[]{:S(2)}) collective-permute-start(bf16[2,64,3072]{2,1,0:T(8,128)(2,1)S(1)} %reshape.21), channel_id=1, source_target_pairs={{0,1},{1,0},{2,3},{3,2},{4,5},{5,4},{6,7},{7,6},{8,9},{9,8},{10,11... | collective-permute-start | bytes 2359304 | tf_op jit(solution)/shard_map/ppermute | solution.py:28
  53.1 2.1 %fusion.22 = bf16[256,256]{1,0:T(8,128)(2,1)S(1)} fusion(s32[]{:T(128)S(6)} %axis_index.15, s32[256]{0:T(256)S(1)} %get-tuple-element.57, s32[256]{0:T(256)S(1)} %get-tuple-element.64, s32[256]{0:T(256)S(1)} %get-tuple-element.58, s32[256]{0:T(256)S(1)} %get-tuple-element.65, s32[256]{0:T(256)S(1)} %get-tuple-element.59, s32[256]{0:T(256)S(1)} %get-tuple-element.66, ...), kind=kLoop, calls=%fused_computation.64 | loop fusion | flops 5767168 | bytes 147204 | tf_op jit(solution)/shard_map/convert_element_type | solution.py:46
  55.2 5.6 %collective-permute-start.2 = (bf16[2,64,3072]{2,1,0:T(8,128)(2,1)S(1)}, bf16[2,64,3072]{2,1,0:T(8,128)(2,1)S(1)}, u32[]{:S(2)}, u32[]{:S(2)}) collective-permute-start(bf16[2,64,3072]{2,1,0:T(8,128)(2,1)S(1)} %collective-permute-done), channel_id=1, source_target_pairs={{0,1},{1,0},{2,3},{3,2},{4,5},{5,4},{6,7},{7,6},{8,9},{9,8},{10,11... | collective-permute-start | bytes 2359304 | tf_op jit(solution)/shard_map/ppermute | solution.py:28
  61.0 1.7 %collective-permute-done.2 = bf16[2,64,3072]{2,1,0:T(8,128)(2,1)S(1)} collective-permute-done((bf16[2,64,3072]{2,1,0:T(8,128)(2,1)S(1)}, bf16[2,64,3072]{2,1,0:T(8,128)(2,1)S(1)}, u32[]{:S(2)}, u32[]{:S(2)}) %collective-permute-start.2) | collective-permute-done | bytes 786464 | tf_op jit(solution)/shard_map/ppermute | solution.py:28
  65.7 2.3 %collective-permute-start.3 = (bf16[128,3072]{1,0:T(8,128)(2,1)}, bf16[128,3072]{1,0:T(8,128)(2,1)}, u32[]{:S(2)}, u32[]{:S(2)}) collective-permute-start(bf16[128,3072]{1,0:T(8,128)(2,1)} %convolution_convert_fusion.1), channel_id=1, source_target_pairs={{0,1},{1,0},{2,3},{3,2},{4,5},{5,4},{6,7},{7,6},{8,9},{9,8},{10,11... | collective-permute-start | bytes 2359304 | tf_op jit(solution)/shard_map/ppermute | solution.py:28
  68.7 2.2 %convolution_convert_fusion = bf16[2,192,3072]{2,1,0:T(8,128)(2,1)} fusion(bf16[2,256,3072]{2,1,0:T(8,128)(2,1)S(1)} %constant_dynamic-update-slice_fusion, bf16[1,256,192]{1,2,0:T(8,128)(2,1)S(1)} %bitcast.32, bf16[1,256,192]{1,2,0:T(8,128)(2,1)S(1)} %bitcast.31), kind=kOutput, calls=%fused_computation.1 | convolution fusion | flops 605257728 | bytes 5701632 | tf_op jit(solution)/shard_map/dot_general | solution.py:115
  70.9 6.6 %all-to-all-start = ((bf16[8,48,3072]{2,1,0:T(8,128)(2,1)}), bf16[8,48,3072]{2,1,0:T(8,128)(2,1)S(1)}, u32[]{:S(2)}, u32[]{:S(2)}) async-start(bf16[8,48,3072]{2,1,0:T(8,128)(2,1)} %bitcast.26), calls=%async_computation | async-start | bytes 4718592 | tf_op jit(solution)/shard_map/all_to_all | solution.py:123
  79.1 1.9 %collective-permute-start.4 = (bf16[32,3072]{1,0:T(8,128)(2,1)S(1)}, bf16[32,3072]{1,0:T(8,128)(2,1)S(1)}, u32[]{:S(2)}, u32[]{:S(2)}) collective-permute-start(bf16[32,3072]{1,0:T(8,128)(2,1)S(1)} %get-tuple-element.43), channel_id=1, source_target_pairs={{0,2},{2,0},{4,6},{6,4},{8,10},{10,8},{12,14},{14,12},{16,18},{18,... | collective-permute-start | bytes 589832 | tf_op jit(solution)/shard_map/ppermute | solution.py:28
  81.1 1.9 %collective-permute-start.5 = (bf16[32,3072]{1,0:T(8,128)(2,1)S(1)}, bf16[32,3072]{1,0:T(8,128)(2,1)S(1)}, u32[]{:S(2)}, u32[]{:S(2)}) collective-permute-start(bf16[32,3072]{1,0:T(8,128)(2,1)S(1)} %get-tuple-element.45), channel_id=1, source_target_pairs={{0,4},{2,6},{4,0},{6,2},{8,12},{10,14},{12,8},{14,10},{16,20},{18,... | collective-permute-start | bytes 589832 | tf_op jit(solution)/shard_map/ppermute | solution.py:28
  83.0 5.4 %collective-permute-start.6 = (bf16[32,3072]{1,0:T(8,128)(2,1)S(1)}, bf16[32,3072]{1,0:T(8,128)(2,1)S(1)}, u32[]{:S(2)}, u32[]{:S(2)}) collective-permute-start(bf16[32,3072]{1,0:T(8,128)(2,1)S(1)} %get-tuple-element.44), channel_id=1, source_target_pairs={{0,6},{2,4},{4,2},{6,0},{8,14},{10,12},{12,10},{14,8},{16,22},{18,... | collective-permute-start | bytes 589832 | tf_op jit(solution)/shard_map/ppermute | solution.py:28
  88.4 9.9 %collective-permute-done.5 = bf16[32,3072]{1,0:T(8,128)(2,1)S(1)} collective-permute-done((bf16[32,3072]{1,0:T(8,128)(2,1)S(1)}, bf16[32,3072]{1,0:T(8,128)(2,1)S(1)}, u32[]{:S(2)}, u32[]{:S(2)}) %collective-permute-start.5) | collective-permute-done | bytes 196640 | tf_op jit(solution)/shard_map/ppermute | solution.py:28
  98.5 2.3 %collective-permute-start.7 = (bf16[16,3072]{1,0:T(8,128)(2,1)S(1)}, bf16[16,3072]{1,0:T(8,128)(2,1)S(1)}, u32[]{:S(2)}, u32[]{:S(2)}) collective-permute-start(bf16[16,3072]{1,0:T(8,128)(2,1)S(1)} %slice.97), channel_id=1, source_target_pairs={{0,32},{32,0},{1,33},{33,1},{2,34},{34,2},{3,35},{35,3},{4,36},{36... | collective-permute-start | bytes 294920 | tf_op jit(solution)/shard_map/ppermute | solution.py:28
  100.8 8.0 %collective-permute-done.7 = bf16[16,3072]{1,0:T(8,128)(2,1)S(1)} collective-permute-done((bf16[16,3072]{1,0:T(8,128)(2,1)S(1)}, bf16[16,3072]{1,0:T(8,128)(2,1)S(1)}, u32[]{:S(2)}, u32[]{:S(2)}) %collective-permute-start.7) | collective-permute-done | bytes 98336 | tf_op jit(solution)/shard_map/ppermute | solution.py:28
  109.5 2.6 %all-to-all-done = bf16[8,48,3072]{2,1,0:T(8,128)(2,1)S(1)} async-done(((bf16[8,48,3072]{2,1,0:T(8,128)(2,1)}), bf16[8,48,3072]{2,1,0:T(8,128)(2,1)S(1)}, u32[]{:S(2)}, u32[]{:S(2)}) %all-to-all-start) | async-done | bytes 2359328 | tf_op jit(solution)/shard_map/all_to_all | solution.py:123
  112.5 1.7 %broadcast_in_dim.5 = bf16[8,48,3072]{2,1,0:T(8,128)(2,1)} broadcast(bf16[48,3072]{1,0:T(8,128)(2,1)S(1)} %multiply_convert_fusion), dimensions={1,2} | broadcast | bytes 2654208 | tf_op jit(solution)/shard_map/broadcast_in_dim | solution.py:136
  114.2 4.0 %all-to-all-start.1 = ((bf16[8,48,3072]{2,1,0:T(8,128)(2,1)}), bf16[8,48,3072]{2,1,0:T(8,128)(2,1)S(1)}, u32[]{:S(2)}, u32[]{:S(2)}) async-start(bf16[8,48,3072]{2,1,0:T(8,128)(2,1)} %broadcast_in_dim.5), calls=%async_computation.1 | async-start | bytes 4718592 | tf_op jit(solution)/shard_map/all_to_all | solution.py:139
  119.1 5.1 %collective-permute-start.10 = (bf16[4,3072]{1,0:T(4,128)(2,1)S(1)}, bf16[4,3072]{1,0:T(4,128)(2,1)}, u32[]{:S(2)}, u32[]{:S(2)}) collective-permute-start(bf16[4,3072]{1,0:T(4,128)(2,1)S(1)} %get-tuple-element.48), channel_id=1, source_target_pairs={{0,24},{2,26},{4,28},{6,30},{8,16},{10,18},{12,20},{14,22},{16,8},... | collective-permute-start | bytes 73736 | tf_op jit(solution)/shard_map/ppermute | solution.py:28
  124.3 3.8 %collective-permute-start.8 = (bf16[4,3072]{1,0:T(4,128)(2,1)S(1)}, bf16[4,3072]{1,0:T(4,128)(2,1)S(1)}, u32[]{:S(2)}, u32[]{:S(2)}) collective-permute-start(bf16[4,3072]{1,0:T(4,128)(2,1)S(1)} %get-tuple-element.50), channel_id=1, source_target_pairs={{0,8},{2,10},{4,12},{6,14},{8,0},{10,2},{12,4},{14,6},{16,24},{18,... | collective-permute-start | bytes 73736 | tf_op jit(solution)/shard_map/ppermute | solution.py:28
  128.1 7.2 %collective-permute-start.9 = (bf16[4,3072]{1,0:T(4,128)(2,1)S(1)}, bf16[4,3072]{1,0:T(4,128)(2,1)S(1)}, u32[]{:S(2)}, u32[]{:S(2)}) collective-permute-start(bf16[4,3072]{1,0:T(4,128)(2,1)S(1)} %get-tuple-element.49), channel_id=1, source_target_pairs={{0,16},{2,18},{4,20},{6,22},{8,24},{10,26},{12,28},{14,30},{16,0},... | collective-permute-start | bytes 73736 | tf_op jit(solution)/shard_map/ppermute | solution.py:28
  136.9 4.5 %collective-permute-done.9.rest_1_ = bf16[4,3072]{1,0:T(4,128)(2,1)S(1)} collective-permute-done((bf16[4,3072]{1,0:T(4,128)(2,1)S(1)}, bf16[4,3072]{1,0:T(4,128)(2,1)S(1)}, u32[]{:S(2)}, u32[]{:S(2)}) %collective-permute-start.9) | collective-permute-done | bytes 24608 | tf_op jit(solution)/shard_map/ppermute | solution.py:28
  143.6 8.1 %all-to-all-done.1 = bf16[8,48,3072]{2,1,0:T(8,128)(2,1)S(1)} async-done(((bf16[8,48,3072]{2,1,0:T(8,128)(2,1)}), bf16[8,48,3072]{2,1,0:T(8,128)(2,1)S(1)}, u32[]{:S(2)}, u32[]{:S(2)}) %all-to-all-start.1) | async-done | bytes 2359328 | tf_op jit(solution)/shard_map/all_to_all | solution.py:139
  (50 shorter events, 16.3 us)
Async XLA Ops:
  0.6 62.8 %copy-start = (bf16[3072,192]{0,1:T(8,128)(2,1)S(1)}, bf16[3072,192]{0,1:T(8,128)(2,1)}, u32[]{:S(2)}) copy-start(bf16[3072,192]{0,1:T(8,128)(2,1)} %param.7) | copy-start | bytes 3538948
  37.0 18.2 %collective-permute-start = (bf16[2,64,3072]{2,1,0:T(8,128)(2,1)S(1)}, bf16[2,64,3072]{2,1,0:T(8,128)(2,1)S(1)}, u32[]{:S(2)}, u32[]{:S(2)}) collective-permute-start(bf16[2,64,3072]{2,1,0:T(8,128)(2,1)S(1)} %reshape.21), channel_id=1, source_target_pairs={{0,32},{32,0},{1,33},{33,1},{2,34},{34,2},{3,35},{35,3},{4,36},{36... | collective-permute-start | bytes 2359304 | tf_op jit(solution)/shard_map/ppermute | solution.py:28
  40.2 15.0 %collective-permute-start.1 = (bf16[2,64,3072]{2,1,0:T(8,128)(2,1)S(1)}, bf16[2,64,3072]{2,1,0:T(8,128)(2,1)S(1)}, u32[]{:S(2)}, u32[]{:S(2)}) collective-permute-start(bf16[2,64,3072]{2,1,0:T(8,128)(2,1)S(1)} %reshape.21), channel_id=1, source_target_pairs={{0,1},{1,0},{2,3},{3,2},{4,5},{5,4},{6,7},{7,6},{8,9},{9,8},{10,11... | collective-permute-start | bytes 2359304 | tf_op jit(solution)/shard_map/ppermute | solution.py:28
  55.2 7.5 %collective-permute-start.2 = (bf16[2,64,3072]{2,1,0:T(8,128)(2,1)S(1)}, bf16[2,64,3072]{2,1,0:T(8,128)(2,1)S(1)}, u32[]{:S(2)}, u32[]{:S(2)}) collective-permute-start(bf16[2,64,3072]{2,1,0:T(8,128)(2,1)S(1)} %collective-permute-done), channel_id=1, source_target_pairs={{0,1},{1,0},{2,3},{3,2},{4,5},{5,4},{6,7},{7,6},{8,9},{9,8},{10,11... | collective-permute-start | bytes 2359304 | tf_op jit(solution)/shard_map/ppermute | solution.py:28
  60.8 1.9 %copy-start.3 = (bf16[192,3072]{1,0:T(8,128)(2,1)S(1)}, bf16[192,3072]{1,0:T(8,128)(2,1)}, u32[]{:S(2)}) copy-start(bf16[192,3072]{1,0:T(8,128)(2,1)} %param.8) | copy-start | bytes 3538948
  65.7 11.8 %collective-permute-start.3 = (bf16[128,3072]{1,0:T(8,128)(2,1)}, bf16[128,3072]{1,0:T(8,128)(2,1)}, u32[]{:S(2)}, u32[]{:S(2)}) collective-permute-start(bf16[128,3072]{1,0:T(8,128)(2,1)} %convolution_convert_fusion.1), channel_id=1, source_target_pairs={{0,1},{1,0},{2,3},{3,2},{4,5},{5,4},{6,7},{7,6},{8,9},{9,8},{10,11... | collective-permute-start | bytes 2359304 | tf_op jit(solution)/shard_map/ppermute | solution.py:28
  70.9 41.3 %all-to-all-start = ((bf16[8,48,3072]{2,1,0:T(8,128)(2,1)}), bf16[8,48,3072]{2,1,0:T(8,128)(2,1)S(1)}, u32[]{:S(2)}, u32[]{:S(2)}) async-start(bf16[8,48,3072]{2,1,0:T(8,128)(2,1)} %bitcast.26), calls=%async_computation | async-start | bytes 4718592 | tf_op jit(solution)/shard_map/all_to_all | solution.py:123
  79.1 9.3 %collective-permute-start.4 = (bf16[32,3072]{1,0:T(8,128)(2,1)S(1)}, bf16[32,3072]{1,0:T(8,128)(2,1)S(1)}, u32[]{:S(2)}, u32[]{:S(2)}) collective-permute-start(bf16[32,3072]{1,0:T(8,128)(2,1)S(1)} %get-tuple-element.43), channel_id=1, source_target_pairs={{0,2},{2,0},{4,6},{6,4},{8,10},{10,8},{12,14},{14,12},{16,18},{18,... | collective-permute-start | bytes 589832 | tf_op jit(solution)/shard_map/ppermute | solution.py:28
  81.1 17.3 %collective-permute-start.5 = (bf16[32,3072]{1,0:T(8,128)(2,1)S(1)}, bf16[32,3072]{1,0:T(8,128)(2,1)S(1)}, u32[]{:S(2)}, u32[]{:S(2)}) collective-permute-start(bf16[32,3072]{1,0:T(8,128)(2,1)S(1)} %get-tuple-element.45), channel_id=1, source_target_pairs={{0,4},{2,6},{4,0},{6,2},{8,12},{10,14},{12,8},{14,10},{16,20},{18,... | collective-permute-start | bytes 589832 | tf_op jit(solution)/shard_map/ppermute | solution.py:28
  83.0 15.4 %collective-permute-start.6 = (bf16[32,3072]{1,0:T(8,128)(2,1)S(1)}, bf16[32,3072]{1,0:T(8,128)(2,1)S(1)}, u32[]{:S(2)}, u32[]{:S(2)}) collective-permute-start(bf16[32,3072]{1,0:T(8,128)(2,1)S(1)} %get-tuple-element.44), channel_id=1, source_target_pairs={{0,6},{2,4},{4,2},{6,0},{8,14},{10,12},{12,10},{14,8},{16,22},{18,... | collective-permute-start | bytes 589832 | tf_op jit(solution)/shard_map/ppermute | solution.py:28
  98.5 10.3 %collective-permute-start.7 = (bf16[16,3072]{1,0:T(8,128)(2,1)S(1)}, bf16[16,3072]{1,0:T(8,128)(2,1)S(1)}, u32[]{:S(2)}, u32[]{:S(2)}) collective-permute-start(bf16[16,3072]{1,0:T(8,128)(2,1)S(1)} %slice.97), channel_id=1, source_target_pairs={{0,32},{32,0},{1,33},{33,1},{2,34},{34,2},{3,35},{35,3},{4,36},{36... | collective-permute-start | bytes 294920 | tf_op jit(solution)/shard_map/ppermute | solution.py:28
  114.2 37.5 %all-to-all-start.1 = ((bf16[8,48,3072]{2,1,0:T(8,128)(2,1)}), bf16[8,48,3072]{2,1,0:T(8,128)(2,1)S(1)}, u32[]{:S(2)}, u32[]{:S(2)}) async-start(bf16[8,48,3072]{2,1,0:T(8,128)(2,1)} %broadcast_in_dim.5), calls=%async_computation.1 | async-start | bytes 4718592 | tf_op jit(solution)/shard_map/all_to_all | solution.py:139
  119.1 17.7 %collective-permute-start.10 = (bf16[4,3072]{1,0:T(4,128)(2,1)S(1)}, bf16[4,3072]{1,0:T(4,128)(2,1)}, u32[]{:S(2)}, u32[]{:S(2)}) collective-permute-start(bf16[4,3072]{1,0:T(4,128)(2,1)S(1)} %get-tuple-element.48), channel_id=1, source_target_pairs={{0,24},{2,26},{4,28},{6,30},{8,16},{10,18},{12,20},{14,22},{16,8},... | collective-permute-start | bytes 73736 | tf_op jit(solution)/shard_map/ppermute | solution.py:28
  124.3 12.6 %collective-permute-start.8 = (bf16[4,3072]{1,0:T(4,128)(2,1)S(1)}, bf16[4,3072]{1,0:T(4,128)(2,1)S(1)}, u32[]{:S(2)}, u32[]{:S(2)}) collective-permute-start(bf16[4,3072]{1,0:T(4,128)(2,1)S(1)} %get-tuple-element.50), channel_id=1, source_target_pairs={{0,8},{2,10},{4,12},{6,14},{8,0},{10,2},{12,4},{14,6},{16,24},{18,... | collective-permute-start | bytes 73736 | tf_op jit(solution)/shard_map/ppermute | solution.py:28
  128.1 13.3 %collective-permute-start.9 = (bf16[4,3072]{1,0:T(4,128)(2,1)S(1)}, bf16[4,3072]{1,0:T(4,128)(2,1)S(1)}, u32[]{:S(2)}, u32[]{:S(2)}) collective-permute-start(bf16[4,3072]{1,0:T(4,128)(2,1)S(1)} %get-tuple-element.49), channel_id=1, source_target_pairs={{0,16},{2,18},{4,20},{6,22},{8,24},{10,26},{12,28},{14,30},{16,0},... | collective-permute-start | bytes 73736 | tf_op jit(solution)/shard_map/ppermute | solution.py:28
  136.9 4.5 %copy-start.1 = (bf16[4,3072]{1,0:T(4,128)(2,1)}, bf16[4,3072]{1,0:T(4,128)(2,1)S(1)}, u32[]{:S(2)}) copy-start(bf16[4,3072]{1,0:T(4,128)(2,1)S(1)} %collective-permute-done.8.rest_0_) | copy-start | bytes 73732
  141.4 0.6 copy-start.2
